TPU v7x, 32 devices: a whole 2x2x4 slice. The times are simulated.
32 devices in a mesh: groups: 2 (over y), expert: 16 (over z, x, core), dp: 1.
Axes of the slice: x: 2, y: 2, z: 4, core: 2. Of those that a mesh axis runs over, the one named last changes fastest.
Arguments:
- hidden_saved: bfloat16 [4096, 8, 768], P(('groups', 'expert', 'dp')), parts along dimension 0, may hold values from -4.6 to 4.6
- grad_out: bfloat16 [4096, 2048], P(('groups', 'expert', 'dp')), parts along dimension 0, may hold values from -4.6 to 4.6
- expert_ids: int32 [4096, 8], P(('groups', 'expert', 'dp')), parts along dimension 0, may hold values from 0 to 15, all different within a row; in each aligned block of 128 rows (0 to 127, 128 to 255, ...) at most 128 rows name the same one
- gate_codes: int32 [4096, 8], P(('groups', 'expert', 'dp')), parts along dimension 0, may hold values from 64 to 255
- clip_bound: float32 [128], P(('groups', 'expert', 'dp')), parts along dimension 0, may hold values from 1605.2976 to 9029.799
Outputs:
- grad_down: bfloat16 [32, 2048, 768], P(('groups', 'expert'), 'dp'), parts along dimension 0
- clip_factors: float32 [128], P(('groups', 'expert', 'dp')), parts along dimension 0
There are 2 independent parts, one for each index of `groups`. A program takes and returns all parts, laid end to end along the dimension named above; each array names one. Nothing has to cross between parts.
Inputs may be any that keep to these rules, and one draw needn't show every extreme that they name: `expert_ids`: each row names 8 different experts. Among the 128 rows of one device no expert is named more than 128 times, a bound that some block reaches.
All inputs are finite; a program needn't handle non-finite values.
Results may differ from a plain program's by a relative error of at most 0.011.
Values may be sent and summed in bfloat16 or wider, within the bound.
No kernel may reach another device: no remote copies, remote signals or barrier semaphores. Data moves between devices by JAX's collectives and lax.ppermute only.
A program may use at most 128 MiB of HBM per device.

v0:
```python
import jax
import jax.numpy as jnp
from jax import lax
from jax.sharding import PartitionSpec as P

TOPK = 8
EXLEN = 32


def per_device(hidden_saved, grad_out, expert_ids, gate_codes, clip_bound):
    experts = lax.axis_size("expert")
    tokens_dev = grad_out.shape[0]
    width = grad_out.shape[1]
    hidden_width = hidden_saved.shape[2]
    examples_dev = clip_bound.shape[0]
    count_pairs = tokens_dev * TOPK
    capacity = min(tokens_dev, 2 * tokens_dev * TOPK // experts)
    ids_flat = expert_ids.reshape(count_pairs)
    onehot = (ids_flat[:, None] == jnp.arange(experts, dtype=jnp.int32)[None, :]).astype(jnp.int32)
    slot_ids = jnp.sum(jnp.cumsum(onehot, axis=0) * onehot, axis=1) - 1
    target = ids_flat * capacity + slot_ids
    hid_rows = hidden_saved.reshape(count_pairs, hidden_width)
    h_buffer = jnp.zeros((experts * capacity, hidden_width), jnp.bfloat16).at[target].set(hid_rows)
    h_buffer = h_buffer.reshape(experts, capacity, hidden_width)
    dy_pairs = jnp.repeat(grad_out, TOPK, axis=0)
    dy_buffer = jnp.zeros((experts * capacity, width), jnp.bfloat16).at[target].set(dy_pairs)
    dy_buffer = dy_buffer.reshape(experts, capacity, width)
    pair_info = jnp.stack(
        [
            gate_codes.reshape(count_pairs),
            jnp.arange(count_pairs, dtype=jnp.int32) // (EXLEN * TOPK),
        ],
        axis=1,
    ).astype(jnp.bfloat16)
    info_buffer = jnp.zeros((experts * capacity, 2), jnp.bfloat16).at[target].set(pair_info)
    info_buffer = info_buffer.reshape(experts, capacity, 2)
    recv_hidden, recv_dy, recv_info = (
        lax.all_to_all(h_buffer, "expert", split_axis=0, concat_axis=0, tiled=True),
        lax.all_to_all(dy_buffer, "expert", split_axis=0, concat_axis=0, tiled=True),
        lax.all_to_all(info_buffer, "expert", split_axis=0, concat_axis=0, tiled=True),
    )
    gate_recv = recv_info[:, :, 0].astype(jnp.float32) / 1024.0
    example_recv = recv_info[:, :, 1].astype(jnp.float32)
    owner_mask = (
        example_recv[:, :, None] == jnp.arange(examples_dev, dtype=jnp.float32)[None, None, :]
    ).astype(jnp.float32)
    hid_gram = jnp.einsum(
        "smh,snh->smn", recv_hidden, recv_hidden, preferred_element_type=jnp.float32
    )
    grad_gram = jnp.einsum("smd,snd->smn", recv_dy, recv_dy, preferred_element_type=jnp.float32)
    weights = hid_gram * grad_gram * gate_recv[:, :, None] * gate_recv[:, None, :]
    partial_value = jnp.sum(jnp.einsum("smn,snx->smx", weights, owner_mask) * owner_mask, axis=1)
    bounds_all = lax.all_gather(clip_bound, "expert", axis=0, tiled=True).reshape(
        experts, examples_dev
    )
    totals = lax.psum(partial_value, "expert")
    factor_all = jnp.minimum(1.0, bounds_all / jnp.sqrt(totals + 1e-06))
    factors = lax.dynamic_index_in_dim(factor_all, lax.axis_index("expert"), 0, keepdims=False)
    pair_scale = jnp.sum(owner_mask * factor_all[:, None, :], axis=2) * gate_recv
    recv_scaled = (pair_scale[:, :, None] * recv_dy.astype(jnp.float32)).astype(jnp.bfloat16)
    summed = lax.psum_scatter(
        lax.dot_general(
            recv_scaled,
            recv_hidden,
            (((0, 1), (0, 1)), ((), ())),
            preferred_element_type=jnp.float32,
        ).astype(jnp.bfloat16),
        "dp",
        scatter_dimension=0,
        tiled=True,
    )
    return (summed[None], factors)


def solution(mesh):
    return jax.shard_map(
        per_device,
        mesh=mesh,
        in_specs=(
            P(("groups", "expert", "dp"), None, None),
            P(("groups", "expert", "dp"), None),
            P(("groups", "expert", "dp"), None),
            P(("groups", "expert", "dp"), None),
            P(("groups", "expert", "dp")),
        ),
        out_specs=(P(("groups", "expert"), "dp", None), P(("groups", "expert", "dp"))),
        check_vma=False,
    )
```

profile of v0, /device:TPU:0, one launch (start us, length us, event | category | flops | bytes accessed | tf_op | source)
XLA Modules:
  0.0 346.0 jit_solution(6454049823626692683)
XLA Ops:
  0.6 0.9 copy.19
  1.6 0.1 eq.47
  1.6 0.1 eq.43
  1.7 0.7 broadcast_multiply_fusion
  2.5 4.5 %reduce-window.6 = s32[16,8,128]{2,1,0:T(8,128)S(1)} reduce-window(s32[16,8,128]{2,1,0:T(8,128)S(1)} %fusion.21, s32[]{:T(128)} %constant.42.clone.1), window={size=1x1x128 pad=0_0x0_0x127_0}, to_apply=%region_0.0 | reduce-window | flops 2080768 | bytes 131076 | tf_op jit(solution)/shard_map/reduce-window
  7.0 0.1 slice.16
  7.1 0.1 copy.21
  7.3 0.1 broadcast_add_fusion
  7.4 0.1 copy.18
  7.5 0.1 mul.67
  7.6 0.7 convert.8
  8.3 0.1 copy.23
  8.4 0.1 stack_reshape.4
  8.6 0.2 copy.24
  8.8 3.3 scatter_custom_fusion
  12.1 0.8 copy.25
  13.0 7.4 %all-to-all-start = ((bf16[16,128,2]{1,2,0:T(2,128)(2,1)}), bf16[16,128,2]{1,2,0:T(2,128)(2,1)S(1)}, u32[]{:S(2)}, u32[]{:S(2)}) async-start(bf16[16,128,2]{1,2,0:T(2,128)(2,1)} %copy.25), calls=%async_computation | async-start | bytes 16384 | tf_op jit(solution)/shard_map/all_to_all | solution.py:40
  20.3 11.7 %scatter_custom_fusion.2 = bf16[2048,2048]{1,0:T(8,128)(2,1)} fusion(s32[1024]{0:T(1024)S(1)} %bitcast.55, bf16[]{:T(256)} %constant.40.clone.1, bf16[128,2048]{1,0:T(8,128)(2,1)} %param.6), kind=kCustom, calls=%fused_computation.7 | custom fusion | bytes 8912898 | tf_op jit(solution)/shard_map/scatter | solution.py:26
  32.0 6.1 %all-to-all-start.2 = ((bf16[16,128,2048]{2,1,0:T(8,128)(2,1)}), bf16[16,128,2048]{2,1,0:T(8,128)(2,1)}, u32[]{:S(2)}, u32[]{:S(2)}) async-start(bf16[16,128,2048]{2,1,0:T(8,128)(2,1)} %bitcast.43), calls=%async_computation.2 | async-start | bytes 16777216 | tf_op jit(solution)/shard_map/all_to_all | solution.py:39
  38.1 7.3 %scatter_custom_fusion.1 = bf16[2048,768]{1,0:T(8,128)(2,1)} fusion(s32[1024]{0:T(1024)S(1)} %bitcast.56, bf16[128,8,768]{2,1,0:T(8,128)(2,1)S(1)} %copy-done, bf16[]{:T(256)} %constant.40.clone.1), kind=kCustom, calls=%fused_computation.12 | custom fusion | bytes 4718594 | tf_op jit(solution)/shard_map/scatter | solution.py:23
  45.4 143.4 %all-to-all-done.2 = bf16[16,128,2048]{2,1,0:T(8,128)(2,1)} async-done(((bf16[16,128,2048]{2,1,0:T(8,128)(2,1)}), bf16[16,128,2048]{2,1,0:T(8,128)(2,1)}, u32[]{:S(2)}, u32[]{:S(2)}) %all-to-all-start.2) | async-done | bytes 8388640 | tf_op jit(solution)/shard_map/all_to_all | solution.py:39
  188.8 36.5 %all-to-all-start.1 = ((bf16[16,128,768]{2,1,0:T(8,128)(2,1)}), bf16[16,128,768]{2,1,0:T(8,128)(2,1)}, u32[]{:S(2)}, u32[]{:S(2)}) async-start(bf16[16,128,768]{2,1,0:T(8,128)(2,1)} %bitcast.44), calls=%async_computation.1 | async-start | bytes 6291456 | tf_op jit(solution)/shard_map/all_to_all | solution.py:38
  225.3 0.6 dynamic-slice
  226.6 0.2 dynamic-update-slice
  226.9 8.1 %fusion.26 = f32[16,128,128]{2,1,0:T(8,128)S(1)} fusion(bf16[16,128,2048]{2,1,0:T(8,128)(2,1)} %all-to-all-done.2), kind=kOutput, calls=%fused_computation.50 | convolution fusion | flops 1073741824 | bytes 9437184 | tf_op jit(solution)/shard_map/smd,snd->smn/dot_general | solution.py:50
  235.0 49.8 %all-to-all-done.1 = bf16[16,128,768]{2,1,0:T(8,128)(2,1)} async-done(((bf16[16,128,768]{2,1,0:T(8,128)(2,1)}), bf16[16,128,768]{2,1,0:T(8,128)(2,1)}, u32[]{:S(2)}, u32[]{:S(2)}) %all-to-all-start.1) | async-done | bytes 3145760 | tf_op jit(solution)/shard_map/all_to_all | solution.py:38
  284.8 4.3 %fusion.14 = f32[16,4]{1,0:T(8,128)S(1)} fusion(f32[16,128,128]{2,1,0:T(8,128)S(1)} %fusion.26, bf16[16,128,768]{2,1,0:T(8,128)(2,1)} %all-to-all-done.1, f32[16,128]{1,0:T(8,128)S(1)} %bitcast.53, f32[16,128]{1,0:T(8,128)S(1)} %bitcast.48), kind=kOutput, calls=%fused_computation.20 | convolution fusion | flops 405569472 | bytes 4210944 | tf_op jit(solution)/shard_map/smn,snx->smx/dot_general | solution.py:52
  289.1 44.4 %all-reduce.1 = (f32[64]{0:T(128)S(1)}, f32[16,4]{1,0:T(8,128)S(1)}) all-reduce(f32[64]{0:T(128)S(1)} %dynamic-update-slice, f32[16,4]{1,0:T(8,128)S(1)} %fusion.14), channel_id=1, replica_groups=mesh['groups'=2,'expert'=16,'dp'=1] {'expert'}, use_global_device_ids=true, to_apply=%add | all-reduce | flops 128 | bytes 1024
  333.5 0.1 reshape.120
  333.6 0.1 select_reduce_fusion
  333.7 0.5 dynamic-slice_bitcast_fusion
  334.2 11.7 %fusion.5 = bf16[1,2048,768]{2,1,0:T(8,128)(2,1)} fusion(bf16[16,128,768]{2,1,0:T(8,128)(2,1)} %all-to-all-done.1, bf16[16,128,2048]{2,1,0:T(8,128)(2,1)} %all-to-all-done.2, f32[16,128]{1,0:T(8,128)S(1)} %bitcast.52), kind=kOutput, calls=%fused_computation.10 | convolution fusion | flops 6456606720 | bytes 14688256 | tf_op jit(solution)/shard_map/dot_general | solution.py:62
  (21 shorter events, 0.2 us)
Async XLA Ops:
  0.6 37.5 %copy-start = (bf16[128,8,768]{2,1,0:T(8,128)(2,1)S(1)}, bf16[128,8,768]{2,1,0:T(8,128)(2,1)}, u32[]{:S(2)}) copy-start(bf16[128,8,768]{2,1,0:T(8,128)(2,1)} %param.5) | copy-start | bytes 4718596
  13.0 19.0 %all-to-all-start = ((bf16[16,128,2]{1,2,0:T(2,128)(2,1)}), bf16[16,128,2]{1,2,0:T(2,128)(2,1)S(1)}, u32[]{:S(2)}, u32[]{:S(2)}) async-start(bf16[16,128,2]{1,2,0:T(2,128)(2,1)} %copy.25), calls=%async_computation | async-start | bytes 16384 | tf_op jit(solution)/shard_map/all_to_all | solution.py:40
  32.0 156.8 %all-to-all-start.2 = ((bf16[16,128,2048]{2,1,0:T(8,128)(2,1)}), bf16[16,128,2048]{2,1,0:T(8,128)(2,1)}, u32[]{:S(2)}, u32[]{:S(2)}) async-start(bf16[16,128,2048]{2,1,0:T(8,128)(2,1)} %bitcast.43), calls=%async_computation.2 | async-start | bytes 16777216 | tf_op jit(solution)/shard_map/all_to_all | solution.py:39
  45.4 179.9 %copy-start.2 = (u32[32]{0:T(128)S(1)}, u32[32]{0:T(128)}, u32[]{:S(2)}) copy-start(u32[32]{0:T(128)} %constant.57) | copy-start | bytes 388
  45.4 181.2 %copy-start.1 = (f32[4]{0:T(128)S(1)}, f32[4]{0:T(128)}, u32[]{:S(2)}) copy-start(f32[4]{0:T(128)} %param.9) | copy-start | bytes 52
  188.8 96.0 %all-to-all-start.1 = ((bf16[16,128,768]{2,1,0:T(8,128)(2,1)}), bf16[16,128,768]{2,1,0:T(8,128)(2,1)}, u32[]{:S(2)}, u32[]{:S(2)}) async-start(bf16[16,128,768]{2,1,0:T(8,128)(2,1)} %bitcast.44), calls=%async_computation.1 | async-start | bytes 6291456 | tf_op jit(solution)/shard_map/all_to_all | solution.py:38
where the time goes:
time: 346 us
  waiting for transfers between devices  193 us (56%)
  starting transfers between devices  50 us (14%)
  blocking collectives  44.4 us (13%)
  local copies, waits for them, and re-layouts  26.6 us (8%)
  matrix products  24.1 us (7%)
  other arithmetic  6.24 us (2%)
    all_to_all x1, waiting for transfers between devices, per_device(): lax.all_to_all(dy_buffer, 'expert', split_axis=0, concat_axis=0, tiled=True)  143 us
    all_to_all x1, waiting for transfers between devices, per_device(): lax.all_to_all(h_buffer, 'expert', split_axis=0, concat_axis=0, tiled=True)  49.8 us
    unnamed x1, blocking collectives  44.4 us
    all_to_all x1, starting transfers between devices, per_device(): lax.all_to_all(h_buffer, 'expert', split_axis=0, concat_axis=0, tiled=True)  36.5 us
    dot_general x1, matrix products, per_device(): lax.dot_general(recv_scaled, recv_hidden, (((0, 1), (0, 1)), ((), ())), p...  11.7 us
    scatter x1, local copies, waits for them, and re-layouts, per_device(): jnp.zeros((experts * capacity, width), jnp.bfloat16).at[target]  11.7 us
    dot_general x1, matrix products, per_device(): jnp.einsum('smd,snd->smn', recv_dy, recv_dy, preferred_element_type=jnp.f...  8.1 us
    all_to_all x1, starting transfers between devices, per_device(): lax.all_to_all(info_buffer, 'expert', split_axis=0, concat_axis=0, tiled=...  7.36 us
  transfers between devices with their start and end apart: 3, of which 2 were waited for; matrix products, arithmetic and copies ran while one was open for 8% of the time, Pallas kernels for 0%

commit v1 on v0

--- a/solution.py
+++ b/solution.py
@@ -1,13 +1,20 @@
+import functools
+
 import jax
 import jax.numpy as jnp
+import numpy as np
 from jax import lax
+from jax.experimental import pallas as pl
+from jax.experimental.pallas import tpu as pltpu
 from jax.sharding import PartitionSpec as P
 
 TOPK = 8
 EXLEN = 32
-
-
-def per_device(hidden_saved, grad_out, expert_ids, gate_codes, clip_bound):
+VMEM_LIMIT = 56 * 1024 * 1024
+HIGHEST = lax.Precision.HIGHEST
+
+
+def per_device_sparse(hidden_saved, grad_out, expert_ids, gate_codes, clip_bound):
     experts = lax.axis_size("expert")
     tokens_dev = grad_out.shape[0]
     width = grad_out.shape[1]
@@ -72,7 +79,156 @@
     return (summed[None], factors)
 
 
+def norm_kernel(experts, dy_ref, hid_ref, ids_ref, gate_ref, bound_ref, meta_ref, factor_ref):
+    examples = ids_ref.shape[0]
+    pairs = EXLEN * TOPK
+    spread = (
+        lax.broadcasted_iota(jnp.int32, (pairs, EXLEN), 0) // TOPK
+        == lax.broadcasted_iota(jnp.int32, (pairs, EXLEN), 1)
+    ).astype(jnp.float32)
+    for x in range(examples):
+        ids_row = ids_ref[x : x + 1, :]
+        gate_row = gate_ref[x : x + 1, :].astype(jnp.float32) / 1024.0
+        hid = hid_ref[x * pairs : (x + 1) * pairs, :]
+        dy = dy_ref[x * EXLEN : (x + 1) * EXLEN, :]
+        hid_gram = lax.dot_general(hid, hid, (((1,), (1,)), ((), ())), preferred_element_type=jnp.float32)
+        dy_gram = lax.dot_general(dy, dy, (((1,), (1,)), ((), ())), preferred_element_type=jnp.float32)
+        half = jnp.dot(spread, dy_gram, precision=HIGHEST, preferred_element_type=jnp.float32)
+        pair_gram = lax.dot_general(
+            half, spread, (((1,), (1,)), ((), ())), precision=HIGHEST, preferred_element_type=jnp.float32
+        )
+        onehot = (lax.broadcasted_iota(jnp.int32, (experts, pairs), 0) == ids_row).astype(jnp.float32)
+        same = lax.dot_general(onehot, onehot, (((0,), (0,)), ((), ())), preferred_element_type=jnp.float32)
+        weights = hid_gram * pair_gram * same
+        sums = jnp.dot(gate_row, weights, precision=HIGHEST, preferred_element_type=jnp.float32)
+        norm = jnp.sum(sums * gate_row, axis=1, keepdims=True)
+        factor = jnp.minimum(1.0, bound_ref[x : x + 1, :] / jnp.sqrt(norm + 1e-06))
+        factor_ref[x : x + 1, :] = factor
+        meta_ref[x : x + 1, :] = factor * gate_row
+        meta_ref[examples + x : examples + x + 1, :] = ids_row.astype(jnp.float32)
+
+
+def build_kernel(chips, place_ref, own_ref, sib_ref, own_meta_ref, sib_meta_ref, *out_refs):
+    examples = own_meta_ref.shape[0] // 2
+    pairs = EXLEN * TOPK
+    rows = chips * EXLEN
+    me = place_ref[0]
+    row = lax.broadcasted_iota(jnp.int32, (rows, pairs), 0)
+    lane = lax.broadcasted_iota(jnp.int32, (rows, pairs), 1)
+    same_token = (row % EXLEN) == (lane // TOPK)
+    expert = (lax.bitwise_xor(row // EXLEN, me // 2) * 2 + me % 2).astype(jnp.float32)
+    for side, (hid_ref, meta_ref) in enumerate(((own_ref, own_meta_ref), (sib_ref, sib_meta_ref))):
+        for x in range(examples):
+            hit = same_token & (meta_ref[examples + x : examples + x + 1, :] == expert)
+            scale = jnp.sum(jnp.where(hit, meta_ref[x : x + 1, :], 0.0), axis=1, keepdims=True)
+            picked = jnp.dot(
+                hit.astype(jnp.float32).astype(jnp.bfloat16),
+                hid_ref[x * pairs : (x + 1) * pairs, :],
+                preferred_element_type=jnp.float32,
+            )
+            message = (picked * scale).astype(jnp.bfloat16)
+            start = (side * examples + x) * EXLEN
+            for j in range(chips):
+                out_refs[j][start : start + EXLEN, :] = message[j * EXLEN : (j + 1) * EXLEN, :]
+
+
+def product_kernel(chips, tokens, pos_ref, own_ref, sib_ref, *refs):
+    hid_refs, out_ref = refs[:chips], refs[chips]
+    total = None
+    for j in range(chips):
+        begin = pl.multiple_of(pos_ref[j] * tokens, tokens)
+        dy = jnp.concatenate([own_ref[pl.ds(begin, tokens), :], sib_ref[pl.ds(begin, tokens), :]], axis=0)
+        term = lax.dot_general(
+            dy, hid_refs[j][...], (((0,), (0,)), ((), ())), preferred_element_type=jnp.float32
+        )
+        total = term if total is None else total + term
+    out_ref[...] = total.astype(jnp.bfloat16)
+
+
+def per_device_dense(hidden_saved, grad_out, expert_ids, gate_codes, clip_bound):
+    devices = lax.axis_size("expert")
+    chips = devices // 2
+    tokens, width = grad_out.shape
+    hidden = hidden_saved.shape[2]
+    examples = clip_bound.shape[0]
+    pairs = EXLEN * TOPK
+    me = lax.axis_index("expert")
+    ring = list(range(0, chips, 2)) + list(range(chips - 1, 0, -2))
+    params = pltpu.CompilerParams(vmem_limit_bytes=VMEM_LIMIT)
+
+    def swap(array, offset):
+        return lax.ppermute(array, "expert", [(i, i ^ offset) for i in range(devices)])
+
+    own_dy = lax.all_gather(
+        grad_out,
+        "expert",
+        axis=0,
+        tiled=True,
+        axis_index_groups=[[2 * chip + core for chip in ring] for core in range(2)],
+    )
+    hid_rows = hidden_saved.reshape(tokens * TOPK, hidden)
+    sib_rows = swap(hid_rows, 1)
+    meta, factors = pl.pallas_call(
+        functools.partial(norm_kernel, devices),
+        out_shape=(
+            jax.ShapeDtypeStruct((2 * examples, pairs), jnp.float32),
+            jax.ShapeDtypeStruct((examples, 1), jnp.float32),
+        ),
+        compiler_params=params,
+        name="norms",
+    )(
+        grad_out,
+        hid_rows,
+        expert_ids.reshape(examples, pairs),
+        gate_codes.reshape(examples, pairs),
+        clip_bound.reshape(examples, 1),
+    )
+    sib_meta = swap(meta, 1)
+    messages = pl.pallas_call(
+        functools.partial(build_kernel, chips),
+        out_shape=[jax.ShapeDtypeStruct((2 * tokens, hidden), jnp.bfloat16)] * chips,
+        in_specs=[pl.BlockSpec(memory_space=pltpu.SMEM)] + [pl.BlockSpec(memory_space=pltpu.VMEM)] * 4,
+        compiler_params=params,
+        name="build",
+    )(me.astype(jnp.int32).reshape(1), hid_rows, sib_rows, meta, sib_meta)
+    order = sorted(range(1, chips), key=lambda j: (-(j // 4 > 0), j))
+    slots = {0: messages[0]}
+    for j in order:
+        slots[j] = swap(messages[j], 2 * j)
+    own_dy = lax.optimization_barrier((own_dy, slots[order[0]]))[0]
+    sib_dy = swap(own_dy, 1)
+    where = np.argsort(np.array(ring)).astype(np.int32)
+    position = jnp.asarray(where)[jnp.arange(chips, dtype=jnp.int32) ^ (me // 2)]
+    block = 256
+    summed = pl.pallas_call(
+        functools.partial(product_kernel, chips, tokens),
+        out_shape=jax.ShapeDtypeStruct((width, hidden), jnp.bfloat16),
+        grid_spec=pltpu.PrefetchScalarGridSpec(
+            num_scalar_prefetch=1,
+            grid=(width // block,),
+            in_specs=[pl.BlockSpec((chips * tokens, block), lambda i, pos: (0, i))] * 2
+            + [pl.BlockSpec((2 * tokens, hidden), lambda i, pos: (0, 0))] * chips,
+            out_specs=pl.BlockSpec((block, hidden), lambda i, pos: (i, 0)),
+        ),
+        compiler_params=params,
+        name="product",
+    )(position, own_dy, sib_dy, *[slots[j] for j in range(chips)])
+    return (summed[None], factors.reshape(examples))
+
+
 def solution(mesh):
+    def per_device(hidden_saved, grad_out, expert_ids, gate_codes, clip_bound):
+        devices = mesh.shape["expert"]
+        tokens = grad_out.shape[0]
+        dense = (
+            mesh.shape["dp"] == 1
+            and devices >= 4
+            and devices & (devices - 1) == 0
+            and 2 * tokens * TOPK // devices >= tokens
+        )
+        run = per_device_dense if dense else per_device_sparse
+        return run(hidden_saved, grad_out, expert_ids, gate_codes, clip_bound)
+
     return jax.shard_map(
         per_device,
         mesh=mesh,

time: 346 us -> 154 us (0.45)
  the two profiles are of different devices: /device:TPU:0 before, /device:TPU:9 now
where the time goes in v1:
time: 154 us; the launch traced here: 152 us
  waiting for transfers between devices  97.9 us (64%)
  Pallas kernels  24.4 us (16%)
  between operations  14.1 us (9%)
  starting transfers between devices  8.12 us (5%)
  local copies, waits for them, and re-layouts  7.33 us (5%)
    ppermute x10, waiting for transfers between devices, swap(): lax.ppermute(array, 'expert', [(i, i ^ offset) for i in range(devices)])  76.8 us
    all_gather x1, waiting for transfers between devices, per_device_dense(): lax.all_gather(grad_out, 'expert', axis=0, tiled=True, axis_index_groups=...  20.4 us
    pallas_call x1, Pallas kernels, per_device_dense(): pl.pallas_call(functools.partial(product_kernel, chips, tokens), out_shap...  13 us
    ppermute x10, starting transfers between devices, swap(): lax.ppermute(array, 'expert', [(i, i ^ offset) for i in range(devices)])  8.08 us
    pallas_call x1, Pallas kernels, per_device_dense(): pl.pallas_call(functools.partial(norm_kernel, devices), out_shape=(jax.Sh...  6.77 us
    pallas_call x1, Pallas kernels, per_device_dense(): pl.pallas_call(functools.partial(build_kernel, chips), out_shape=[jax.Sha...  4.61 us
    unnamed x24, local copies, waits for them, and re-layouts  3.47 us
  transfers between devices with their start and end apart: 11, of which 9 were waited for; matrix products, arithmetic and copies ran while one was open for 4% of the time, Pallas kernels for 7%

profile of v1, /device:TPU:9, one launch (start us, length us, event | category | flops | bytes accessed | tf_op | source)
XLA Modules:
  0.0 152.5 jit_solution(12553089813908216463)
XLA Ops:
  7.2 0.0 all-gather.2.cloned.1.call-start
  7.2 0.7 all-gather.2.cloned.1.call-update
  7.9 0.7 collective-permute-start
  8.7 1.3 copy.13.bound_ref
  10.0 0.8 copy.11
  10.8 0.7 reshape.40.ids_ref
  11.4 0.8 copy.12
  12.2 0.7 reshape.41.gate_ref
  12.9 6.8 %norms.1 = (f32[8,256]{1,0:T(8,128)}, f32[4,1]{1,0:T(4,128)}) custom-call(bf16[128,2048]{1,0:T(8,128)(2,1)} %dy_ref.1, bf16[1024,768]{1,0:T(8,128)(2,1)} %bitcast.7, s32[4,256]{1,0:T(4,128)} %reshape.40.ids_ref, s32[4,256]{1,0:T(4,128)} %reshape.41.gate_ref, f32[4,1]{1,0:T(4,128)} %copy.13.bound_ref), custom_call_target="tpu_custom_call" | custom-call | tf_op jit(solution)/shard_map/norms/pallas_call | solution.py:171
  19.7 1.4 collective-permute-done.1.sib_meta_ref
  21.1 0.6 copy-done.9
  21.7 0.6 copy-done.1
  22.2 4.6 %build.1 = (bf16[256,768]{1,0:T(8,128)(2,1)}, bf16[256,768]{1,0:T(8,128)(2,1)}, bf16[256,768]{1,0:T(8,128)(2,1)}, bf16[256,768]{1,0:T(8,128)(2,1)}, bf16[256,768...) custom-call(s32[1]{0:T(128)} %bitcast.1.place_ref, ...), custom_call_target="tpu_custom_call" | custom-call | tf_op jit(solution)/shard_map/build/pallas_call | solution.py:187
  26.8 2.3 %collective-permute-start.2 = (bf16[256,768]{1,0:T(8,128)(2,1)}, bf16[256,768]{1,0:T(8,128)(2,1)S(1)}, u32[]{:S(2)}, u32[]{:S(2)}) collective-permute-start(bf16[256,768]{1,0:T(8,128)(2,1)} %get-tuple-element.14), channel_id=1, source_target_pairs={{0,8},{1,9},{2,10},{3,11},{4,12},{5,13},{6,14},{7,15},{8,0},{9,1},... | collective-permute-start | bytes 1179656 | tf_op jit(solution)/shard_map/ppermute | solution.py:160
  29.1 25.9 %collective-permute-done.2.refs_4_ = bf16[256,768]{1,0:T(8,128)(2,1)S(1)} collective-permute-done((bf16[256,768]{1,0:T(8,128)(2,1)}, bf16[256,768]{1,0:T(8,128)(2,1)S(1)}, u32[]{:S(2)}, u32[]{:S(2)}) %collective-permute-start.2) | collective-permute-done | bytes 393248 | tf_op jit(solution)/shard_map/ppermute | solution.py:160
  55.1 20.4 %all-gather.2.cloned.1.call-done.own_ref = bf16[1024,2048]{1,0:T(8,128)(2,1)} async-done(((bf16[128,2048]{1,0:T(8,128)(2,1)}), bf16[1024,2048]{1,0:T(8,128)(2,1)}) %all-gather.2.cloned.1.call-update) | async-done | bytes 4194320 | tf_op jit(solution)/shard_map/all_gather | solution.py:162
  75.5 0.7 collective-permute-start.3
  76.2 1.2 collective-permute-start.4
  77.4 1.4 collective-permute-start.6
  78.8 1.0 collective-permute-start.7
  79.8 7.3 %collective-permute-done.4.refs_1_ = bf16[256,768]{1,0:T(8,128)(2,1)S(1)} collective-permute-done((bf16[256,768]{1,0:T(8,128)(2,1)}, bf16[256,768]{1,0:T(8,128)(2,1)S(1)}, u32[]{:S(2)}, u32[]{:S(2)}) %collective-permute-start.4) | collective-permute-done | bytes 393248 | tf_op jit(solution)/shard_map/ppermute | solution.py:160
  87.1 0.4 collective-permute-start.8
  87.5 7.2 %collective-permute-done.5.refs_2_ = bf16[256,768]{1,0:T(8,128)(2,1)S(1)} collective-permute-done((bf16[256,768]{1,0:T(8,128)(2,1)}, bf16[256,768]{1,0:T(8,128)(2,1)S(1)}, u32[]{:S(2)}, u32[]{:S(2)}) %collective-permute-start.5) | collective-permute-done | bytes 393248 | tf_op jit(solution)/shard_map/ppermute | solution.py:160
  94.7 0.3 collective-permute-start.9
  95.0 1.2 gather_fusion
  96.2 0.6 reduce
  96.8 6.3 %collective-permute-done.6.refs_3_ = bf16[256,768]{1,0:T(8,128)(2,1)S(1)} collective-permute-done((bf16[256,768]{1,0:T(8,128)(2,1)}, bf16[256,768]{1,0:T(8,128)(2,1)S(1)}, u32[]{:S(2)}, u32[]{:S(2)}) %collective-permute-start.6) | collective-permute-done | bytes 393248 | tf_op jit(solution)/shard_map/ppermute | solution.py:160
  103.1 1.9 %collective-permute-done.7.refs_5_ = bf16[256,768]{1,0:T(8,128)(2,1)S(1)} collective-permute-done((bf16[256,768]{1,0:T(8,128)(2,1)}, bf16[256,768]{1,0:T(8,128)(2,1)S(1)}, u32[]{:S(2)}, u32[]{:S(2)}) %collective-permute-start.7) | collective-permute-done | bytes 393248 | tf_op jit(solution)/shard_map/ppermute | solution.py:160
  105.0 18.8 %collective-permute-done.8.refs_6_ = bf16[256,768]{1,0:T(8,128)(2,1)S(1)} collective-permute-done((bf16[256,768]{1,0:T(8,128)(2,1)}, bf16[256,768]{1,0:T(8,128)(2,1)S(1)}, u32[]{:S(2)}, u32[]{:S(2)}) %collective-permute-start.8) | collective-permute-done | bytes 393248 | tf_op jit(solution)/shard_map/ppermute | solution.py:160
  123.8 8.0 %collective-permute-done.9.refs_7_ = bf16[256,768]{1,0:T(8,128)(2,1)S(1)} collective-permute-done((bf16[256,768]{1,0:T(8,128)(2,1)}, bf16[256,768]{1,0:T(8,128)(2,1)S(1)}, u32[]{:S(2)}, u32[]{:S(2)}) %collective-permute-start.9) | collective-permute-done | bytes 393248 | tf_op jit(solution)/shard_map/ppermute | solution.py:160
  131.9 0.7 copy-done.8
  132.6 13.0 %product.1 = bf16[2048,768]{1,0:T(8,128)(2,1)} custom-call(s32[8]{0:T(128)} %gather_fusion, bf16[1024,2048]{1,0:T(8,128)(2,1)} %all-gather.2.cloned.1.call-done.own_ref, bf16[1024,2048]{1,0:T(8,128)(2,1)} %collective-permute-done.3.sib_ref, bf16[256,768]{1,0:T(8,128)(2,1)} %get-tuple-element.16.refs_0_, bf16[256,768]{1,0:T(8,128)(2,1)} %copy-done.3, ...), custom_call_target="tpu_custom_call" | custom-call | tf_op jit(solution)/shard_map/product/pallas_call | solution.py:203
  (25 shorter events, 0.1 us)
Async XLA Ops:
  7.2 87.9 %copy-start = (s32[8]{0:T(128)S(1)}, s32[8]{0:T(128)}, u32[]{:S(2)}) copy-start(s32[8]{0:T(128)} %constant.23.clone) | copy-start | bytes 100
  7.2 68.3 %all-gather.2.cloned.1.call-start = ((), (), s32[]{:S(2)}) async-start(), calls=%async_computation | async-start | bytes 4718592 | tf_op jit(solution)/shard_map/all_gather | solution.py:162
  7.9 13.2 %collective-permute-start = (bf16[1024,768]{1,0:T(8,128)(2,1)}, bf16[1024,768]{1,0:T(8,128)(2,1)S(1)}, u32[]{:S(2)}, u32[]{:S(2)}) collective-permute-start(bf16[1024,768]{1,0:T(8,128)(2,1)} %bitcast.6), channel_id=1, source_target_pairs={{0,1},{1,0},{2,3},{3,2},{4,5},{5,4},{6,7},{7,6},{8,9},{9,8},{10,11... | collective-permute-start | bytes 4718600 | tf_op jit(solution)/shard_map/ppermute | solution.py:160
  19.7 76.5 %copy-start.10 = (f32[4,1]{1,0:T(4,128)S(1)}, f32[4,1]{1,0:T(4,128)}, u32[]{:S(2)}) copy-start(f32[4,1]{1,0:T(4,128)} %get-tuple-element.23) | copy-start | bytes 52
  19.7 1.4 collective-permute-start.1
  21.1 0.6 copy-start.9
  21.1 1.1 copy-start.1
  26.8 28.2 %collective-permute-start.2 = (bf16[256,768]{1,0:T(8,128)(2,1)}, bf16[256,768]{1,0:T(8,128)(2,1)S(1)}, u32[]{:S(2)}, u32[]{:S(2)}) collective-permute-start(bf16[256,768]{1,0:T(8,128)(2,1)} %get-tuple-element.14), channel_id=1, source_target_pairs={{0,8},{1,9},{2,10},{3,11},{4,12},{5,13},{6,14},{7,15},{8,0},{9,1},... | collective-permute-start | bytes 1179656 | tf_op jit(solution)/shard_map/ppermute | solution.py:160
  55.1 76.8 %copy-start.2 = (bf16[256,768]{1,0:T(8,128)(2,1)}, bf16[256,768]{1,0:T(8,128)(2,1)S(1)}, u32[]{:S(2)}) copy-start(bf16[256,768]{1,0:T(8,128)(2,1)S(1)} %collective-permute-done.2.refs_4_) | copy-start | bytes 1179652
  75.5 56.4 %collective-permute-start.3 = (bf16[1024,2048]{1,0:T(8,128)(2,1)}, bf16[1024,2048]{1,0:T(8,128)(2,1)}, u32[]{:S(2)}, u32[]{:S(2)}) collective-permute-start(bf16[1024,2048]{1,0:T(8,128)(2,1)} %all-gather.2.cloned.1.call-done.own_ref), channel_id=1, source_target_pairs={{0,1},{1,0},{2,3},{3,2},{4,5},{5,4},{6,7},{7,6},{8,9},{9,8},{10,11... | collective-permute-start | bytes 12582920 | tf_op jit(solution)/shard_map/ppermute | solution.py:160
  76.2 11.0 %collective-permute-start.4 = (bf16[256,768]{1,0:T(8,128)(2,1)}, bf16[256,768]{1,0:T(8,128)(2,1)S(1)}, u32[]{:S(2)}, u32[]{:S(2)}) collective-permute-start(bf16[256,768]{1,0:T(8,128)(2,1)} %get-tuple-element.17), channel_id=1, source_target_pairs={{0,2},{1,3},{2,0},{3,1},{4,6},{5,7},{6,4},{7,5},{8,10},{9,11},{10,... | collective-permute-start | bytes 1179656 | tf_op jit(solution)/shard_map/ppermute | solution.py:160
  77.4 17.3 %collective-permute-start.5 = (bf16[256,768]{1,0:T(8,128)(2,1)}, bf16[256,768]{1,0:T(8,128)(2,1)S(1)}, u32[]{:S(2)}, u32[]{:S(2)}) collective-permute-start(bf16[256,768]{1,0:T(8,128)(2,1)} %get-tuple-element.18), channel_id=1, source_target_pairs={{0,4},{1,5},{2,6},{3,7},{4,0},{5,1},{6,2},{7,3},{8,12},{9,13},{10,... | collective-permute-start | bytes 1179656 | tf_op jit(solution)/shard_map/ppermute | solution.py:160
  77.4 25.7 %collective-permute-start.6 = (bf16[256,768]{1,0:T(8,128)(2,1)}, bf16[256,768]{1,0:T(8,128)(2,1)S(1)}, u32[]{:S(2)}, u32[]{:S(2)}) collective-permute-start(bf16[256,768]{1,0:T(8,128)(2,1)} %get-tuple-element.19), channel_id=1, source_target_pairs={{0,6},{1,7},{2,4},{3,5},{4,2},{5,3},{6,0},{7,1},{8,14},{9,15},{10,... | collective-permute-start | bytes 1179656 | tf_op jit(solution)/shard_map/ppermute | solution.py:160
  78.8 26.2 %collective-permute-start.7 = (bf16[256,768]{1,0:T(8,128)(2,1)}, bf16[256,768]{1,0:T(8,128)(2,1)S(1)}, u32[]{:S(2)}, u32[]{:S(2)}) collective-permute-start(bf16[256,768]{1,0:T(8,128)(2,1)} %get-tuple-element.20), channel_id=1, source_target_pairs={{0,10},{1,11},{2,8},{3,9},{4,14},{5,15},{6,12},{7,13},{8,2},{9,3},... | collective-permute-start | bytes 1179656 | tf_op jit(solution)/shard_map/ppermute | solution.py:160
  87.1 44.7 %copy-start.3 = (bf16[256,768]{1,0:T(8,128)(2,1)}, bf16[256,768]{1,0:T(8,128)(2,1)S(1)}, u32[]{:S(2)}) copy-start(bf16[256,768]{1,0:T(8,128)(2,1)S(1)} %collective-permute-done.4.refs_1_) | copy-start | bytes 1179652
  87.1 36.7 %collective-permute-start.8 = (bf16[256,768]{1,0:T(8,128)(2,1)}, bf16[256,768]{1,0:T(8,128)(2,1)S(1)}, u32[]{:S(2)}, u32[]{:S(2)}) collective-permute-start(bf16[256,768]{1,0:T(8,128)(2,1)} %get-tuple-element.21), channel_id=1, source_target_pairs={{0,12},{1,13},{2,14},{3,15},{4,8},{5,9},{6,10},{7,11},{8,4},{9,5},... | collective-permute-start | bytes 1179656 | tf_op jit(solution)/shard_map/ppermute | solution.py:160
  94.7 37.2 %copy-start.4 = (bf16[256,768]{1,0:T(8,128)(2,1)}, bf16[256,768]{1,0:T(8,128)(2,1)S(1)}, u32[]{:S(2)}) copy-start(bf16[256,768]{1,0:T(8,128)(2,1)S(1)} %collective-permute-done.5.refs_2_) | copy-start | bytes 1179652
  94.7 37.2 %collective-permute-start.9 = (bf16[256,768]{1,0:T(8,128)(2,1)}, bf16[256,768]{1,0:T(8,128)(2,1)S(1)}, u32[]{:S(2)}, u32[]{:S(2)}) collective-permute-start(bf16[256,768]{1,0:T(8,128)(2,1)} %get-tuple-element.22), channel_id=1, source_target_pairs={{0,14},{1,15},{2,12},{3,13},{4,10},{5,11},{6,8},{7,9},{8,6},{9,7},... | collective-permute-start | bytes 1179656 | tf_op jit(solution)/shard_map/ppermute | solution.py:160
  103.1 28.8 %copy-start.5 = (bf16[256,768]{1,0:T(8,128)(2,1)}, bf16[256,768]{1,0:T(8,128)(2,1)S(1)}, u32[]{:S(2)}) copy-start(bf16[256,768]{1,0:T(8,128)(2,1)S(1)} %collective-permute-done.6.refs_3_) | copy-start | bytes 1179652
  105.0 26.9 %copy-start.6 = (bf16[256,768]{1,0:T(8,128)(2,1)}, bf16[256,768]{1,0:T(8,128)(2,1)S(1)}, u32[]{:S(2)}) copy-start(bf16[256,768]{1,0:T(8,128)(2,1)S(1)} %collective-permute-done.7.refs_5_) | copy-start | bytes 1179652
  123.8 8.1 %copy-start.7 = (bf16[256,768]{1,0:T(8,128)(2,1)}, bf16[256,768]{1,0:T(8,128)(2,1)S(1)}, u32[]{:S(2)}) copy-start(bf16[256,768]{1,0:T(8,128)(2,1)S(1)} %collective-permute-done.8.refs_6_) | copy-start | bytes 1179652
  131.8 0.8 copy-start.8
Sparse Core Ops, SparseCore 0:
  9.5 65.8 all-gather.1

commit v2 on v1

--- a/solution.py
+++ b/solution.py
@@ -2,7 +2,6 @@
 
 import jax
 import jax.numpy as jnp
-import numpy as np
 from jax import lax
 from jax.experimental import pallas as pl
 from jax.experimental.pallas import tpu as pltpu
@@ -80,15 +79,27 @@
 
 
 def norm_kernel(experts, dy_ref, hid_ref, ids_ref, gate_ref, bound_ref, meta_ref, factor_ref):
-    examples = ids_ref.shape[0]
+    examples = bound_ref.shape[1]
+    tokens = dy_ref.shape[0]
     pairs = EXLEN * TOPK
     spread = (
         lax.broadcasted_iota(jnp.int32, (pairs, EXLEN), 0) // TOPK
         == lax.broadcasted_iota(jnp.int32, (pairs, EXLEN), 1)
     ).astype(jnp.float32)
+    token = lax.broadcasted_iota(jnp.int32, (tokens, tokens * TOPK), 0)
+    place = lax.broadcasted_iota(jnp.int32, (tokens, tokens * TOPK), 1)
+    widen = (token == place // TOPK).astype(jnp.float32).astype(jnp.bfloat16)
+    codes = jnp.concatenate([ids_ref[...], gate_ref[...]], axis=0).astype(jnp.float32).astype(jnp.bfloat16)
+    wide = jnp.dot(codes, widen, preferred_element_type=jnp.float32)
+    rank = lax.broadcasted_iota(jnp.int32, wide.shape, 0)
+    own = rank % TOPK == lax.broadcasted_iota(jnp.int32, wide.shape, 1) % TOPK
+    wide = jnp.where(own, wide, 0.0)
+    ids_all = jnp.sum(wide[:TOPK], axis=0, keepdims=True)
+    gate_all = jnp.sum(wide[TOPK:], axis=0, keepdims=True) / 1024.0
+    factor_row = jnp.zeros((1, examples), jnp.float32)
     for x in range(examples):
-        ids_row = ids_ref[x : x + 1, :]
-        gate_row = gate_ref[x : x + 1, :].astype(jnp.float32) / 1024.0
+        ids_row = ids_all[:, x * pairs : (x + 1) * pairs]
+        gate_row = gate_all[:, x * pairs : (x + 1) * pairs]
         hid = hid_ref[x * pairs : (x + 1) * pairs, :]
         dy = dy_ref[x * EXLEN : (x + 1) * EXLEN, :]
         hid_gram = lax.dot_general(hid, hid, (((1,), (1,)), ((), ())), preferred_element_type=jnp.float32)
@@ -97,15 +108,18 @@
         pair_gram = lax.dot_general(
             half, spread, (((1,), (1,)), ((), ())), precision=HIGHEST, preferred_element_type=jnp.float32
         )
-        onehot = (lax.broadcasted_iota(jnp.int32, (experts, pairs), 0) == ids_row).astype(jnp.float32)
+        name = lax.broadcasted_iota(jnp.int32, (experts, pairs), 0).astype(jnp.float32)
+        onehot = (name == ids_row).astype(jnp.float32)
         same = lax.dot_general(onehot, onehot, (((0,), (0,)), ((), ())), preferred_element_type=jnp.float32)
         weights = hid_gram * pair_gram * same
         sums = jnp.dot(gate_row, weights, precision=HIGHEST, preferred_element_type=jnp.float32)
         norm = jnp.sum(sums * gate_row, axis=1, keepdims=True)
-        factor = jnp.minimum(1.0, bound_ref[x : x + 1, :] / jnp.sqrt(norm + 1e-06))
-        factor_ref[x : x + 1, :] = factor
+        factor = jnp.minimum(1.0, bound_ref[:, x : x + 1] / jnp.sqrt(norm + 1e-06))
+        lane = lax.broadcasted_iota(jnp.int32, (1, examples), 1)
+        factor_row = jnp.where(lane == x, factor, factor_row)
         meta_ref[x : x + 1, :] = factor * gate_row
-        meta_ref[examples + x : examples + x + 1, :] = ids_row.astype(jnp.float32)
+        meta_ref[examples + x : examples + x + 1, :] = ids_row
+    factor_ref[...] = factor_row
 
 
 def build_kernel(chips, place_ref, own_ref, sib_ref, own_meta_ref, sib_meta_ref, *out_refs):
@@ -132,17 +146,50 @@
                 out_refs[j][start : start + EXLEN, :] = message[j * EXLEN : (j + 1) * EXLEN, :]
 
 
-def product_kernel(chips, tokens, pos_ref, own_ref, sib_ref, *refs):
-    hid_refs, out_ref = refs[:chips], refs[chips]
-    total = None
-    for j in range(chips):
-        begin = pl.multiple_of(pos_ref[j] * tokens, tokens)
-        dy = jnp.concatenate([own_ref[pl.ds(begin, tokens), :], sib_ref[pl.ds(begin, tokens), :]], axis=0)
+def product_kernel(places, count, has_total, *refs):
+    dy_refs, hid_refs, out_ref = refs[:count], refs[count : count + len(places)], refs[-1]
+    total = refs[-2][...] if has_total else None
+    for hid_ref, sides in zip(hid_refs, places):
+        dy = jnp.concatenate([dy_refs[k][begin : begin + rows, :] for k, begin, rows in sides], axis=0)
         term = lax.dot_general(
-            dy, hid_refs[j][...], (((0,), (0,)), ((), ())), preferred_element_type=jnp.float32
+            dy, hid_ref[...], (((0,), (0,)), ((), ())), preferred_element_type=jnp.float32
         )
         total = term if total is None else total + term
-    out_ref[...] = total.astype(jnp.bfloat16)
+    out_ref[...] = total.astype(out_ref.dtype)
+
+
+def product(name, offsets, slots, where, total, dtype):
+    arrays, places = [], []
+    for j in offsets:
+        sides = []
+        for array, begin, rows in where[j]:
+            known = [k for k, other in enumerate(arrays) if other is array]
+            if not known:
+                arrays.append(array)
+            sides.append((known[0] if known else len(arrays) - 1, begin, rows))
+        places.append(sides)
+    width, hidden = arrays[0].shape[1], slots[0].shape[1]
+    block = min(width, 256)
+    operands = arrays + [slots[j] for j in offsets]
+    specs = [pl.BlockSpec((array.shape[0], block), lambda i: (0, i)) for array in arrays]
+    specs += [pl.BlockSpec(slots[j].shape, lambda i: (0, 0)) for j in offsets]
+    if total is not None:
+        operands.append(total)
+        specs.append(pl.BlockSpec((block, hidden), lambda i: (i, 0)))
+    return pl.pallas_call(
+        functools.partial(product_kernel, places, len(arrays), total is not None),
+        out_shape=jax.ShapeDtypeStruct((width, hidden), dtype),
+        grid=(width // block,),
+        in_specs=specs,
+        out_specs=pl.BlockSpec((block, hidden), lambda i: (i, 0)),
+        compiler_params=pltpu.CompilerParams(vmem_limit_bytes=VMEM_LIMIT),
+        cost_estimate=pl.CostEstimate(
+            flops=2 * width * hidden * sum(slots[j].shape[0] for j in offsets),
+            bytes_accessed=sum(a.size * a.dtype.itemsize for a in operands) + width * hidden * 4,
+            transcendentals=0,
+        ),
+        name=name,
+    )(*operands)
 
 
 def per_device_dense(hidden_saved, grad_out, expert_ids, gate_codes, clip_bound):
@@ -153,66 +200,64 @@
     examples = clip_bound.shape[0]
     pairs = EXLEN * TOPK
     me = lax.axis_index("expert")
-    ring = list(range(0, chips, 2)) + list(range(chips - 1, 0, -2))
     params = pltpu.CompilerParams(vmem_limit_bytes=VMEM_LIMIT)
 
     def swap(array, offset):
         return lax.ppermute(array, "expert", [(i, i ^ offset) for i in range(devices)])
 
-    own_dy = lax.all_gather(
-        grad_out,
-        "expert",
-        axis=0,
-        tiled=True,
-        axis_index_groups=[[2 * chip + core for chip in ring] for core in range(2)],
-    )
+    def after(arrays, done):
+        return lax.optimization_barrier(tuple(arrays) + tuple(done))[: len(arrays)]
+
     hid_rows = hidden_saved.reshape(tokens * TOPK, hidden)
     sib_rows = swap(hid_rows, 1)
+    dy_z2, dy_z1, dy_x = swap(grad_out, 8), swap(grad_out, 4), swap(grad_out, 2)
     meta, factors = pl.pallas_call(
         functools.partial(norm_kernel, devices),
         out_shape=(
             jax.ShapeDtypeStruct((2 * examples, pairs), jnp.float32),
-            jax.ShapeDtypeStruct((examples, 1), jnp.float32),
+            jax.ShapeDtypeStruct((1, examples), jnp.float32),
         ),
         compiler_params=params,
         name="norms",
-    )(
-        grad_out,
-        hid_rows,
-        expert_ids.reshape(examples, pairs),
-        gate_codes.reshape(examples, pairs),
-        clip_bound.reshape(examples, 1),
-    )
+    )(grad_out, hid_rows, expert_ids.T, gate_codes.T, clip_bound.reshape(1, examples))
     sib_meta = swap(meta, 1)
-    messages = pl.pallas_call(
+    slots = pl.pallas_call(
         functools.partial(build_kernel, chips),
         out_shape=[jax.ShapeDtypeStruct((2 * tokens, hidden), jnp.bfloat16)] * chips,
         in_specs=[pl.BlockSpec(memory_space=pltpu.SMEM)] + [pl.BlockSpec(memory_space=pltpu.VMEM)] * 4,
         compiler_params=params,
         name="build",
     )(me.astype(jnp.int32).reshape(1), hid_rows, sib_rows, meta, sib_meta)
-    order = sorted(range(1, chips), key=lambda j: (-(j // 4 > 0), j))
-    slots = {0: messages[0]}
-    for j in order:
-        slots[j] = swap(messages[j], 2 * j)
-    own_dy = lax.optimization_barrier((own_dy, slots[order[0]]))[0]
-    sib_dy = swap(own_dy, 1)
-    where = np.argsort(np.array(ring)).astype(np.int32)
-    position = jnp.asarray(where)[jnp.arange(chips, dtype=jnp.int32) ^ (me // 2)]
-    block = 256
-    summed = pl.pallas_call(
-        functools.partial(product_kernel, chips, tokens),
-        out_shape=jax.ShapeDtypeStruct((width, hidden), jnp.bfloat16),
-        grid_spec=pltpu.PrefetchScalarGridSpec(
-            num_scalar_prefetch=1,
-            grid=(width // block,),
-            in_specs=[pl.BlockSpec((chips * tokens, block), lambda i, pos: (0, i))] * 2
-            + [pl.BlockSpec((2 * tokens, hidden), lambda i, pos: (0, 0))] * chips,
-            out_specs=pl.BlockSpec((block, hidden), lambda i, pos: (i, 0)),
-        ),
-        compiler_params=params,
-        name="product",
-    )(position, own_dy, sib_dy, *[slots[j] for j in range(chips)])
+    slots = list(slots)
+    slots[1] = swap(slots[1], 2)
+    first = (dy_z2, dy_z1, dy_x, slots[1])
+
+    near = jnp.concatenate([grad_out, dy_z1, dy_x, dy_z2])
+    both = jnp.concatenate([dy_z1, dy_z2])
+    slot4, slot6, slot3, dy_z2b, both, near = after((slots[4], slots[6], slots[3], dy_z2, both, near), first)
+    slots[4], slots[6], slots[3] = swap(slot4, 8), swap(slot6, 12), swap(slot3, 6)
+    dy_z3, dy_xz, sib_near = swap(dy_z2b, 4), swap(both, 2), swap(near, 1)
+    second = (slots[4], slots[6], slots[3], dy_z3, dy_xz, sib_near)
+
+    far = jnp.concatenate([dy_z3, dy_xz])
+    slot5, slot7, slot2, dy_z3b, far = after((slots[5], slots[7], slots[2], dy_z3, far), second)
+    slots[5], slots[7], slots[2] = swap(slot5, 10), swap(slot7, 14), swap(slot2, 4)
+    dy_xz3, sib_far = swap(dy_z3b, 2), swap(far, 1)
+    third = (slots[5], slots[7], slots[2], dy_xz3, sib_far)
+    sib_last = swap(after((dy_xz3,), third)[0], 1)
+
+    t = tokens
+    where = {
+        0: [(grad_out, 0, t), (sib_near, 0, t)],
+        1: [(dy_x, 0, t), (sib_near, 2 * t, t)],
+        2: [(dy_z1, 0, t), (sib_near, t, t)],
+        3: [(dy_xz, 0, t), (sib_far, t, t)],
+        4: [(dy_z2, 0, t), (sib_near, 3 * t, t)],
+        5: [(dy_xz, t, t), (sib_far, 2 * t, t)],
+        6: [(dy_z3, 0, t), (sib_far, 0, t)],
+        7: [(dy_xz3, 0, t), (sib_last, 0, t)],
+    }
+    summed = product("product", range(chips), slots, where, None, jnp.bfloat16)
     return (summed[None], factors.reshape(examples))
 
 
@@ -222,8 +267,7 @@
         tokens = grad_out.shape[0]
         dense = (
             mesh.shape["dp"] == 1
-            and devices >= 4
-            and devices & (devices - 1) == 0
+            and devices == 16
             and 2 * tokens * TOPK // devices >= tokens
         )
         run = per_device_dense if dense else per_device_sparse

time: 154 us -> 127 us (0.82)
  waiting for transfers between devices: 97.9 us -> 77.4 us
  between operations: 14.1 us -> 0.85 us
  starting transfers between devices: 8.12 us -> 21.1 us
  local copies, waits for them, and re-layouts: 7.33 us -> 2.66 us
    all_gather x1 -> x0, waiting for transfers between devices: 20.4 us -> none  [per_device_dense(): lax.all_gather(grad_out, 'expert', axis=0, tiled=True, axis_index_groups=...]
    ppermute x10 -> x18, starting transfers between devices: 8.08 us -> 21.1 us  [swap(): lax.ppermute(array, 'expert', [(i, i ^ offset) for i in range(devices)])]
    reshape x3 -> x0, local copies, waits for them, and re-layouts: 2.69 us -> none  [the longest x1 1.31 us: per_device_dense(): clip_bound.reshape(examples, 1)]
    unnamed x24 -> x50, local copies, waits for them, and re-layouts: 3.47 us -> 2.66 us
    ppermute x10 -> x18, waiting for transfers between devices: 76.8 us -> 77.4 us  [swap(): lax.ppermute(array, 'expert', [(i, i ^ offset) for i in range(devices)])]
  transfers between devices with their start and end apart: 11 -> 18, of which waited for: 9 -> 11; matrix products, arithmetic and copies ran while one was open for 4% -> 0% of each run, Pallas kernels for 7% -> 9%
where the time goes in v2:
time: 127 us; the launch traced here: 126 us
  waiting for transfers between devices  77.4 us (61%)
  Pallas kernels  23.9 us (19%)
  starting transfers between devices  21.1 us (17%)
  local copies, waits for them, and re-layouts  2.66 us (2%)
    ppermute x18, waiting for transfers between devices, swap(): lax.ppermute(array, 'expert', [(i, i ^ offset) for i in range(devices)])  77.4 us
    ppermute x18, starting transfers between devices, swap(): lax.ppermute(array, 'expert', [(i, i ^ offset) for i in range(devices)])  21.1 us
    pallas_call x1, Pallas kernels, product(): pl.pallas_call(functools.partial(product_kernel, places, len(arrays), tot...  12.4 us
    pallas_call x1, Pallas kernels, per_device_dense(): pl.pallas_call(functools.partial(norm_kernel, devices), out_shape=(jax.Sh...  6.86 us
    pallas_call x1, Pallas kernels, per_device_dense(): pl.pallas_call(functools.partial(build_kernel, chips), out_shape=[jax.Sha...  4.59 us
    unnamed x50, local copies, waits for them, and re-layouts  2.66 us
  transfers between devices with their start and end apart: 18, of which 11 were waited for; matrix products, arithmetic and copies ran while one was open for 0% of the time, Pallas kernels for 9%

profile of v2, /device:TPU:9, one launch (start us, length us, event | category | flops | bytes accessed | tf_op | source)
XLA Modules:
  0.0 126.2 jit_solution(3229202154852895485)
XLA Ops:
  0.6 0.7 collective-permute-start
  1.4 2.5 %collective-permute-start.2 = (bf16[128,2048]{1,0:T(8,128)(2,1)}, bf16[128,2048]{1,0:T(8,128)(2,1)S(1)}, u32[]{:S(2)}, u32[]{:S(2)}) collective-permute-start(bf16[128,2048]{1,0:T(8,128)(2,1)} %refs_0_.1), channel_id=1, source_target_pairs={{0,8},{1,9},{2,10},{3,11},{4,12},{5,13},{6,14},{7,15},{8,0},{9,1},... | collective-permute-start | bytes 1572872 | tf_op jit(solution)/shard_map/ppermute | solution.py:206
  3.9 1.2 collective-permute-start.4
  5.1 6.9 %norms.1 = (f32[8,256]{1,0:T(8,128)}, f32[1,4]{1,0:T(1,128)}) custom-call(bf16[128,2048]{1,0:T(8,128)(2,1)} %refs_0_.1, bf16[1024,768]{1,0:T(8,128)(2,1)} %bitcast.8, s32[8,128]{1,0:T(8,128)} %bitcast.10, s32[8,128]{1,0:T(8,128)} %bitcast.11, f32[1,4]{1,0:T(1,128)} %bitcast.12), custom_call_target="tpu_custom_call" | custom-call | tf_op jit(solution)/shard_map/norms/pallas_call | solution.py:214
  11.9 0.9 collective-permute-start.1
  12.8 1.0 collective-permute-done.1.sib_meta_ref
  13.9 0.6 copy-done.7
  14.5 0.5 copy-done.3
  15.0 4.6 %build.1 = (bf16[256,768]{1,0:T(8,128)(2,1)}, bf16[256,768]{1,0:T(8,128)(2,1)}, bf16[256,768]{1,0:T(8,128)(2,1)}, bf16[256,768]{1,0:T(8,128)(2,1)}, bf16[256,768...) custom-call(s32[1]{0:T(128)} %bitcast.place_ref, ...), custom_call_target="tpu_custom_call" | custom-call | tf_op jit(solution)/shard_map/build/pallas_call | solution.py:224
  19.9 4.4 %collective-permute-done.3.refs_3_ = bf16[128,2048]{1,0:T(8,128)(2,1)S(1)} collective-permute-done((bf16[128,2048]{1,0:T(8,128)(2,1)}, bf16[128,2048]{1,0:T(8,128)(2,1)S(1)}, u32[]{:S(2)}, u32[]{:S(2)}) %collective-permute-start.3) | collective-permute-done | bytes 524320 | tf_op jit(solution)/shard_map/ppermute | solution.py:206
  24.3 3.1 %collective-permute-done.2.refs_6_ = bf16[128,2048]{1,0:T(8,128)(2,1)S(1)} collective-permute-done((bf16[128,2048]{1,0:T(8,128)(2,1)}, bf16[128,2048]{1,0:T(8,128)(2,1)S(1)}, u32[]{:S(2)}, u32[]{:S(2)}) %collective-permute-start.2) | collective-permute-done | bytes 524320 | tf_op jit(solution)/shard_map/ppermute | solution.py:206
  27.7 0.7 copy-done.6
  28.4 1.8 %collective-permute-done.5.refs_11_ = bf16[256,768]{1,0:T(8,128)(2,1)S(1)} collective-permute-done((bf16[256,768]{1,0:T(8,128)(2,1)}, bf16[256,768]{1,0:T(8,128)(2,1)S(1)}, u32[]{:S(2)}, u32[]{:S(2)}) %collective-permute-start.5) | collective-permute-done | bytes 393248 | tf_op jit(solution)/shard_map/ppermute | solution.py:206
  30.2 1.2 collective-permute-start.6
  31.6 1.3 %collective-permute-start.8 = (bf16[128,2048]{1,0:T(8,128)(2,1)S(1)}, bf16[128,2048]{1,0:T(8,128)(2,1)S(1)}, u32[]{:S(2)}, u32[]{:S(2)}) collective-permute-start(bf16[128,2048]{1,0:T(8,128)(2,1)S(1)} %collective-permute-done.2.refs_6_), channel_id=1, source_target_pairs={{0,4},{1,5},{2,6},{3,7},{4,0},{5,1},{6,2},{7,3},{8,12},{9,13},{10,... | collective-permute-start | bytes 1572872 | tf_op jit(solution)/shard_map/ppermute | solution.py:206
  33.0 1.3 %collective-permute-start.10 = (bf16[256,768]{1,0:T(8,128)(2,1)S(1)}, bf16[256,768]{1,0:T(8,128)(2,1)S(1)}, u32[]{:S(2)}, u32[]{:S(2)}) collective-permute-start(bf16[256,768]{1,0:T(8,128)(2,1)S(1)} %copy-done.20), channel_id=1, source_target_pairs={{0,12},{1,13},{2,14},{3,15},{4,8},{5,9},{6,10},{7,11},{8,4},{9,5},... | collective-permute-start | bytes 1179656 | tf_op jit(solution)/shard_map/ppermute | solution.py:206
  34.3 18.1 %collective-permute-done.8.refs_7_ = bf16[128,2048]{1,0:T(8,128)(2,1)S(1)} collective-permute-done((bf16[128,2048]{1,0:T(8,128)(2,1)S(1)}, bf16[128,2048]{1,0:T(8,128)(2,1)S(1)}, u32[]{:S(2)}, u32[]{:S(2)}) %collective-permute-start.8) | collective-permute-done | bytes 524320 | tf_op jit(solution)/shard_map/ppermute | solution.py:206
  52.4 3.2 %collective-permute-start.11 = (bf16[256,768]{1,0:T(8,128)(2,1)S(1)}, bf16[256,768]{1,0:T(8,128)(2,1)S(1)}, u32[]{:S(2)}, u32[]{:S(2)}) collective-permute-start(bf16[256,768]{1,0:T(8,128)(2,1)S(1)} %copy-done.19), channel_id=1, source_target_pairs={{0,6},{1,7},{2,4},{3,5},{4,2},{5,3},{6,0},{7,1},{8,14},{9,15},{10,... | collective-permute-start | bytes 1179656 | tf_op jit(solution)/shard_map/ppermute | solution.py:206
  55.6 0.5 collective-permute-done.7.refs_4_
  56.3 12.0 %collective-permute-done.10.refs_16_ = bf16[256,768]{1,0:T(8,128)(2,1)S(1)} collective-permute-done((bf16[256,768]{1,0:T(8,128)(2,1)S(1)}, bf16[256,768]{1,0:T(8,128)(2,1)S(1)}, u32[]{:S(2)}, u32[]{:S(2)}) %collective-permute-start.10) | collective-permute-done | bytes 393248 | tf_op jit(solution)/shard_map/ppermute | solution.py:206
  68.3 1.1 collective-permute-done.11.refs_13_
  69.4 3.0 %collective-permute-start.12 = (bf16[384,2048]{1,0:T(8,128)(2,1)S(1)}, bf16[384,2048]{1,0:T(8,128)(2,1)S(1)}, u32[]{:S(2)}, u32[]{:S(2)}) collective-permute-start(bf16[384,2048]{1,0:T(8,128)(2,1)S(1)} %pad_maximum_fusion.1), channel_id=1, source_target_pairs={{0,1},{1,0},{2,3},{3,2},{4,5},{5,4},{6,7},{7,6},{8,9},{9,8},{10,11... | collective-permute-start | bytes 4718600 | tf_op jit(solution)/shard_map/ppermute | solution.py:206
  72.3 0.3 collective-permute-start.13
  72.6 3.0 %collective-permute-start.14 = (bf16[256,768]{1,0:T(8,128)(2,1)S(1)}, bf16[256,768]{1,0:T(8,128)(2,1)S(1)}, u32[]{:S(2)}, u32[]{:S(2)}) collective-permute-start(bf16[256,768]{1,0:T(8,128)(2,1)S(1)} %copy-done.15), channel_id=1, source_target_pairs={{0,10},{1,11},{2,8},{3,9},{4,14},{5,15},{6,12},{7,13},{8,2},{9,3},... | collective-permute-start | bytes 1179656 | tf_op jit(solution)/shard_map/ppermute | solution.py:206
  75.6 0.3 collective-permute-start.15
  75.9 1.2 collective-permute-start.16
  77.1 23.4 %collective-permute-done.14.refs_15_ = bf16[256,768]{1,0:T(8,128)(2,1)S(1)} collective-permute-done((bf16[256,768]{1,0:T(8,128)(2,1)S(1)}, bf16[256,768]{1,0:T(8,128)(2,1)S(1)}, u32[]{:S(2)}, u32[]{:S(2)}) %collective-permute-start.14) | collective-permute-done | bytes 393248 | tf_op jit(solution)/shard_map/ppermute | solution.py:206
  100.4 10.4 %collective-permute-done.15.refs_17_ = bf16[256,768]{1,0:T(8,128)(2,1)S(1)} collective-permute-done((bf16[256,768]{1,0:T(8,128)(2,1)S(1)}, bf16[256,768]{1,0:T(8,128)(2,1)S(1)}, u32[]{:S(2)}, u32[]{:S(2)}) %collective-permute-start.15) | collective-permute-done | bytes 393248 | tf_op jit(solution)/shard_map/ppermute | solution.py:206
  110.8 0.5 collective-permute-start.17
  111.4 1.5 %collective-permute-done.17.refs_9_ = bf16[128,2048]{1,0:T(8,128)(2,1)S(1)} collective-permute-done((bf16[128,2048]{1,0:T(8,128)(2,1)S(1)}, bf16[128,2048]{1,0:T(8,128)(2,1)S(1)}, u32[]{:S(2)}, u32[]{:S(2)}) %collective-permute-start.17) | collective-permute-done | bytes 524320 | tf_op jit(solution)/shard_map/ppermute | solution.py:206
  113.0 0.8 copy-done.11
  113.8 12.4 %product.1 = bf16[2048,768]{1,0:T(8,128)(2,1)} custom-call(bf16[128,2048]{1,0:T(8,128)(2,1)} %refs_0_.1, bf16[512,2048]{1,0:T(8,128)(2,1)} %copy-done.8, bf16[128,2048]{1,0:T(8,128)(2,1)} %copy-done.6, bf16[128,2048]{1,0:T(8,128)(2,1)} %copy-done.1, bf16[256,2048]{1,0:T(8,128)(2,1)} %copy-done.4, bf16[384,2048]{1,0:T(8,128)(2,1)} %copy-done.9, ...), custom_call_target="tpu_custom_call" | custom-call | flops 6442450944 | bytes 17825792 | tf_op jit(solution)/shard_map/product/pallas_call | solution.py:179
  (60 shorter events, 1.0 us)
Async XLA Ops:
  0.6 13.3 %collective-permute-start = (bf16[1024,768]{1,0:T(8,128)(2,1)}, bf16[1024,768]{1,0:T(8,128)(2,1)S(1)}, u32[]{:S(2)}, u32[]{:S(2)}) collective-permute-start(bf16[1024,768]{1,0:T(8,128)(2,1)} %bitcast.7), channel_id=1, source_target_pairs={{0,1},{1,0},{2,3},{3,2},{4,5},{5,4},{6,7},{7,6},{8,9},{9,8},{10,11... | collective-permute-start | bytes 4718600 | tf_op jit(solution)/shard_map/ppermute | solution.py:206
  1.4 22.9 %collective-permute-start.3 = (bf16[128,2048]{1,0:T(8,128)(2,1)}, bf16[128,2048]{1,0:T(8,128)(2,1)S(1)}, u32[]{:S(2)}, u32[]{:S(2)}) collective-permute-start(bf16[128,2048]{1,0:T(8,128)(2,1)} %refs_0_.1), channel_id=1, source_target_pairs={{0,4},{1,5},{2,6},{3,7},{4,0},{5,1},{6,2},{7,3},{8,12},{9,13},{10,... | collective-permute-start | bytes 1572872 | tf_op jit(solution)/shard_map/ppermute | solution.py:206
  1.4 26.0 %collective-permute-start.2 = (bf16[128,2048]{1,0:T(8,128)(2,1)}, bf16[128,2048]{1,0:T(8,128)(2,1)S(1)}, u32[]{:S(2)}, u32[]{:S(2)}) collective-permute-start(bf16[128,2048]{1,0:T(8,128)(2,1)} %refs_0_.1), channel_id=1, source_target_pairs={{0,8},{1,9},{2,10},{3,11},{4,12},{5,13},{6,14},{7,15},{8,0},{9,1},... | collective-permute-start | bytes 1572872 | tf_op jit(solution)/shard_map/ppermute | solution.py:206
  3.9 23.6 %collective-permute-start.4 = (bf16[128,2048]{1,0:T(8,128)(2,1)}, bf16[128,2048]{1,0:T(8,128)(2,1)S(1)}, u32[]{:S(2)}, u32[]{:S(2)}) collective-permute-start(bf16[128,2048]{1,0:T(8,128)(2,1)} %refs_0_.1), channel_id=1, source_target_pairs={{0,2},{1,3},{2,0},{3,1},{4,6},{5,7},{6,4},{7,5},{8,10},{9,11},{10,... | collective-permute-start | bytes 1572872 | tf_op jit(solution)/shard_map/ppermute | solution.py:206
  11.9 1.9 %collective-permute-start.1 = (f32[8,256]{1,0:T(8,128)}, f32[8,256]{1,0:T(8,128)S(1)}, u32[]{:S(2)}, u32[]{:S(2)}) collective-permute-start(f32[8,256]{1,0:T(8,128)} %get-tuple-element.24.own_meta_ref), channel_id=1, source_target_pairs={{0,1},{1,0},{2,3},{3,2},{4,5},{5,4},{6,7},{7,6},{8,9},{9,8},{10,11... | collective-permute-start | bytes 24584 | tf_op jit(solution)/shard_map/ppermute | solution.py:206
  15.0 12.5 %copy-start = (bf16[128,2048]{1,0:T(8,128)(2,1)S(1)}, bf16[128,2048]{1,0:T(8,128)(2,1)}, u32[]{:S(2)}) copy-start(bf16[128,2048]{1,0:T(8,128)(2,1)} %refs_0_.1) | copy-start | bytes 1572868
  19.6 10.6 %collective-permute-start.5 = (bf16[256,768]{1,0:T(8,128)(2,1)}, bf16[256,768]{1,0:T(8,128)(2,1)S(1)}, u32[]{:S(2)}, u32[]{:S(2)}) collective-permute-start(bf16[256,768]{1,0:T(8,128)(2,1)} %get-tuple-element.28), channel_id=1, source_target_pairs={{0,2},{1,3},{2,0},{3,1},{4,6},{5,7},{6,4},{7,5},{8,10},{9,11},{10,... | collective-permute-start | bytes 1179656 | tf_op jit(solution)/shard_map/ppermute | solution.py:206
  27.5 5.5 %copy-start.20 = (bf16[256,768]{1,0:T(8,128)(2,1)S(1)}, bf16[256,768]{1,0:T(8,128)(2,1)}, u32[]{:S(2)}) copy-start(bf16[256,768]{1,0:T(8,128)(2,1)} %get-tuple-element.36) | copy-start | bytes 1179652
  27.5 24.9 %copy-start.19 = (bf16[256,768]{1,0:T(8,128)(2,1)S(1)}, bf16[256,768]{1,0:T(8,128)(2,1)}, u32[]{:S(2)}) copy-start(bf16[256,768]{1,0:T(8,128)(2,1)} %get-tuple-element.37) | copy-start | bytes 1179652
  28.3 44.2 %copy-start.15 = (bf16[256,768]{1,0:T(8,128)(2,1)S(1)}, bf16[256,768]{1,0:T(8,128)(2,1)}, u32[]{:S(2)}) copy-start(bf16[256,768]{1,0:T(8,128)(2,1)} %get-tuple-element.40) | copy-start | bytes 1179652
  28.4 47.3 %copy-start.14 = (bf16[256,768]{1,0:T(8,128)(2,1)S(1)}, bf16[256,768]{1,0:T(8,128)(2,1)}, u32[]{:S(2)}) copy-start(bf16[256,768]{1,0:T(8,128)(2,1)} %get-tuple-element.41) | copy-start | bytes 1179652
  28.4 47.5 %copy-start.13 = (bf16[256,768]{1,0:T(8,128)(2,1)S(1)}, bf16[256,768]{1,0:T(8,128)(2,1)}, u32[]{:S(2)}) copy-start(bf16[256,768]{1,0:T(8,128)(2,1)} %get-tuple-element.42) | copy-start | bytes 1179652
  30.2 82.7 %copy-start.12 = (bf16[256,768]{1,0:T(8,128)(2,1)}, bf16[256,768]{1,0:T(8,128)(2,1)S(1)}, u32[]{:S(2)}) copy-start(bf16[256,768]{1,0:T(8,128)(2,1)S(1)} %collective-permute-done.5.refs_11_) | copy-start | bytes 1179652
  30.2 39.2 %collective-permute-start.6 = (bf16[512,2048]{1,0:T(8,128)(2,1)S(1)}, bf16[512,2048]{1,0:T(8,128)(2,1)S(1)}, u32[]{:S(2)}, u32[]{:S(2)}) collective-permute-start(bf16[512,2048]{1,0:T(8,128)(2,1)S(1)} %pad_maximum_fusion), channel_id=1, source_target_pairs={{0,1},{1,0},{2,3},{3,2},{4,5},{5,4},{6,7},{7,6},{8,9},{9,8},{10,11... | collective-permute-start | bytes 6291464 | tf_op jit(solution)/shard_map/ppermute | solution.py:206
  31.4 24.8 %collective-permute-start.7 = (bf16[256,2048]{1,0:T(8,128)(2,1)S(1)}, bf16[256,2048]{1,0:T(8,128)(2,1)S(1)}, u32[]{:S(2)}, u32[]{:S(2)}) collective-permute-start(bf16[256,2048]{1,0:T(8,128)(2,1)S(1)} %pad_maximum_fusion.2), channel_id=1, source_target_pairs={{0,2},{1,3},{2,0},{3,1},{4,6},{5,7},{6,4},{7,5},{8,10},{9,11},{10,... | collective-permute-start | bytes 3145736 | tf_op jit(solution)/shard_map/ppermute | solution.py:206
  31.6 20.8 %collective-permute-start.8 = (bf16[128,2048]{1,0:T(8,128)(2,1)S(1)}, bf16[128,2048]{1,0:T(8,128)(2,1)S(1)}, u32[]{:S(2)}, u32[]{:S(2)}) collective-permute-start(bf16[128,2048]{1,0:T(8,128)(2,1)S(1)} %collective-permute-done.2.refs_6_), channel_id=1, source_target_pairs={{0,4},{1,5},{2,6},{3,7},{4,0},{5,1},{6,2},{7,3},{8,12},{9,13},{10,... | collective-permute-start | bytes 1572872 | tf_op jit(solution)/shard_map/ppermute | solution.py:206
  32.9 23.3 %collective-permute-start.9 = (bf16[256,768]{1,0:T(8,128)(2,1)S(1)}, bf16[256,768]{1,0:T(8,128)(2,1)S(1)}, u32[]{:S(2)}, u32[]{:S(2)}) collective-permute-start(bf16[256,768]{1,0:T(8,128)(2,1)S(1)} %copy-done.21), channel_id=1, source_target_pairs={{0,8},{1,9},{2,10},{3,11},{4,12},{5,13},{6,14},{7,15},{8,0},{9,1},... | collective-permute-start | bytes 1179656 | tf_op jit(solution)/shard_map/ppermute | solution.py:206
  33.0 35.3 %collective-permute-start.10 = (bf16[256,768]{1,0:T(8,128)(2,1)S(1)}, bf16[256,768]{1,0:T(8,128)(2,1)S(1)}, u32[]{:S(2)}, u32[]{:S(2)}) collective-permute-start(bf16[256,768]{1,0:T(8,128)(2,1)S(1)} %copy-done.20), channel_id=1, source_target_pairs={{0,12},{1,13},{2,14},{3,15},{4,8},{5,9},{6,10},{7,11},{8,4},{9,5},... | collective-permute-start | bytes 1179656 | tf_op jit(solution)/shard_map/ppermute | solution.py:206
  52.4 60.5 %copy-start.5 = (bf16[128,2048]{1,0:T(8,128)(2,1)}, bf16[128,2048]{1,0:T(8,128)(2,1)S(1)}, u32[]{:S(2)}) copy-start(bf16[128,2048]{1,0:T(8,128)(2,1)S(1)} %collective-permute-done.8.refs_7_) | copy-start | bytes 1572868
  52.4 17.0 %collective-permute-start.11 = (bf16[256,768]{1,0:T(8,128)(2,1)S(1)}, bf16[256,768]{1,0:T(8,128)(2,1)S(1)}, u32[]{:S(2)}, u32[]{:S(2)}) collective-permute-start(bf16[256,768]{1,0:T(8,128)(2,1)S(1)} %copy-done.19), channel_id=1, source_target_pairs={{0,6},{1,7},{2,4},{3,5},{4,2},{5,3},{6,0},{7,1},{8,14},{9,15},{10,... | collective-permute-start | bytes 1179656 | tf_op jit(solution)/shard_map/ppermute | solution.py:206
  56.2 56.8 %copy-start.4 = (bf16[256,2048]{1,0:T(8,128)(2,1)}, bf16[256,2048]{1,0:T(8,128)(2,1)S(1)}, u32[]{:S(2)}) copy-start(bf16[256,2048]{1,0:T(8,128)(2,1)S(1)} %collective-permute-done.7.refs_4_) | copy-start | bytes 3145732
  56.3 56.7 %copy-start.16 = (bf16[256,768]{1,0:T(8,128)(2,1)}, bf16[256,768]{1,0:T(8,128)(2,1)S(1)}, u32[]{:S(2)}) copy-start(bf16[256,768]{1,0:T(8,128)(2,1)S(1)} %collective-permute-done.9.refs_14_) | copy-start | bytes 1179652
  68.3 44.7 %copy-start.17 = (bf16[256,768]{1,0:T(8,128)(2,1)}, bf16[256,768]{1,0:T(8,128)(2,1)S(1)}, u32[]{:S(2)}) copy-start(bf16[256,768]{1,0:T(8,128)(2,1)S(1)} %collective-permute-done.10.refs_16_) | copy-start | bytes 1179652
  69.4 43.6 %copy-start.18 = (bf16[256,768]{1,0:T(8,128)(2,1)}, bf16[256,768]{1,0:T(8,128)(2,1)S(1)}, u32[]{:S(2)}) copy-start(bf16[256,768]{1,0:T(8,128)(2,1)S(1)} %collective-permute-done.11.refs_13_) | copy-start | bytes 1179652
  69.4 43.6 %copy-start.8 = (bf16[512,2048]{1,0:T(8,128)(2,1)}, bf16[512,2048]{1,0:T(8,128)(2,1)S(1)}, u32[]{:S(2)}) copy-start(bf16[512,2048]{1,0:T(8,128)(2,1)S(1)} %collective-permute-done.6.refs_1_) | copy-start | bytes 6291460
  69.4 41.5 %collective-permute-start.12 = (bf16[384,2048]{1,0:T(8,128)(2,1)S(1)}, bf16[384,2048]{1,0:T(8,128)(2,1)S(1)}, u32[]{:S(2)}, u32[]{:S(2)}) collective-permute-start(bf16[384,2048]{1,0:T(8,128)(2,1)S(1)} %pad_maximum_fusion.1), channel_id=1, source_target_pairs={{0,1},{1,0},{2,3},{3,2},{4,5},{5,4},{6,7},{7,6},{8,9},{9,8},{10,11... | collective-permute-start | bytes 4718600 | tf_op jit(solution)/shard_map/ppermute | solution.py:206
  72.3 38.5 %collective-permute-start.13 = (bf16[128,2048]{1,0:T(8,128)(2,1)S(1)}, bf16[128,2048]{1,0:T(8,128)(2,1)S(1)}, u32[]{:S(2)}, u32[]{:S(2)}) collective-permute-start(bf16[128,2048]{1,0:T(8,128)(2,1)S(1)} %collective-permute-done.8.refs_7_), channel_id=1, source_target_pairs={{0,2},{1,3},{2,0},{3,1},{4,6},{5,7},{6,4},{7,5},{8,10},{9,11},{10,... | collective-permute-start | bytes 1572872 | tf_op jit(solution)/shard_map/ppermute | solution.py:206
  72.6 27.8 %collective-permute-start.14 = (bf16[256,768]{1,0:T(8,128)(2,1)S(1)}, bf16[256,768]{1,0:T(8,128)(2,1)S(1)}, u32[]{:S(2)}, u32[]{:S(2)}) collective-permute-start(bf16[256,768]{1,0:T(8,128)(2,1)S(1)} %copy-done.15), channel_id=1, source_target_pairs={{0,10},{1,11},{2,8},{3,9},{4,14},{5,15},{6,12},{7,13},{8,2},{9,3},... | collective-permute-start | bytes 1179656 | tf_op jit(solution)/shard_map/ppermute | solution.py:206
  75.6 35.2 %collective-permute-start.15 = (bf16[256,768]{1,0:T(8,128)(2,1)S(1)}, bf16[256,768]{1,0:T(8,128)(2,1)S(1)}, u32[]{:S(2)}, u32[]{:S(2)}) collective-permute-start(bf16[256,768]{1,0:T(8,128)(2,1)S(1)} %copy-done.14), channel_id=1, source_target_pairs={{0,14},{1,15},{2,12},{3,13},{4,10},{5,11},{6,8},{7,9},{8,6},{9,7},... | collective-permute-start | bytes 1179656 | tf_op jit(solution)/shard_map/ppermute | solution.py:206
  75.9 34.9 %collective-permute-start.16 = (bf16[256,768]{1,0:T(8,128)(2,1)S(1)}, bf16[256,768]{1,0:T(8,128)(2,1)S(1)}, u32[]{:S(2)}, u32[]{:S(2)}) collective-permute-start(bf16[256,768]{1,0:T(8,128)(2,1)S(1)} %copy-done.13), channel_id=1, source_target_pairs={{0,4},{1,5},{2,6},{3,7},{4,0},{5,1},{6,2},{7,3},{8,12},{9,13},{10,... | collective-permute-start | bytes 1179656 | tf_op jit(solution)/shard_map/ppermute | solution.py:206
  100.4 10.4 %copy-start.22 = (bf16[256,768]{1,0:T(8,128)(2,1)}, bf16[256,768]{1,0:T(8,128)(2,1)S(1)}, u32[]{:S(2)}) copy-start(bf16[256,768]{1,0:T(8,128)(2,1)S(1)} %collective-permute-done.14.refs_15_) | copy-start | bytes 1179652
  110.8 2.1 %collective-permute-start.17 = (bf16[128,2048]{1,0:T(8,128)(2,1)S(1)}, bf16[128,2048]{1,0:T(8,128)(2,1)S(1)}, u32[]{:S(2)}, u32[]{:S(2)}) collective-permute-start(bf16[128,2048]{1,0:T(8,128)(2,1)S(1)} %collective-permute-done.13.refs_8_), channel_id=1, source_target_pairs={{0,1},{1,0},{2,3},{3,2},{4,5},{5,4},{6,7},{7,6},{8,9},{9,8},{10,11... | collective-permute-start | bytes 1572872 | tf_op jit(solution)/shard_map/ppermute | solution.py:206
  (11 other events, 25.2 us)

commit v3 on v2

--- a/solution.py
+++ b/solution.py
@@ -9,7 +9,9 @@
 
 TOPK = 8
 EXLEN = 32
-VMEM_LIMIT = 56 * 1024 * 1024
+VMEM_LIMIT = 16 * 1024 * 1024
+PRODUCT_LIMIT = 32 * 1024 * 1024
+LATE_BLOCK = 1024
 HIGHEST = lax.Precision.HIGHEST
 
 
@@ -146,19 +148,48 @@
                 out_refs[j][start : start + EXLEN, :] = message[j * EXLEN : (j + 1) * EXLEN, :]
 
 
-def product_kernel(places, count, has_total, *refs):
-    dy_refs, hid_refs, out_ref = refs[:count], refs[count : count + len(places)], refs[-1]
-    total = refs[-2][...] if has_total else None
-    for hid_ref, sides in zip(hid_refs, places):
-        dy = jnp.concatenate([dy_refs[k][begin : begin + rows, :] for k, begin, rows in sides], axis=0)
-        term = lax.dot_general(
-            dy, hid_ref[...], (((0,), (0,)), ((), ())), preferred_element_type=jnp.float32
-        )
-        total = term if total is None else total + term
-    out_ref[...] = total.astype(out_ref.dtype)
-
-
-def product(name, offsets, slots, where, total, dtype):
+def product_kernel(places, block, has_total, *refs):
+    m = len(places)
+    n = len(refs) - m - 3 - has_total
+    dy_refs, hid_refs, (out_ref, out_tiles, out_sems) = refs[:n], refs[n : n + m], refs[n + m + has_total :]
+    chunks = out_ref.shape[0] // block
+
+    def out_copy(c):
+        return pltpu.make_async_copy(
+            out_tiles.at[c % 2], out_ref.at[pl.ds(c * block, block), :], out_sems.at[c % 2]
+        )
+
+    for c in range(chunks):
+        if c >= 2:
+            out_copy(c - 2).wait()
+        columns = slice(c * block, (c + 1) * block)
+        dy = jnp.concatenate(
+            [dy_refs[k][begin : begin + rows, columns] for sides in places for k, begin, rows in sides], axis=0
+        )
+        hid = jnp.concatenate([hid_ref[...] for hid_ref in hid_refs], axis=0)
+        value = lax.dot_general(dy, hid, (((0,), (0,)), ((), ())), preferred_element_type=jnp.float32)
+        if has_total:
+            value = value + refs[n + m][columns, :]
+        out_tiles[c % 2] = value.astype(out_tiles.dtype)
+        out_copy(c).start()
+    for c in range(max(chunks - 2, 0), chunks):
+        out_copy(c).wait()
+
+
+def early_kernel(places, block, *refs):
+    m = len(places)
+    n = len(refs) - m - 1
+    dy_refs, hid_refs, out_ref = refs[:n], refs[n : n + m], refs[n + m]
+    for c in range(out_ref.shape[0] // block):
+        columns = slice(c * block, (c + 1) * block)
+        dy = jnp.concatenate(
+            [dy_refs[k][begin : begin + rows, columns] for sides in places for k, begin, rows in sides], axis=0
+        )
+        hid = jnp.concatenate([hid_ref[...] for hid_ref in hid_refs], axis=0)
+        out_ref[columns, :] = lax.dot_general(dy, hid, (((0,), (0,)), ((), ())), preferred_element_type=jnp.float32)
+
+
+def product(offsets, slots, where, early, total=None):
     arrays, places = [], []
     for j in offsets:
         sides = []
@@ -169,26 +200,29 @@
             sides.append((known[0] if known else len(arrays) - 1, begin, rows))
         places.append(sides)
     width, hidden = arrays[0].shape[1], slots[0].shape[1]
-    block = min(width, 256)
-    operands = arrays + [slots[j] for j in offsets]
-    specs = [pl.BlockSpec((array.shape[0], block), lambda i: (0, i)) for array in arrays]
-    specs += [pl.BlockSpec(slots[j].shape, lambda i: (0, 0)) for j in offsets]
-    if total is not None:
-        operands.append(total)
-        specs.append(pl.BlockSpec((block, hidden), lambda i: (i, 0)))
+    operands = arrays + [slots[j] for j in offsets] + ([] if total is None else [total])
+    if early:
+        block = min(width, 512)
+        kernel = functools.partial(early_kernel, places, block)
+        out_space, scratch = pltpu.VMEM, ()
+    else:
+        block = min(width, LATE_BLOCK)
+        kernel = functools.partial(product_kernel, places, block, int(total is not None))
+        out_space = pl.ANY
+        scratch = (pltpu.VMEM((2, block, hidden), jnp.bfloat16), pltpu.SemaphoreType.DMA((2,)))
     return pl.pallas_call(
-        functools.partial(product_kernel, places, len(arrays), total is not None),
-        out_shape=jax.ShapeDtypeStruct((width, hidden), dtype),
-        grid=(width // block,),
-        in_specs=specs,
-        out_specs=pl.BlockSpec((block, hidden), lambda i: (i, 0)),
-        compiler_params=pltpu.CompilerParams(vmem_limit_bytes=VMEM_LIMIT),
+        kernel,
+        out_shape=jax.ShapeDtypeStruct((width, hidden), jnp.float32 if early else jnp.bfloat16),
+        in_specs=[pl.BlockSpec(memory_space=pltpu.VMEM)] * len(operands),
+        out_specs=pl.BlockSpec(memory_space=out_space),
+        scratch_shapes=scratch,
+        compiler_params=pltpu.CompilerParams(vmem_limit_bytes=PRODUCT_LIMIT),
         cost_estimate=pl.CostEstimate(
             flops=2 * width * hidden * sum(slots[j].shape[0] for j in offsets),
-            bytes_accessed=sum(a.size * a.dtype.itemsize for a in operands) + width * hidden * 4,
+            bytes_accessed=2 * width * hidden,
             transcendentals=0,
         ),
-        name=name,
+        name="early_product" if early else "product",
     )(*operands)
 
 
@@ -240,13 +274,9 @@
     second = (slots[4], slots[6], slots[3], dy_z3, dy_xz, sib_near)
 
     far = jnp.concatenate([dy_z3, dy_xz])
+    t = tokens
     slot5, slot7, slot2, dy_z3b, far = after((slots[5], slots[7], slots[2], dy_z3, far), second)
-    slots[5], slots[7], slots[2] = swap(slot5, 10), swap(slot7, 14), swap(slot2, 4)
     dy_xz3, sib_far = swap(dy_z3b, 2), swap(far, 1)
-    third = (slots[5], slots[7], slots[2], dy_xz3, sib_far)
-    sib_last = swap(after((dy_xz3,), third)[0], 1)
-
-    t = tokens
     where = {
         0: [(grad_out, 0, t), (sib_near, 0, t)],
         1: [(dy_x, 0, t), (sib_near, 2 * t, t)],
@@ -255,9 +285,14 @@
         4: [(dy_z2, 0, t), (sib_near, 3 * t, t)],
         5: [(dy_xz, t, t), (sib_far, 2 * t, t)],
         6: [(dy_z3, 0, t), (sib_far, 0, t)],
-        7: [(dy_xz3, 0, t), (sib_last, 0, t)],
     }
-    summed = product("product", range(chips), slots, where, None, jnp.bfloat16)
+    slots[5], slots[7], slots[2] = swap(slot5, 10), swap(slot7, 14), swap(slot2, 4)
+    third = (slots[5], slots[7], slots[2], dy_xz3, sib_far)
+    total = product((0, 1, 4, 3, 6), slots, where, True)
+    sib_last = swap(after((dy_xz3,), third + (total,))[0], 1)
+    where[7] = [(dy_xz3, 0, t), (sib_last, 0, t)]
+    rest = [j for j in (3, 6, 5, 2, 7) if j not in (0, 1, 4, 3, 6)]
+    summed = product(rest, slots, where, False, total)
     return (summed[None], factors.reshape(examples))
 
 

time: 127 us -> 116 us (0.913)
  Pallas kernels: 23.9 us -> 15.9 us
  waiting for transfers between devices: 77.4 us -> 73.3 us
  local copies, waits for them, and re-layouts: 2.66 us -> 4.48 us
    pallas_call x1 -> x2, Pallas kernels: 12.4 us -> 8.11 us  [product(): pl.pallas_call(kernel, out_shape=jax.ShapeDtypeStruct((width, hidden), jn...]
    ppermute x18, waiting for transfers between devices: 77.4 us -> 73.3 us  [swap(): lax.ppermute(array, 'expert', [(i, i ^ offset) for i in range(devices)])]
    pallas_call x1, Pallas kernels: 4.59 us -> 2.5 us  [per_device_dense(): pl.pallas_call(functools.partial(build_kernel, chips), out_shape=[jax.Sha...]
    unnamed x50 -> x14, local copies, waits for them, and re-layouts: 2.66 us -> 4.48 us
    pallas_call x1, Pallas kernels: 6.86 us -> 5.26 us  [per_device_dense(): pl.pallas_call(functools.partial(norm_kernel, devices), out_shape=(jax.Sh...]
  transfers between devices with their start and end apart: 18 -> 18, of which waited for: 11 -> 11; matrix products, arithmetic and copies ran while one was open for 0% -> 0% of each run, Pallas kernels for 9% -> 10%
where the time goes in v3:
time: 116 us
  waiting for transfers between devices  73.3 us (63%)
  starting transfers between devices  21.1 us (18%)
  Pallas kernels  15.9 us (14%)
  local copies, waits for them, and re-layouts  4.48 us (4%)
    ppermute x18, waiting for transfers between devices, swap(): lax.ppermute(array, 'expert', [(i, i ^ offset) for i in range(devices)])  73.3 us
    ppermute x18, starting transfers between devices, swap(): lax.ppermute(array, 'expert', [(i, i ^ offset) for i in range(devices)])  21.1 us
    pallas_call x2, Pallas kernels, product(): pl.pallas_call(kernel, out_shape=jax.ShapeDtypeStruct((width, hidden), jn...  8.11 us
    pallas_call x1, Pallas kernels, per_device_dense(): pl.pallas_call(functools.partial(norm_kernel, devices), out_shape=(jax.Sh...  5.26 us
    unnamed x14, local copies, waits for them, and re-layouts  4.48 us
    pallas_call x1, Pallas kernels, per_device_dense(): pl.pallas_call(functools.partial(build_kernel, chips), out_shape=[jax.Sha...  2.5 us
  transfers between devices with their start and end apart: 18, of which 11 were waited for; matrix products, arithmetic and copies ran while one was open for 0% of the time, Pallas kernels for 10%

profile of v3, /device:TPU:9, one launch (start us, length us, event | category | flops | bytes accessed | tf_op | source)
XLA Modules:
  0.0 115.9 jit_solution(14397798112560188000)
XLA Ops:
  0.6 0.7 collective-permute-start
  1.4 2.5 %collective-permute-start.2 = (bf16[128,2048]{1,0:T(8,128)(2,1)}, bf16[128,2048]{1,0:T(8,128)(2,1)S(1)}, u32[]{:S(2)}, u32[]{:S(2)}) collective-permute-start(bf16[128,2048]{1,0:T(8,128)(2,1)} %refs_0_.1), channel_id=1, source_target_pairs={{0,8},{1,9},{2,10},{3,11},{4,12},{5,13},{6,14},{7,15},{8,0},{9,1},... | collective-permute-start | bytes 1572872 | tf_op jit(solution)/shard_map/ppermute | solution.py:240
  3.9 1.2 %collective-permute-start.4 = (bf16[128,2048]{1,0:T(8,128)(2,1)}, bf16[128,2048]{1,0:T(8,128)(2,1)S(1)}, u32[]{:S(2)}, u32[]{:S(2)}) collective-permute-start(bf16[128,2048]{1,0:T(8,128)(2,1)} %refs_0_.1), channel_id=1, source_target_pairs={{0,2},{1,3},{2,0},{3,1},{4,6},{5,7},{6,4},{7,5},{8,10},{9,11},{10,... | collective-permute-start | bytes 1572872 | tf_op jit(solution)/shard_map/ppermute | solution.py:240
  5.1 1.4 %copy-done = bf16[128,8,768]{2,1,0:T(8,128)(2,1)S(1)} copy-done((bf16[128,8,768]{2,1,0:T(8,128)(2,1)S(1)}, bf16[128,8,768]{2,1,0:T(8,128)(2,1)}, u32[]{:S(2)}) %copy-start) | copy-done | bytes 1572888
  6.5 1.0 copy-done.2
  7.5 0.7 copy-done.4
  8.2 0.7 copy-done.5
  8.9 0.7 copy-done.6
  9.6 5.3 %norms.1 = (f32[8,256]{1,0:T(8,128)S(1)}, f32[1,4]{1,0:T(1,128)}) custom-call(bf16[128,2048]{1,0:T(8,128)(2,1)S(1)} %copy-done.2, bf16[1024,768]{1,0:T(8,128)(2,1)S(1)} %bitcast.8, s32[8,128]{1,0:T(8,128)S(1)} %bitcast.10, s32[8,128]{1,0:T(8,128)S(1)} %bitcast.11, f32[1,4]{1,0:T(1,128)S(1)} %bitcast.12), custom_call_target="tpu_custom_call" | custom-call | tf_op jit(solution)/shard_map/norms/pallas_call | solution.py:248
  14.8 0.9 collective-permute-start.1
  15.7 0.8 collective-permute-done.1.sib_meta_ref
  16.6 2.5 %build.1 = (bf16[256,768]{1,0:T(8,128)(2,1)S(1)}, bf16[256,768]{1,0:T(8,128)(2,1)S(1)}, bf16[256,768]{1,0:T(8,128)(2,1)S(1)}, bf16[256,768]{1,0:T(8,128)(2,1)S(1...) custom-call(s32[1]{0:T(128)} %bitcast.place_ref, ...), custom_call_target="tpu_custom_call" | custom-call | tf_op jit(solution)/shard_map/build/pallas_call | solution.py:258
  19.4 4.9 %collective-permute-done.3.refs_2_ = bf16[128,2048]{1,0:T(8,128)(2,1)S(1)} collective-permute-done((bf16[128,2048]{1,0:T(8,128)(2,1)}, bf16[128,2048]{1,0:T(8,128)(2,1)S(1)}, u32[]{:S(2)}, u32[]{:S(2)}) %collective-permute-start.3) | collective-permute-done | bytes 524320 | tf_op jit(solution)/shard_map/ppermute | solution.py:240
  24.3 3.1 %collective-permute-done.2.refs_3_ = bf16[128,2048]{1,0:T(8,128)(2,1)S(1)} collective-permute-done((bf16[128,2048]{1,0:T(8,128)(2,1)}, bf16[128,2048]{1,0:T(8,128)(2,1)S(1)}, u32[]{:S(2)}, u32[]{:S(2)}) %collective-permute-start.2) | collective-permute-done | bytes 524320 | tf_op jit(solution)/shard_map/ppermute | solution.py:240
  27.6 1.9 %collective-permute-done.5.refs_8_ = bf16[256,768]{1,0:T(8,128)(2,1)S(1)} collective-permute-done((bf16[256,768]{1,0:T(8,128)(2,1)S(1)}, bf16[256,768]{1,0:T(8,128)(2,1)S(1)}, u32[]{:S(2)}, u32[]{:S(2)}) %collective-permute-start.5) | collective-permute-done | bytes 393248 | tf_op jit(solution)/shard_map/ppermute | solution.py:240
  29.5 1.2 %collective-permute-start.11 = (bf16[512,2048]{1,0:T(8,128)(2,1)S(1)}, bf16[512,2048]{1,0:T(8,128)(2,1)S(1)}, u32[]{:S(2)}, u32[]{:S(2)}) collective-permute-start(bf16[512,2048]{1,0:T(8,128)(2,1)S(1)} %pad_maximum_fusion), channel_id=1, source_target_pairs={{0,1},{1,0},{2,3},{3,2},{4,5},{5,4},{6,7},{7,6},{8,9},{9,8},{10,11... | collective-permute-start | bytes 6291464 | tf_op jit(solution)/shard_map/ppermute | solution.py:240
  30.9 1.3 %collective-permute-start.7 = (bf16[128,2048]{1,0:T(8,128)(2,1)S(1)}, bf16[128,2048]{1,0:T(8,128)(2,1)S(1)}, u32[]{:S(2)}, u32[]{:S(2)}) collective-permute-start(bf16[128,2048]{1,0:T(8,128)(2,1)S(1)} %collective-permute-done.2.refs_3_), channel_id=1, source_target_pairs={{0,4},{1,5},{2,6},{3,7},{4,0},{5,1},{6,2},{7,3},{8,12},{9,13},{10,... | collective-permute-start | bytes 1572872 | tf_op jit(solution)/shard_map/ppermute | solution.py:240
  32.3 1.3 %collective-permute-start.9 = (bf16[256,768]{1,0:T(8,128)(2,1)S(1)}, bf16[256,768]{1,0:T(8,128)(2,1)S(1)}, u32[]{:S(2)}, u32[]{:S(2)}) collective-permute-start(bf16[256,768]{1,0:T(8,128)(2,1)S(1)} %get-tuple-element.35), channel_id=1, source_target_pairs={{0,12},{1,13},{2,14},{3,15},{4,8},{5,9},{6,10},{7,11},{8,4},{9,5},... | collective-permute-start | bytes 1179656 | tf_op jit(solution)/shard_map/ppermute | solution.py:240
  33.6 18.1 %collective-permute-done.7.refs_6_ = bf16[128,2048]{1,0:T(8,128)(2,1)S(1)} collective-permute-done((bf16[128,2048]{1,0:T(8,128)(2,1)S(1)}, bf16[128,2048]{1,0:T(8,128)(2,1)S(1)}, u32[]{:S(2)}, u32[]{:S(2)}) %collective-permute-start.7) | collective-permute-done | bytes 524320 | tf_op jit(solution)/shard_map/ppermute | solution.py:240
  51.7 3.2 %collective-permute-start.10 = (bf16[256,768]{1,0:T(8,128)(2,1)S(1)}, bf16[256,768]{1,0:T(8,128)(2,1)S(1)}, u32[]{:S(2)}, u32[]{:S(2)}) collective-permute-start(bf16[256,768]{1,0:T(8,128)(2,1)S(1)} %get-tuple-element.36), channel_id=1, source_target_pairs={{0,6},{1,7},{2,4},{3,5},{4,2},{5,3},{6,0},{7,1},{8,14},{9,15},{10,... | collective-permute-start | bytes 1179656 | tf_op jit(solution)/shard_map/ppermute | solution.py:240
  54.9 0.5 collective-permute-done.6.refs_4_.refs_0_
  55.6 11.9 %collective-permute-done.9.refs_11_ = bf16[256,768]{1,0:T(8,128)(2,1)S(1)} collective-permute-done((bf16[256,768]{1,0:T(8,128)(2,1)S(1)}, bf16[256,768]{1,0:T(8,128)(2,1)S(1)}, u32[]{:S(2)}, u32[]{:S(2)}) %collective-permute-start.9) | collective-permute-done | bytes 393248 | tf_op jit(solution)/shard_map/ppermute | solution.py:240
  67.6 1.1 collective-permute-done.10.refs_10_
  68.6 2.9 %collective-permute-start.12 = (bf16[384,2048]{1,0:T(8,128)(2,1)S(1)}, bf16[384,2048]{1,0:T(8,128)(2,1)S(1)}, u32[]{:S(2)}, u32[]{:S(2)}) collective-permute-start(bf16[384,2048]{1,0:T(8,128)(2,1)S(1)} %pad_maximum_fusion.1), channel_id=1, source_target_pairs={{0,1},{1,0},{2,3},{3,2},{4,5},{5,4},{6,7},{7,6},{8,9},{9,8},{10,11... | collective-permute-start | bytes 4718600 | tf_op jit(solution)/shard_map/ppermute | solution.py:240
  71.8 3.0 %collective-permute-start.14 = (bf16[256,768]{1,0:T(8,128)(2,1)S(1)}, bf16[256,768]{1,0:T(8,128)(2,1)S(1)}, u32[]{:S(2)}, u32[]{:S(2)}) collective-permute-start(bf16[256,768]{1,0:T(8,128)(2,1)S(1)} %get-tuple-element.40), channel_id=1, source_target_pairs={{0,10},{1,11},{2,8},{3,9},{4,14},{5,15},{6,12},{7,13},{8,2},{9,3},... | collective-permute-start | bytes 1179656 | tf_op jit(solution)/shard_map/ppermute | solution.py:240
  75.1 1.2 %collective-permute-start.16 = (bf16[256,768]{1,0:T(8,128)(2,1)S(1)}, bf16[256,768]{1,0:T(8,128)(2,1)S(1)}, u32[]{:S(2)}, u32[]{:S(2)}) collective-permute-start(bf16[256,768]{1,0:T(8,128)(2,1)S(1)} %get-tuple-element.42), channel_id=1, source_target_pairs={{0,4},{1,5},{2,6},{3,7},{4,0},{5,1},{6,2},{7,3},{8,12},{9,13},{10,... | collective-permute-start | bytes 1179656 | tf_op jit(solution)/shard_map/ppermute | solution.py:240
  76.3 4.3 %early_product.1.refs_9_ = f32[2048,768]{1,0:T(8,128)S(1)} custom-call(bf16[128,2048]{1,0:T(8,128)(2,1)S(1)} %copy-done.3, bf16[512,2048]{1,0:T(8,128)(2,1)S(1)} %collective-permute-done.11.refs_1_.refs_3_, bf16[128,2048]{1,0:T(8,128)(2,1)S(1)} %collective-permute-done.4.refs_2_, bf16[128,2048]{1,0:T(8,128)(2,1)S(1)} %collective-permute-done.2.refs_3_, ...), custom_call_target="tpu_custom_call" | custom-call | flops 4026531840 | bytes 3145728 | tf_op jit(solution)/shard_map/early_product/pallas_call | solution.py:213
  80.5 19.1 %collective-permute-done.14.refs_6_ = bf16[256,768]{1,0:T(8,128)(2,1)S(1)} collective-permute-done((bf16[256,768]{1,0:T(8,128)(2,1)S(1)}, bf16[256,768]{1,0:T(8,128)(2,1)S(1)}, u32[]{:S(2)}, u32[]{:S(2)}) %collective-permute-start.14) | collective-permute-done | bytes 393248 | tf_op jit(solution)/shard_map/ppermute | solution.py:240
  99.6 10.4 %collective-permute-done.15.refs_8_ = bf16[256,768]{1,0:T(8,128)(2,1)S(1)} collective-permute-done((bf16[256,768]{1,0:T(8,128)(2,1)S(1)}, bf16[256,768]{1,0:T(8,128)(2,1)S(1)}, u32[]{:S(2)}, u32[]{:S(2)}) %collective-permute-start.15) | collective-permute-done | bytes 393248 | tf_op jit(solution)/shard_map/ppermute | solution.py:240
  110.0 0.5 collective-permute-start.17
  110.5 1.5 %collective-permute-done.17.refs_5_ = bf16[128,2048]{1,0:T(8,128)(2,1)S(1)} collective-permute-done((bf16[128,2048]{1,0:T(8,128)(2,1)S(1)}, bf16[128,2048]{1,0:T(8,128)(2,1)S(1)}, u32[]{:S(2)}, u32[]{:S(2)}) %collective-permute-start.17) | collective-permute-done | bytes 524320 | tf_op jit(solution)/shard_map/ppermute | solution.py:240
  112.0 3.9 %product.1 = bf16[2048,768]{1,0:T(8,128)(2,1)} custom-call(bf16[256,2048]{1,0:T(8,128)(2,1)S(1)} %collective-permute-done.6.refs_4_.refs_0_, bf16[384,2048]{1,0:T(8,128)(2,1)S(1)} %collective-permute-done.12.refs_5_.refs_1_, bf16[128,2048]{1,0:T(8,128)(2,1)S(1)} %collective-permute-done.3.refs_2_, ...), custom_call_target="tpu_custom_call" | custom-call | flops 2415919104 | bytes 3145728 | tf_op jit(solution)/shard_map/product/pallas_call | solution.py:213
  (25 shorter events, 1.6 us)
Async XLA Ops:
  0.6 15.9 %collective-permute-start = (bf16[1024,768]{1,0:T(8,128)(2,1)}, bf16[1024,768]{1,0:T(8,128)(2,1)}, u32[]{:S(2)}, u32[]{:S(2)}) collective-permute-start(bf16[1024,768]{1,0:T(8,128)(2,1)} %bitcast.7), channel_id=1, source_target_pairs={{0,1},{1,0},{2,3},{3,2},{4,5},{5,4},{6,7},{7,6},{8,9},{9,8},{10,11... | collective-permute-start | bytes 4718600 | tf_op jit(solution)/shard_map/ppermute | solution.py:240
  1.4 22.9 %collective-permute-start.3 = (bf16[128,2048]{1,0:T(8,128)(2,1)}, bf16[128,2048]{1,0:T(8,128)(2,1)S(1)}, u32[]{:S(2)}, u32[]{:S(2)}) collective-permute-start(bf16[128,2048]{1,0:T(8,128)(2,1)} %refs_0_.1), channel_id=1, source_target_pairs={{0,4},{1,5},{2,6},{3,7},{4,0},{5,1},{6,2},{7,3},{8,12},{9,13},{10,... | collective-permute-start | bytes 1572872 | tf_op jit(solution)/shard_map/ppermute | solution.py:240
  1.4 26.0 %collective-permute-start.2 = (bf16[128,2048]{1,0:T(8,128)(2,1)}, bf16[128,2048]{1,0:T(8,128)(2,1)S(1)}, u32[]{:S(2)}, u32[]{:S(2)}) collective-permute-start(bf16[128,2048]{1,0:T(8,128)(2,1)} %refs_0_.1), channel_id=1, source_target_pairs={{0,8},{1,9},{2,10},{3,11},{4,12},{5,13},{6,14},{7,15},{8,0},{9,1},... | collective-permute-start | bytes 1572872 | tf_op jit(solution)/shard_map/ppermute | solution.py:240
  3.9 23.6 %collective-permute-start.4 = (bf16[128,2048]{1,0:T(8,128)(2,1)}, bf16[128,2048]{1,0:T(8,128)(2,1)S(1)}, u32[]{:S(2)}, u32[]{:S(2)}) collective-permute-start(bf16[128,2048]{1,0:T(8,128)(2,1)} %refs_0_.1), channel_id=1, source_target_pairs={{0,2},{1,3},{2,0},{3,1},{4,6},{5,7},{6,4},{7,5},{8,10},{9,11},{10,... | collective-permute-start | bytes 1572872 | tf_op jit(solution)/shard_map/ppermute | solution.py:240
  5.1 1.4 %copy-start = (bf16[128,8,768]{2,1,0:T(8,128)(2,1)S(1)}, bf16[128,8,768]{2,1,0:T(8,128)(2,1)}, u32[]{:S(2)}) copy-start(bf16[128,8,768]{2,1,0:T(8,128)(2,1)} %param.5) | copy-start | bytes 4718596
  6.5 1.0 copy-start.2
  7.5 0.7 copy-start.4
  8.2 0.7 copy-start.5
  8.9 0.7 copy-start.6
  9.6 7.0 %copy-start.1 = (bf16[128,8,768]{2,1,0:T(8,128)(2,1)S(1)}, bf16[128,8,768]{2,1,0:T(8,128)(2,1)}, u32[]{:S(2)}) copy-start(bf16[128,8,768]{2,1,0:T(8,128)(2,1)} %param.5) | copy-start | bytes 4718596
  14.8 1.7 %collective-permute-start.1 = (f32[8,256]{1,0:T(8,128)S(1)}, f32[8,256]{1,0:T(8,128)S(1)}, u32[]{:S(2)}, u32[]{:S(2)}) collective-permute-start(f32[8,256]{1,0:T(8,128)S(1)} %get-tuple-element.24.own_meta_ref), channel_id=1, source_target_pairs={{0,1},{1,0},{2,3},{3,2},{4,5},{5,4},{6,7},{7,6},{8,9},{9,8},{10,11... | collective-permute-start | bytes 24584 | tf_op jit(solution)/shard_map/ppermute | solution.py:240
  16.6 10.9 %copy-start.3 = (bf16[128,2048]{1,0:T(8,128)(2,1)S(1)}, bf16[128,2048]{1,0:T(8,128)(2,1)}, u32[]{:S(2)}) copy-start(bf16[128,2048]{1,0:T(8,128)(2,1)} %refs_0_.1) | copy-start | bytes 1572868
  19.1 10.4 %collective-permute-start.5 = (bf16[256,768]{1,0:T(8,128)(2,1)S(1)}, bf16[256,768]{1,0:T(8,128)(2,1)S(1)}, u32[]{:S(2)}, u32[]{:S(2)}) collective-permute-start(bf16[256,768]{1,0:T(8,128)(2,1)S(1)} %get-tuple-element.28), channel_id=1, source_target_pairs={{0,2},{1,3},{2,0},{3,1},{4,6},{5,7},{6,4},{7,5},{8,10},{9,11},{10,... | collective-permute-start | bytes 1179656 | tf_op jit(solution)/shard_map/ppermute | solution.py:240
  29.5 39.2 %collective-permute-start.11 = (bf16[512,2048]{1,0:T(8,128)(2,1)S(1)}, bf16[512,2048]{1,0:T(8,128)(2,1)S(1)}, u32[]{:S(2)}, u32[]{:S(2)}) collective-permute-start(bf16[512,2048]{1,0:T(8,128)(2,1)S(1)} %pad_maximum_fusion), channel_id=1, source_target_pairs={{0,1},{1,0},{2,3},{3,2},{4,5},{5,4},{6,7},{7,6},{8,9},{9,8},{10,11... | collective-permute-start | bytes 6291464 | tf_op jit(solution)/shard_map/ppermute | solution.py:240
  30.7 24.8 %collective-permute-start.6 = (bf16[256,2048]{1,0:T(8,128)(2,1)S(1)}, bf16[256,2048]{1,0:T(8,128)(2,1)S(1)}, u32[]{:S(2)}, u32[]{:S(2)}) collective-permute-start(bf16[256,2048]{1,0:T(8,128)(2,1)S(1)} %pad_maximum_fusion.2), channel_id=1, source_target_pairs={{0,2},{1,3},{2,0},{3,1},{4,6},{5,7},{6,4},{7,5},{8,10},{9,11},{10,... | collective-permute-start | bytes 3145736 | tf_op jit(solution)/shard_map/ppermute | solution.py:240
  30.9 20.8 %collective-permute-start.7 = (bf16[128,2048]{1,0:T(8,128)(2,1)S(1)}, bf16[128,2048]{1,0:T(8,128)(2,1)S(1)}, u32[]{:S(2)}, u32[]{:S(2)}) collective-permute-start(bf16[128,2048]{1,0:T(8,128)(2,1)S(1)} %collective-permute-done.2.refs_3_), channel_id=1, source_target_pairs={{0,4},{1,5},{2,6},{3,7},{4,0},{5,1},{6,2},{7,3},{8,12},{9,13},{10,... | collective-permute-start | bytes 1572872 | tf_op jit(solution)/shard_map/ppermute | solution.py:240
  32.2 23.4 %collective-permute-start.8 = (bf16[256,768]{1,0:T(8,128)(2,1)S(1)}, bf16[256,768]{1,0:T(8,128)(2,1)S(1)}, u32[]{:S(2)}, u32[]{:S(2)}) collective-permute-start(bf16[256,768]{1,0:T(8,128)(2,1)S(1)} %get-tuple-element.34), channel_id=1, source_target_pairs={{0,8},{1,9},{2,10},{3,11},{4,12},{5,13},{6,14},{7,15},{8,0},{9,1},... | collective-permute-start | bytes 1179656 | tf_op jit(solution)/shard_map/ppermute | solution.py:240
  32.3 35.3 %collective-permute-start.9 = (bf16[256,768]{1,0:T(8,128)(2,1)S(1)}, bf16[256,768]{1,0:T(8,128)(2,1)S(1)}, u32[]{:S(2)}, u32[]{:S(2)}) collective-permute-start(bf16[256,768]{1,0:T(8,128)(2,1)S(1)} %get-tuple-element.35), channel_id=1, source_target_pairs={{0,12},{1,13},{2,14},{3,15},{4,8},{5,9},{6,10},{7,11},{8,4},{9,5},... | collective-permute-start | bytes 1179656 | tf_op jit(solution)/shard_map/ppermute | solution.py:240
  51.7 17.0 %collective-permute-start.10 = (bf16[256,768]{1,0:T(8,128)(2,1)S(1)}, bf16[256,768]{1,0:T(8,128)(2,1)S(1)}, u32[]{:S(2)}, u32[]{:S(2)}) collective-permute-start(bf16[256,768]{1,0:T(8,128)(2,1)S(1)} %get-tuple-element.36), channel_id=1, source_target_pairs={{0,6},{1,7},{2,4},{3,5},{4,2},{5,3},{6,0},{7,1},{8,14},{9,15},{10,... | collective-permute-start | bytes 1179656 | tf_op jit(solution)/shard_map/ppermute | solution.py:240
  68.6 7.6 %collective-permute-start.12 = (bf16[384,2048]{1,0:T(8,128)(2,1)S(1)}, bf16[384,2048]{1,0:T(8,128)(2,1)S(1)}, u32[]{:S(2)}, u32[]{:S(2)}) collective-permute-start(bf16[384,2048]{1,0:T(8,128)(2,1)S(1)} %pad_maximum_fusion.1), channel_id=1, source_target_pairs={{0,1},{1,0},{2,3},{3,2},{4,5},{5,4},{6,7},{7,6},{8,9},{9,8},{10,11... | collective-permute-start | bytes 4718600 | tf_op jit(solution)/shard_map/ppermute | solution.py:240
  71.6 38.5 %collective-permute-start.13 = (bf16[128,2048]{1,0:T(8,128)(2,1)S(1)}, bf16[128,2048]{1,0:T(8,128)(2,1)S(1)}, u32[]{:S(2)}, u32[]{:S(2)}) collective-permute-start(bf16[128,2048]{1,0:T(8,128)(2,1)S(1)} %collective-permute-done.7.refs_6_), channel_id=1, source_target_pairs={{0,2},{1,3},{2,0},{3,1},{4,6},{5,7},{6,4},{7,5},{8,10},{9,11},{10,... | collective-permute-start | bytes 1572872 | tf_op jit(solution)/shard_map/ppermute | solution.py:240
  71.8 27.8 %collective-permute-start.14 = (bf16[256,768]{1,0:T(8,128)(2,1)S(1)}, bf16[256,768]{1,0:T(8,128)(2,1)S(1)}, u32[]{:S(2)}, u32[]{:S(2)}) collective-permute-start(bf16[256,768]{1,0:T(8,128)(2,1)S(1)} %get-tuple-element.40), channel_id=1, source_target_pairs={{0,10},{1,11},{2,8},{3,9},{4,14},{5,15},{6,12},{7,13},{8,2},{9,3},... | collective-permute-start | bytes 1179656 | tf_op jit(solution)/shard_map/ppermute | solution.py:240
  74.8 35.2 %collective-permute-start.15 = (bf16[256,768]{1,0:T(8,128)(2,1)S(1)}, bf16[256,768]{1,0:T(8,128)(2,1)S(1)}, u32[]{:S(2)}, u32[]{:S(2)}) collective-permute-start(bf16[256,768]{1,0:T(8,128)(2,1)S(1)} %get-tuple-element.41), channel_id=1, source_target_pairs={{0,14},{1,15},{2,12},{3,13},{4,10},{5,11},{6,8},{7,9},{8,6},{9,7},... | collective-permute-start | bytes 1179656 | tf_op jit(solution)/shard_map/ppermute | solution.py:240
  75.1 34.9 %collective-permute-start.16 = (bf16[256,768]{1,0:T(8,128)(2,1)S(1)}, bf16[256,768]{1,0:T(8,128)(2,1)S(1)}, u32[]{:S(2)}, u32[]{:S(2)}) collective-permute-start(bf16[256,768]{1,0:T(8,128)(2,1)S(1)} %get-tuple-element.42), channel_id=1, source_target_pairs={{0,4},{1,5},{2,6},{3,7},{4,0},{5,1},{6,2},{7,3},{8,12},{9,13},{10,... | collective-permute-start | bytes 1179656 | tf_op jit(solution)/shard_map/ppermute | solution.py:240
  110.0 2.0 %collective-permute-start.17 = (bf16[128,2048]{1,0:T(8,128)(2,1)S(1)}, bf16[128,2048]{1,0:T(8,128)(2,1)S(1)}, u32[]{:S(2)}, u32[]{:S(2)}) collective-permute-start(bf16[128,2048]{1,0:T(8,128)(2,1)S(1)} %collective-permute-done.13.refs_4_), channel_id=1, source_target_pairs={{0,1},{1,0},{2,3},{3,2},{4,5},{5,4},{6,7},{7,6},{8,9},{9,8},{10,11... | collective-permute-start | bytes 1572872 | tf_op jit(solution)/shard_map/ppermute | solution.py:240

commit v4 on v3

--- a/solution.py
+++ b/solution.py
@@ -251,7 +251,7 @@
             jax.ShapeDtypeStruct((2 * examples, pairs), jnp.float32),
             jax.ShapeDtypeStruct((1, examples), jnp.float32),
         ),
-        compiler_params=params,
+        compiler_params=pltpu.CompilerParams(vmem_limit_bytes=54 * 1024 * 1024),
         name="norms",
     )(grad_out, hid_rows, expert_ids.T, gate_codes.T, clip_bound.reshape(1, examples))
     sib_meta = swap(meta, 1)

time: 116 us -> 115 us (level)
  local copies, waits for them, and re-layouts: 4.48 us -> 0.71 us
  waiting for transfers between devices: 73.3 us -> 75.9 us
  Pallas kernels: 15.9 us -> 17.5 us
  starting transfers between devices: 21.1 us -> 19.6 us
    unnamed x14 -> x6, local copies, waits for them, and re-layouts: 4.48 us -> 0.71 us
    ppermute x18, waiting for transfers between devices: 73.3 us -> 75.9 us  [swap(): lax.ppermute(array, 'expert', [(i, i ^ offset) for i in range(devices)])]
    pallas_call x1, Pallas kernels: 5.26 us -> 6.89 us  [per_device_dense(): pl.pallas_call(functools.partial(norm_kernel, devices), out_shape=(jax.Sh...]
    ppermute x18, starting transfers between devices: 21.1 us -> 19.6 us  [swap(): lax.ppermute(array, 'expert', [(i, i ^ offset) for i in range(devices)])]
  transfers between devices with their start and end apart: 18 -> 18, of which waited for: 11 -> 10; matrix products, arithmetic and copies ran while one was open for 0% -> 0% of each run, Pallas kernels for 10% -> 12%
where the time goes in v4:
time: 115 us
  waiting for transfers between devices  75.9 us (66%)
  starting transfers between devices  19.6 us (17%)
  Pallas kernels  17.5 us (15%)
    ppermute x18, waiting for transfers between devices, swap(): lax.ppermute(array, 'expert', [(i, i ^ offset) for i in range(devices)])  75.9 us
    ppermute x18, starting transfers between devices, swap(): lax.ppermute(array, 'expert', [(i, i ^ offset) for i in range(devices)])  19.6 us
    pallas_call x2, Pallas kernels, product(): pl.pallas_call(kernel, out_shape=jax.ShapeDtypeStruct((width, hidden), jn...  8.11 us
    pallas_call x1, Pallas kernels, per_device_dense(): pl.pallas_call(functools.partial(norm_kernel, devices), out_shape=(jax.Sh...  6.89 us
    pallas_call x1, Pallas kernels, per_device_dense(): pl.pallas_call(functools.partial(build_kernel, chips), out_shape=[jax.Sha...  2.5 us
  transfers between devices with their start and end apart: 18, of which 10 were waited for; matrix products, arithmetic and copies ran while one was open for 0% of the time, Pallas kernels for 12%

profile of v4, /device:TPU:9, one launch (start us, length us, event | category | flops | bytes accessed | tf_op | source)
XLA Modules:
  0.0 114.8 jit_solution(4206971044911581544)
XLA Ops:
  0.6 0.7 collective-permute-start
  1.4 2.5 %collective-permute-start.2 = (bf16[128,2048]{1,0:T(8,128)(2,1)}, bf16[128,2048]{1,0:T(8,128)(2,1)S(1)}, u32[]{:S(2)}, u32[]{:S(2)}) collective-permute-start(bf16[128,2048]{1,0:T(8,128)(2,1)} %refs_0_.1), channel_id=1, source_target_pairs={{0,8},{1,9},{2,10},{3,11},{4,12},{5,13},{6,14},{7,15},{8,0},{9,1},... | collective-permute-start | bytes 1572872 | tf_op jit(solution)/shard_map/ppermute | solution.py:240
  3.9 1.2 %collective-permute-start.4 = (bf16[128,2048]{1,0:T(8,128)(2,1)}, bf16[128,2048]{1,0:T(8,128)(2,1)S(1)}, u32[]{:S(2)}, u32[]{:S(2)}) collective-permute-start(bf16[128,2048]{1,0:T(8,128)(2,1)} %refs_0_.1), channel_id=1, source_target_pairs={{0,2},{1,3},{2,0},{3,1},{4,6},{5,7},{6,4},{7,5},{8,10},{9,11},{10,... | collective-permute-start | bytes 1572872 | tf_op jit(solution)/shard_map/ppermute | solution.py:240
  5.1 6.9 %norms.1 = (f32[8,256]{1,0:T(8,128)}, f32[1,4]{1,0:T(1,128)}) custom-call(bf16[128,2048]{1,0:T(8,128)(2,1)} %refs_0_.1, bf16[1024,768]{1,0:T(8,128)(2,1)} %bitcast.8, s32[8,128]{1,0:T(8,128)} %bitcast.11, s32[8,128]{1,0:T(8,128)} %bitcast.12, f32[1,4]{1,0:T(1,128)} %bitcast.13), custom_call_target="tpu_custom_call" | custom-call | tf_op jit(solution)/shard_map/norms/pallas_call | solution.py:248
  12.0 0.9 collective-permute-start.1
  12.9 1.0 collective-permute-done.1.sib_meta_ref
  13.9 0.7 copy-done.2
  14.6 2.5 %build.1 = (bf16[256,768]{1,0:T(8,128)(2,1)S(1)}, bf16[256,768]{1,0:T(8,128)(2,1)S(1)}, bf16[256,768]{1,0:T(8,128)(2,1)S(1)}, bf16[256,768]{1,0:T(8,128)(2,1)S(1...) custom-call(s32[1]{0:T(128)} %bitcast.place_ref, ...), custom_call_target="tpu_custom_call" | custom-call | tf_op jit(solution)/shard_map/build/pallas_call | solution.py:258
  17.1 0.3 collective-permute-start.5
  17.4 6.8 %collective-permute-done.3.refs_2_ = bf16[128,2048]{1,0:T(8,128)(2,1)S(1)} collective-permute-done((bf16[128,2048]{1,0:T(8,128)(2,1)}, bf16[128,2048]{1,0:T(8,128)(2,1)S(1)}, u32[]{:S(2)}, u32[]{:S(2)}) %collective-permute-start.3) | collective-permute-done | bytes 524320 | tf_op jit(solution)/shard_map/ppermute | solution.py:240
  24.3 3.1 %collective-permute-done.2.refs_3_ = bf16[128,2048]{1,0:T(8,128)(2,1)S(1)} collective-permute-done((bf16[128,2048]{1,0:T(8,128)(2,1)}, bf16[128,2048]{1,0:T(8,128)(2,1)S(1)}, u32[]{:S(2)}, u32[]{:S(2)}) %collective-permute-start.2) | collective-permute-done | bytes 524320 | tf_op jit(solution)/shard_map/ppermute | solution.py:240
  27.6 1.1 collective-permute-start.11
  28.7 1.1 collective-permute-start.6
  29.8 1.3 %collective-permute-start.7 = (bf16[128,2048]{1,0:T(8,128)(2,1)S(1)}, bf16[128,2048]{1,0:T(8,128)(2,1)S(1)}, u32[]{:S(2)}, u32[]{:S(2)}) collective-permute-start(bf16[128,2048]{1,0:T(8,128)(2,1)S(1)} %collective-permute-done.2.refs_3_), channel_id=1, source_target_pairs={{0,4},{1,5},{2,6},{3,7},{4,0},{5,1},{6,2},{7,3},{8,12},{9,13},{10,... | collective-permute-start | bytes 1572872 | tf_op jit(solution)/shard_map/ppermute | solution.py:240
  31.2 1.0 collective-permute-start.8
  32.2 0.3 collective-permute-start.9
  32.5 18.1 %collective-permute-done.7.refs_6_ = bf16[128,2048]{1,0:T(8,128)(2,1)S(1)} collective-permute-done((bf16[128,2048]{1,0:T(8,128)(2,1)S(1)}, bf16[128,2048]{1,0:T(8,128)(2,1)S(1)}, u32[]{:S(2)}, u32[]{:S(2)}) %collective-permute-start.7) | collective-permute-done | bytes 524320 | tf_op jit(solution)/shard_map/ppermute | solution.py:240
  50.6 2.3 %collective-permute-start.10 = (bf16[256,768]{1,0:T(8,128)(2,1)S(1)}, bf16[256,768]{1,0:T(8,128)(2,1)S(1)}, u32[]{:S(2)}, u32[]{:S(2)}) collective-permute-start(bf16[256,768]{1,0:T(8,128)(2,1)S(1)} %get-tuple-element.36), channel_id=1, source_target_pairs={{0,6},{1,7},{2,4},{3,5},{4,2},{5,3},{6,0},{7,1},{8,14},{9,15},{10,... | collective-permute-start | bytes 1179656 | tf_op jit(solution)/shard_map/ppermute | solution.py:240
  52.9 0.6 collective-permute-done.6.refs_4_.refs_0_
  53.7 12.7 %collective-permute-done.9.refs_11_ = bf16[256,768]{1,0:T(8,128)(2,1)S(1)} collective-permute-done((bf16[256,768]{1,0:T(8,128)(2,1)S(1)}, bf16[256,768]{1,0:T(8,128)(2,1)S(1)}, u32[]{:S(2)}, u32[]{:S(2)}) %collective-permute-start.9) | collective-permute-done | bytes 393248 | tf_op jit(solution)/shard_map/ppermute | solution.py:240
  66.4 2.5 %collective-permute-done.10.refs_10_ = bf16[256,768]{1,0:T(8,128)(2,1)S(1)} collective-permute-done((bf16[256,768]{1,0:T(8,128)(2,1)S(1)}, bf16[256,768]{1,0:T(8,128)(2,1)S(1)}, u32[]{:S(2)}, u32[]{:S(2)}) %collective-permute-start.10) | collective-permute-done | bytes 393248 | tf_op jit(solution)/shard_map/ppermute | solution.py:240
  68.9 0.7 collective-permute-start.12
  69.6 1.1 collective-permute-start.13
  70.7 2.2 %collective-permute-start.14 = (bf16[256,768]{1,0:T(8,128)(2,1)S(1)}, bf16[256,768]{1,0:T(8,128)(2,1)S(1)}, u32[]{:S(2)}, u32[]{:S(2)}) collective-permute-start(bf16[256,768]{1,0:T(8,128)(2,1)S(1)} %get-tuple-element.40), channel_id=1, source_target_pairs={{0,10},{1,11},{2,8},{3,9},{4,14},{5,15},{6,12},{7,13},{8,2},{9,3},... | collective-permute-start | bytes 1179656 | tf_op jit(solution)/shard_map/ppermute | solution.py:240
  72.9 1.9 %collective-permute-start.15 = (bf16[256,768]{1,0:T(8,128)(2,1)S(1)}, bf16[256,768]{1,0:T(8,128)(2,1)S(1)}, u32[]{:S(2)}, u32[]{:S(2)}) collective-permute-start(bf16[256,768]{1,0:T(8,128)(2,1)S(1)} %get-tuple-element.41), channel_id=1, source_target_pairs={{0,14},{1,15},{2,12},{3,13},{4,10},{5,11},{6,8},{7,9},{8,6},{9,7},... | collective-permute-start | bytes 1179656 | tf_op jit(solution)/shard_map/ppermute | solution.py:240
  74.9 0.3 collective-permute-start.16
  75.2 4.3 %early_product.1.refs_9_ = f32[2048,768]{1,0:T(8,128)S(1)} custom-call(bf16[128,2048]{1,0:T(8,128)(2,1)S(1)} %copy-done.1, bf16[512,2048]{1,0:T(8,128)(2,1)S(1)} %collective-permute-done.11.refs_1_.refs_3_, bf16[128,2048]{1,0:T(8,128)(2,1)S(1)} %collective-permute-done.4.refs_2_, bf16[128,2048]{1,0:T(8,128)(2,1)S(1)} %collective-permute-done.2.refs_3_, ...), custom_call_target="tpu_custom_call" | custom-call | flops 4026531840 | bytes 3145728 | tf_op jit(solution)/shard_map/early_product/pallas_call | solution.py:213
  79.5 19.0 %collective-permute-done.14.refs_6_ = bf16[256,768]{1,0:T(8,128)(2,1)S(1)} collective-permute-done((bf16[256,768]{1,0:T(8,128)(2,1)S(1)}, bf16[256,768]{1,0:T(8,128)(2,1)S(1)}, u32[]{:S(2)}, u32[]{:S(2)}) %collective-permute-start.14) | collective-permute-done | bytes 393248 | tf_op jit(solution)/shard_map/ppermute | solution.py:240
  98.5 10.4 %collective-permute-done.15.refs_8_ = bf16[256,768]{1,0:T(8,128)(2,1)S(1)} collective-permute-done((bf16[256,768]{1,0:T(8,128)(2,1)S(1)}, bf16[256,768]{1,0:T(8,128)(2,1)S(1)}, u32[]{:S(2)}, u32[]{:S(2)}) %collective-permute-start.15) | collective-permute-done | bytes 393248 | tf_op jit(solution)/shard_map/ppermute | solution.py:240
  108.9 0.5 collective-permute-start.17
  109.4 1.5 %collective-permute-done.17.refs_5_ = bf16[128,2048]{1,0:T(8,128)(2,1)S(1)} collective-permute-done((bf16[128,2048]{1,0:T(8,128)(2,1)S(1)}, bf16[128,2048]{1,0:T(8,128)(2,1)S(1)}, u32[]{:S(2)}, u32[]{:S(2)}) %collective-permute-start.17) | collective-permute-done | bytes 524320 | tf_op jit(solution)/shard_map/ppermute | solution.py:240
  110.9 3.9 %product.1 = bf16[2048,768]{1,0:T(8,128)(2,1)} custom-call(bf16[256,2048]{1,0:T(8,128)(2,1)S(1)} %collective-permute-done.6.refs_4_.refs_0_, bf16[384,2048]{1,0:T(8,128)(2,1)S(1)} %collective-permute-done.12.refs_5_.refs_1_, bf16[128,2048]{1,0:T(8,128)(2,1)S(1)} %collective-permute-done.3.refs_2_, ...), custom_call_target="tpu_custom_call" | custom-call | flops 2415919104 | bytes 3145728 | tf_op jit(solution)/shard_map/product/pallas_call | solution.py:213
  (17 shorter events, 0.4 us)
Async XLA Ops:
  0.6 13.3 %copy-start = (bf16[128,8,768]{2,1,0:T(8,128)(2,1)S(1)}, bf16[128,8,768]{2,1,0:T(8,128)(2,1)}, u32[]{:S(2)}) copy-start(bf16[128,8,768]{2,1,0:T(8,128)(2,1)} %param.5) | copy-start | bytes 4718596
  0.6 13.3 %collective-permute-start = (bf16[1024,768]{1,0:T(8,128)(2,1)}, bf16[1024,768]{1,0:T(8,128)(2,1)}, u32[]{:S(2)}, u32[]{:S(2)}) collective-permute-start(bf16[1024,768]{1,0:T(8,128)(2,1)} %bitcast.7), channel_id=1, source_target_pairs={{0,1},{1,0},{2,3},{3,2},{4,5},{5,4},{6,7},{7,6},{8,9},{9,8},{10,11... | collective-permute-start | bytes 4718600 | tf_op jit(solution)/shard_map/ppermute | solution.py:240
  1.4 22.9 %collective-permute-start.3 = (bf16[128,2048]{1,0:T(8,128)(2,1)}, bf16[128,2048]{1,0:T(8,128)(2,1)S(1)}, u32[]{:S(2)}, u32[]{:S(2)}) collective-permute-start(bf16[128,2048]{1,0:T(8,128)(2,1)} %refs_0_.1), channel_id=1, source_target_pairs={{0,4},{1,5},{2,6},{3,7},{4,0},{5,1},{6,2},{7,3},{8,12},{9,13},{10,... | collective-permute-start | bytes 1572872 | tf_op jit(solution)/shard_map/ppermute | solution.py:240
  1.4 26.0 %collective-permute-start.2 = (bf16[128,2048]{1,0:T(8,128)(2,1)}, bf16[128,2048]{1,0:T(8,128)(2,1)S(1)}, u32[]{:S(2)}, u32[]{:S(2)}) collective-permute-start(bf16[128,2048]{1,0:T(8,128)(2,1)} %refs_0_.1), channel_id=1, source_target_pairs={{0,8},{1,9},{2,10},{3,11},{4,12},{5,13},{6,14},{7,15},{8,0},{9,1},... | collective-permute-start | bytes 1572872 | tf_op jit(solution)/shard_map/ppermute | solution.py:240
  3.9 23.6 %collective-permute-start.4 = (bf16[128,2048]{1,0:T(8,128)(2,1)}, bf16[128,2048]{1,0:T(8,128)(2,1)S(1)}, u32[]{:S(2)}, u32[]{:S(2)}) collective-permute-start(bf16[128,2048]{1,0:T(8,128)(2,1)} %refs_0_.1), channel_id=1, source_target_pairs={{0,2},{1,3},{2,0},{3,1},{4,6},{5,7},{6,4},{7,5},{8,10},{9,11},{10,... | collective-permute-start | bytes 1572872 | tf_op jit(solution)/shard_map/ppermute | solution.py:240
  12.0 1.9 %collective-permute-start.1 = (f32[8,256]{1,0:T(8,128)}, f32[8,256]{1,0:T(8,128)S(1)}, u32[]{:S(2)}, u32[]{:S(2)}) collective-permute-start(f32[8,256]{1,0:T(8,128)} %get-tuple-element.24.own_meta_ref), channel_id=1, source_target_pairs={{0,1},{1,0},{2,3},{3,2},{4,5},{5,4},{6,7},{7,6},{8,9},{9,8},{10,11... | collective-permute-start | bytes 24584 | tf_op jit(solution)/shard_map/ppermute | solution.py:240
  13.9 0.7 copy-start.2
  14.6 12.9 %copy-start.1 = (bf16[128,2048]{1,0:T(8,128)(2,1)S(1)}, bf16[128,2048]{1,0:T(8,128)(2,1)}, u32[]{:S(2)}) copy-start(bf16[128,2048]{1,0:T(8,128)(2,1)} %refs_0_.1) | copy-start | bytes 1572868
  17.1 10.5 %collective-permute-start.5 = (bf16[256,768]{1,0:T(8,128)(2,1)S(1)}, bf16[256,768]{1,0:T(8,128)(2,1)S(1)}, u32[]{:S(2)}, u32[]{:S(2)}) collective-permute-start(bf16[256,768]{1,0:T(8,128)(2,1)S(1)} %get-tuple-element.28), channel_id=1, source_target_pairs={{0,2},{1,3},{2,0},{3,1},{4,6},{5,7},{6,4},{7,5},{8,10},{9,11},{10,... | collective-permute-start | bytes 1179656 | tf_op jit(solution)/shard_map/ppermute | solution.py:240
  27.6 41.3 %collective-permute-start.11 = (bf16[512,2048]{1,0:T(8,128)(2,1)S(1)}, bf16[512,2048]{1,0:T(8,128)(2,1)S(1)}, u32[]{:S(2)}, u32[]{:S(2)}) collective-permute-start(bf16[512,2048]{1,0:T(8,128)(2,1)S(1)} %pad_maximum_fusion), channel_id=1, source_target_pairs={{0,1},{1,0},{2,3},{3,2},{4,5},{5,4},{6,7},{7,6},{8,9},{9,8},{10,11... | collective-permute-start | bytes 6291464 | tf_op jit(solution)/shard_map/ppermute | solution.py:240
  28.7 24.8 %collective-permute-start.6 = (bf16[256,2048]{1,0:T(8,128)(2,1)S(1)}, bf16[256,2048]{1,0:T(8,128)(2,1)S(1)}, u32[]{:S(2)}, u32[]{:S(2)}) collective-permute-start(bf16[256,2048]{1,0:T(8,128)(2,1)S(1)} %pad_maximum_fusion.2), channel_id=1, source_target_pairs={{0,2},{1,3},{2,0},{3,1},{4,6},{5,7},{6,4},{7,5},{8,10},{9,11},{10,... | collective-permute-start | bytes 3145736 | tf_op jit(solution)/shard_map/ppermute | solution.py:240
  29.8 20.7 %collective-permute-start.7 = (bf16[128,2048]{1,0:T(8,128)(2,1)S(1)}, bf16[128,2048]{1,0:T(8,128)(2,1)S(1)}, u32[]{:S(2)}, u32[]{:S(2)}) collective-permute-start(bf16[128,2048]{1,0:T(8,128)(2,1)S(1)} %collective-permute-done.2.refs_3_), channel_id=1, source_target_pairs={{0,4},{1,5},{2,6},{3,7},{4,0},{5,1},{6,2},{7,3},{8,12},{9,13},{10,... | collective-permute-start | bytes 1572872 | tf_op jit(solution)/shard_map/ppermute | solution.py:240
  31.2 22.5 %collective-permute-start.8 = (bf16[256,768]{1,0:T(8,128)(2,1)S(1)}, bf16[256,768]{1,0:T(8,128)(2,1)S(1)}, u32[]{:S(2)}, u32[]{:S(2)}) collective-permute-start(bf16[256,768]{1,0:T(8,128)(2,1)S(1)} %get-tuple-element.34), channel_id=1, source_target_pairs={{0,8},{1,9},{2,10},{3,11},{4,12},{5,13},{6,14},{7,15},{8,0},{9,1},... | collective-permute-start | bytes 1179656 | tf_op jit(solution)/shard_map/ppermute | solution.py:240
  32.2 34.3 %collective-permute-start.9 = (bf16[256,768]{1,0:T(8,128)(2,1)S(1)}, bf16[256,768]{1,0:T(8,128)(2,1)S(1)}, u32[]{:S(2)}, u32[]{:S(2)}) collective-permute-start(bf16[256,768]{1,0:T(8,128)(2,1)S(1)} %get-tuple-element.35), channel_id=1, source_target_pairs={{0,12},{1,13},{2,14},{3,15},{4,8},{5,9},{6,10},{7,11},{8,4},{9,5},... | collective-permute-start | bytes 1179656 | tf_op jit(solution)/shard_map/ppermute | solution.py:240
  50.6 18.3 %collective-permute-start.10 = (bf16[256,768]{1,0:T(8,128)(2,1)S(1)}, bf16[256,768]{1,0:T(8,128)(2,1)S(1)}, u32[]{:S(2)}, u32[]{:S(2)}) collective-permute-start(bf16[256,768]{1,0:T(8,128)(2,1)S(1)} %get-tuple-element.36), channel_id=1, source_target_pairs={{0,6},{1,7},{2,4},{3,5},{4,2},{5,3},{6,0},{7,1},{8,14},{9,15},{10,... | collective-permute-start | bytes 1179656 | tf_op jit(solution)/shard_map/ppermute | solution.py:240
  68.9 6.3 %collective-permute-start.12 = (bf16[384,2048]{1,0:T(8,128)(2,1)S(1)}, bf16[384,2048]{1,0:T(8,128)(2,1)S(1)}, u32[]{:S(2)}, u32[]{:S(2)}) collective-permute-start(bf16[384,2048]{1,0:T(8,128)(2,1)S(1)} %pad_maximum_fusion.1), channel_id=1, source_target_pairs={{0,1},{1,0},{2,3},{3,2},{4,5},{5,4},{6,7},{7,6},{8,9},{9,8},{10,11... | collective-permute-start | bytes 4718600 | tf_op jit(solution)/shard_map/ppermute | solution.py:240
  69.6 39.3 %collective-permute-start.13 = (bf16[128,2048]{1,0:T(8,128)(2,1)S(1)}, bf16[128,2048]{1,0:T(8,128)(2,1)S(1)}, u32[]{:S(2)}, u32[]{:S(2)}) collective-permute-start(bf16[128,2048]{1,0:T(8,128)(2,1)S(1)} %collective-permute-done.7.refs_6_), channel_id=1, source_target_pairs={{0,2},{1,3},{2,0},{3,1},{4,6},{5,7},{6,4},{7,5},{8,10},{9,11},{10,... | collective-permute-start | bytes 1572872 | tf_op jit(solution)/shard_map/ppermute | solution.py:240
  70.7 27.8 %collective-permute-start.14 = (bf16[256,768]{1,0:T(8,128)(2,1)S(1)}, bf16[256,768]{1,0:T(8,128)(2,1)S(1)}, u32[]{:S(2)}, u32[]{:S(2)}) collective-permute-start(bf16[256,768]{1,0:T(8,128)(2,1)S(1)} %get-tuple-element.40), channel_id=1, source_target_pairs={{0,10},{1,11},{2,8},{3,9},{4,14},{5,15},{6,12},{7,13},{8,2},{9,3},... | collective-permute-start | bytes 1179656 | tf_op jit(solution)/shard_map/ppermute | solution.py:240
  72.9 36.0 %collective-permute-start.15 = (bf16[256,768]{1,0:T(8,128)(2,1)S(1)}, bf16[256,768]{1,0:T(8,128)(2,1)S(1)}, u32[]{:S(2)}, u32[]{:S(2)}) collective-permute-start(bf16[256,768]{1,0:T(8,128)(2,1)S(1)} %get-tuple-element.41), channel_id=1, source_target_pairs={{0,14},{1,15},{2,12},{3,13},{4,10},{5,11},{6,8},{7,9},{8,6},{9,7},... | collective-permute-start | bytes 1179656 | tf_op jit(solution)/shard_map/ppermute | solution.py:240
  74.9 34.0 %collective-permute-start.16 = (bf16[256,768]{1,0:T(8,128)(2,1)S(1)}, bf16[256,768]{1,0:T(8,128)(2,1)S(1)}, u32[]{:S(2)}, u32[]{:S(2)}) collective-permute-start(bf16[256,768]{1,0:T(8,128)(2,1)S(1)} %get-tuple-element.42), channel_id=1, source_target_pairs={{0,4},{1,5},{2,6},{3,7},{4,0},{5,1},{6,2},{7,3},{8,12},{9,13},{10,... | collective-permute-start | bytes 1179656 | tf_op jit(solution)/shard_map/ppermute | solution.py:240
  108.9 2.0 %collective-permute-start.17 = (bf16[128,2048]{1,0:T(8,128)(2,1)S(1)}, bf16[128,2048]{1,0:T(8,128)(2,1)S(1)}, u32[]{:S(2)}, u32[]{:S(2)}) collective-permute-start(bf16[128,2048]{1,0:T(8,128)(2,1)S(1)} %collective-permute-done.13.refs_4_), channel_id=1, source_target_pairs={{0,1},{1,0},{2,3},{3,2},{4,5},{5,4},{6,7},{7,6},{8,9},{9,8},{10,11... | collective-permute-start | bytes 1572872 | tf_op jit(solution)/shard_map/ppermute | solution.py:240

commit v5 on v4

--- a/solution.py
+++ b/solution.py
@@ -266,32 +266,31 @@
     slots[1] = swap(slots[1], 2)
     first = (dy_z2, dy_z1, dy_x, slots[1])
 
-    near = jnp.concatenate([grad_out, dy_z1, dy_x, dy_z2])
     both = jnp.concatenate([dy_z1, dy_z2])
-    slot4, slot6, slot3, dy_z2b, both, near = after((slots[4], slots[6], slots[3], dy_z2, both, near), first)
-    slots[4], slots[6], slots[3] = swap(slot4, 8), swap(slot6, 12), swap(slot3, 6)
-    dy_z3, dy_xz, sib_near = swap(dy_z2b, 4), swap(both, 2), swap(near, 1)
-    second = (slots[4], slots[6], slots[3], dy_z3, dy_xz, sib_near)
-
-    far = jnp.concatenate([dy_z3, dy_xz])
+    slot4, slot6, slot3, dy_z2b, both = after((slots[5], slots[6], slots[2], dy_z2, both), first)
+    slots[5], slots[6], slots[2] = swap(slot4, 10), swap(slot6, 12), swap(slot3, 4)
+    dy_z3, dy_xz = swap(dy_z2b, 4), swap(both, 2)
+    second = (slots[5], slots[6], slots[2], dy_z3, dy_xz)
+
+    far = jnp.concatenate([grad_out, dy_z1, dy_x, dy_z2, dy_z3, dy_xz])
     t = tokens
-    slot5, slot7, slot2, dy_z3b, far = after((slots[5], slots[7], slots[2], dy_z3, far), second)
+    slot5, slot7, slot2, dy_z3b, far = after((slots[4], slots[7], slots[3], dy_z3, far), second)
     dy_xz3, sib_far = swap(dy_z3b, 2), swap(far, 1)
     where = {
-        0: [(grad_out, 0, t), (sib_near, 0, t)],
-        1: [(dy_x, 0, t), (sib_near, 2 * t, t)],
-        2: [(dy_z1, 0, t), (sib_near, t, t)],
-        3: [(dy_xz, 0, t), (sib_far, t, t)],
-        4: [(dy_z2, 0, t), (sib_near, 3 * t, t)],
-        5: [(dy_xz, t, t), (sib_far, 2 * t, t)],
-        6: [(dy_z3, 0, t), (sib_far, 0, t)],
+        0: [(grad_out, 0, t), (sib_far, 0, t)],
+        1: [(dy_x, 0, t), (sib_far, 2 * t, t)],
+        2: [(dy_z1, 0, t), (sib_far, t, t)],
+        3: [(dy_xz, 0, t), (sib_far, 5 * t, t)],
+        4: [(dy_z2, 0, t), (sib_far, 3 * t, t)],
+        5: [(dy_xz, t, t), (sib_far, 6 * t, t)],
+        6: [(dy_z3, 0, t), (sib_far, 4 * t, t)],
     }
-    slots[5], slots[7], slots[2] = swap(slot5, 10), swap(slot7, 14), swap(slot2, 4)
-    third = (slots[5], slots[7], slots[2], dy_xz3, sib_far)
-    total = product((0, 1, 4, 3, 6), slots, where, True)
+    slots[4], slots[7], slots[3] = swap(slot5, 8), swap(slot7, 14), swap(slot2, 6)
+    third = (slots[4], slots[7], slots[3], dy_xz3, sib_far)
+    total = product((0, 1, 5, 6, 2), slots, where, True)
     sib_last = swap(after((dy_xz3,), third + (total,))[0], 1)
     where[7] = [(dy_xz3, 0, t), (sib_last, 0, t)]
-    rest = [j for j in (3, 6, 5, 2, 7) if j not in (0, 1, 4, 3, 6)]
+    rest = [4, 7, 3]
     summed = product(rest, slots, where, False, total)
     return (summed[None], factors.reshape(examples))
 

time: 115 us -> 114 us (level)
  waiting for transfers between devices: 75.9 us -> 72.4 us
  local copies, waits for them, and re-layouts: 0.71 us -> 2.39 us
    ppermute x18 -> x17, waiting for transfers between devices: 75.9 us -> 72.4 us  [swap(): lax.ppermute(array, 'expert', [(i, i ^ offset) for i in range(devices)])]
    unnamed x6 -> x11, local copies, waits for them, and re-layouts: 0.71 us -> 2.29 us
    ppermute x18 -> x17, starting transfers between devices: 19.6 us -> 20.3 us  [swap(): lax.ppermute(array, 'expert', [(i, i ^ offset) for i in range(devices)])]
  transfers between devices with their start and end apart: 18 -> 17, of which waited for: 10 -> 12; matrix products, arithmetic and copies ran while one was open for 0% -> 0% of each run, Pallas kernels for 12% -> 12%
where the time goes in v5:
time: 114 us; the launch traced here: 113 us
  waiting for transfers between devices  72.4 us (64%)
  starting transfers between devices  20.3 us (18%)
  Pallas kernels  17.5 us (15%)
  local copies, waits for them, and re-layouts  2.39 us (2%)
    ppermute x17, waiting for transfers between devices, swap(): lax.ppermute(array, 'expert', [(i, i ^ offset) for i in range(devices)])  72.4 us
    ppermute x17, starting transfers between devices, swap(): lax.ppermute(array, 'expert', [(i, i ^ offset) for i in range(devices)])  20.3 us
    pallas_call x2, Pallas kernels, product(): pl.pallas_call(kernel, out_shape=jax.ShapeDtypeStruct((width, hidden), jn...  8.11 us
    pallas_call x1, Pallas kernels, per_device_dense(): pl.pallas_call(functools.partial(norm_kernel, devices), out_shape=(jax.Sh...  6.94 us
    pallas_call x1, Pallas kernels, per_device_dense(): pl.pallas_call(functools.partial(build_kernel, chips), out_shape=[jax.Sha...  2.44 us
    unnamed x11, local copies, waits for them, and re-layouts  2.29 us
  transfers between devices with their start and end apart: 17, of which 12 were waited for; matrix products, arithmetic and copies ran while one was open for 0% of the time, Pallas kernels for 12%

profile of v5, /device:TPU:9, one launch (start us, length us, event | category | flops | bytes accessed | tf_op | source)
XLA Modules:
  0.0 113.4 jit_solution(7215437763482132015)
XLA Ops:
  0.6 0.7 collective-permute-start.1
  1.4 2.5 %collective-permute-start = (bf16[128,2048]{1,0:T(8,128)(2,1)}, bf16[128,2048]{1,0:T(8,128)(2,1)S(1)}, u32[]{:S(2)}, u32[]{:S(2)}) collective-permute-start(bf16[128,2048]{1,0:T(8,128)(2,1)} %refs_0_.1), channel_id=1, source_target_pairs={{0,8},{1,9},{2,10},{3,11},{4,12},{5,13},{6,14},{7,15},{8,0},{9,1},... | collective-permute-start | bytes 1572872 | tf_op jit(solution)/shard_map/ppermute | solution.py:240
  3.9 1.2 %collective-permute-start.4 = (bf16[128,2048]{1,0:T(8,128)(2,1)}, bf16[128,2048]{1,0:T(8,128)(2,1)S(1)}, u32[]{:S(2)}, u32[]{:S(2)}) collective-permute-start(bf16[128,2048]{1,0:T(8,128)(2,1)} %refs_0_.1), channel_id=1, source_target_pairs={{0,2},{1,3},{2,0},{3,1},{4,6},{5,7},{6,4},{7,5},{8,10},{9,11},{10,... | collective-permute-start | bytes 1572872 | tf_op jit(solution)/shard_map/ppermute | solution.py:240
  5.1 6.9 %norms.1 = (f32[8,256]{1,0:T(8,128)}, f32[1,4]{1,0:T(1,128)}) custom-call(bf16[128,2048]{1,0:T(8,128)(2,1)} %refs_0_.1, bf16[1024,768]{1,0:T(8,128)(2,1)} %bitcast.8, s32[8,128]{1,0:T(8,128)} %bitcast.11, s32[8,128]{1,0:T(8,128)} %bitcast.12, f32[1,4]{1,0:T(1,128)} %bitcast.13), custom_call_target="tpu_custom_call" | custom-call | tf_op jit(solution)/shard_map/norms/pallas_call | solution.py:248
  12.0 0.9 collective-permute-start.2
  12.9 1.0 collective-permute-done.2.sib_meta_ref
  14.0 1.4 %copy-done = bf16[128,8,768]{2,1,0:T(8,128)(2,1)S(1)} copy-done((bf16[128,8,768]{2,1,0:T(8,128)(2,1)S(1)}, bf16[128,8,768]{2,1,0:T(8,128)(2,1)}, u32[]{:S(2)}) %copy-start) | copy-done | bytes 1572888
  15.4 0.7 copy-done.2
  16.1 2.4 %build.1 = (bf16[256,768]{1,0:T(8,128)(2,1)S(1)}, bf16[256,768]{1,0:T(8,128)(2,1)S(1)}, bf16[256,768]{1,0:T(8,128)(2,1)S(1)}, bf16[256,768]{1,0:T(8,128)(2,1)S(1...) custom-call(s32[1]{0:T(128)} %bitcast.place_ref, ...), custom_call_target="tpu_custom_call" | custom-call | tf_op jit(solution)/shard_map/build/pallas_call | solution.py:258
  18.8 5.4 %collective-permute-done.3.refs_5_ = bf16[128,2048]{1,0:T(8,128)(2,1)S(1)} collective-permute-done((bf16[128,2048]{1,0:T(8,128)(2,1)}, bf16[128,2048]{1,0:T(8,128)(2,1)S(1)}, u32[]{:S(2)}, u32[]{:S(2)}) %collective-permute-start.3) | collective-permute-done | bytes 524320 | tf_op jit(solution)/shard_map/ppermute | solution.py:240
  24.3 3.1 %collective-permute-done.refs_0_ = bf16[128,2048]{1,0:T(8,128)(2,1)S(1)} collective-permute-done((bf16[128,2048]{1,0:T(8,128)(2,1)}, bf16[128,2048]{1,0:T(8,128)(2,1)S(1)}, u32[]{:S(2)}, u32[]{:S(2)}) %collective-permute-start) | collective-permute-done | bytes 524320 | tf_op jit(solution)/shard_map/ppermute | solution.py:240
  27.5 1.5 %collective-permute-done.5.refs_7_ = bf16[256,768]{1,0:T(8,128)(2,1)S(1)} collective-permute-done((bf16[256,768]{1,0:T(8,128)(2,1)S(1)}, bf16[256,768]{1,0:T(8,128)(2,1)S(1)}, u32[]{:S(2)}, u32[]{:S(2)}) %collective-permute-start.5) | collective-permute-done | bytes 393248 | tf_op jit(solution)/shard_map/ppermute | solution.py:240
  29.2 1.4 %collective-permute-start.6 = (bf16[128,2048]{1,0:T(8,128)(2,1)S(1)}, bf16[128,2048]{1,0:T(8,128)(2,1)S(1)}, u32[]{:S(2)}, u32[]{:S(2)}) collective-permute-start(bf16[128,2048]{1,0:T(8,128)(2,1)S(1)} %collective-permute-done.refs_0_), channel_id=1, source_target_pairs={{0,4},{1,5},{2,6},{3,7},{4,0},{5,1},{6,2},{7,3},{8,12},{9,13},{10,... | collective-permute-start | bytes 1572872 | tf_op jit(solution)/shard_map/ppermute | solution.py:240
  30.7 1.1 collective-permute-start.8
  31.8 1.3 %collective-permute-start.9 = (bf16[256,768]{1,0:T(8,128)(2,1)S(1)}, bf16[256,768]{1,0:T(8,128)(2,1)S(1)}, u32[]{:S(2)}, u32[]{:S(2)}) collective-permute-start(bf16[256,768]{1,0:T(8,128)(2,1)S(1)} %get-tuple-element.34), channel_id=1, source_target_pairs={{0,12},{1,13},{2,14},{3,15},{4,8},{5,9},{6,10},{7,11},{8,4},{9,5},... | collective-permute-start | bytes 1179656 | tf_op jit(solution)/shard_map/ppermute | solution.py:240
  33.1 2.2 %collective-permute-start.10 = (bf16[256,768]{1,0:T(8,128)(2,1)S(1)}, bf16[256,768]{1,0:T(8,128)(2,1)S(1)}, u32[]{:S(2)}, u32[]{:S(2)}) collective-permute-start(bf16[256,768]{1,0:T(8,128)(2,1)S(1)} %get-tuple-element.35), channel_id=1, source_target_pairs={{0,4},{1,5},{2,6},{3,7},{4,0},{5,1},{6,2},{7,3},{8,12},{9,13},{10,... | collective-permute-start | bytes 1179656 | tf_op jit(solution)/shard_map/ppermute | solution.py:240
  35.3 12.8 %collective-permute-done.6.refs_4_ = bf16[128,2048]{1,0:T(8,128)(2,1)S(1)} collective-permute-done((bf16[128,2048]{1,0:T(8,128)(2,1)S(1)}, bf16[128,2048]{1,0:T(8,128)(2,1)S(1)}, u32[]{:S(2)}, u32[]{:S(2)}) %collective-permute-start.6) | collective-permute-done | bytes 524320 | tf_op jit(solution)/shard_map/ppermute | solution.py:240
  48.1 12.8 %collective-permute-done.7.refs_3_.refs_4_ = bf16[256,2048]{1,0:T(8,128)(2,1)S(1)} collective-permute-done((bf16[256,2048]{1,0:T(8,128)(2,1)S(1)}, bf16[256,2048]{1,0:T(8,128)(2,1)S(1)}, u32[]{:S(2)}, u32[]{:S(2)}) %collective-permute-start.7) | collective-permute-done | bytes 1048608 | tf_op jit(solution)/shard_map/ppermute | solution.py:240
  61.0 4.9 %collective-permute-done.9.refs_9_ = bf16[256,768]{1,0:T(8,128)(2,1)S(1)} collective-permute-done((bf16[256,768]{1,0:T(8,128)(2,1)S(1)}, bf16[256,768]{1,0:T(8,128)(2,1)S(1)}, u32[]{:S(2)}, u32[]{:S(2)}) %collective-permute-start.9) | collective-permute-done | bytes 393248 | tf_op jit(solution)/shard_map/ppermute | solution.py:240
  65.9 0.7 collective-permute-done.10.refs_10_
  66.6 2.4 %collective-permute-start.11 = (bf16[896,2048]{1,0:T(8,128)(2,1)S(1)}, bf16[896,2048]{1,0:T(8,128)(2,1)S(1)}, u32[]{:S(2)}, u32[]{:S(2)}) collective-permute-start(bf16[896,2048]{1,0:T(8,128)(2,1)S(1)} %constant_dynamic-update-slice_fusion), channel_id=1, source_target_pairs={{0,1},{1,0},{2,3},{3,2},{4,5},{5,4},{6,7},{7,6},{8,9},{9,8},{10,11... | collective-permute-start | bytes 11010056 | tf_op jit(solution)/shard_map/ppermute | solution.py:240
  69.0 1.2 %collective-permute-start.12 = (bf16[128,2048]{1,0:T(8,128)(2,1)S(1)}, bf16[128,2048]{1,0:T(8,128)(2,1)S(1)}, u32[]{:S(2)}, u32[]{:S(2)}) collective-permute-start(bf16[128,2048]{1,0:T(8,128)(2,1)S(1)} %collective-permute-done.6.refs_4_), channel_id=1, source_target_pairs={{0,2},{1,3},{2,0},{3,1},{4,6},{5,7},{6,4},{7,5},{8,10},{9,11},{10,... | collective-permute-start | bytes 1572872 | tf_op jit(solution)/shard_map/ppermute | solution.py:240
  70.2 0.5 collective-permute-start.13
  70.8 1.8 %collective-permute-start.14 = (bf16[256,768]{1,0:T(8,128)(2,1)S(1)}, bf16[256,768]{1,0:T(8,128)(2,1)S(1)}, u32[]{:S(2)}, u32[]{:S(2)}) collective-permute-start(bf16[256,768]{1,0:T(8,128)(2,1)S(1)} %get-tuple-element.39), channel_id=1, source_target_pairs={{0,14},{1,15},{2,12},{3,13},{4,10},{5,11},{6,8},{7,9},{8,6},{9,7},... | collective-permute-start | bytes 1179656 | tf_op jit(solution)/shard_map/ppermute | solution.py:240
  72.6 2.1 %collective-permute-start.15 = (bf16[256,768]{1,0:T(8,128)(2,1)S(1)}, bf16[256,768]{1,0:T(8,128)(2,1)S(1)}, u32[]{:S(2)}, u32[]{:S(2)}) collective-permute-start(bf16[256,768]{1,0:T(8,128)(2,1)S(1)} %get-tuple-element.40), channel_id=1, source_target_pairs={{0,6},{1,7},{2,4},{3,5},{4,2},{5,3},{6,0},{7,1},{8,14},{9,15},{10,... | collective-permute-start | bytes 1179656 | tf_op jit(solution)/shard_map/ppermute | solution.py:240
  74.7 0.4 collective-permute-done.11.refs_1_
  75.1 4.3 %early_product.1.refs_8_ = f32[2048,768]{1,0:T(8,128)S(1)} custom-call(bf16[128,2048]{1,0:T(8,128)(2,1)S(1)} %copy-done.1, bf16[896,2048]{1,0:T(8,128)(2,1)S(1)} %collective-permute-done.11.refs_1_, bf16[128,2048]{1,0:T(8,128)(2,1)S(1)} %collective-permute-done.4.refs_2_, bf16[256,2048]{1,0:T(8,128)(2,1)S(1)} %collective-permute-done.7.refs_3_.refs_4_, ...), custom_call_target="tpu_custom_call" | custom-call | flops 4026531840 | bytes 3145728 | tf_op jit(solution)/shard_map/early_product/pallas_call | solution.py:213
  79.3 16.7 %collective-permute-done.13.refs_5_ = bf16[256,768]{1,0:T(8,128)(2,1)S(1)} collective-permute-done((bf16[256,768]{1,0:T(8,128)(2,1)S(1)}, bf16[256,768]{1,0:T(8,128)(2,1)S(1)}, u32[]{:S(2)}, u32[]{:S(2)}) %collective-permute-start.13) | collective-permute-done | bytes 393248 | tf_op jit(solution)/shard_map/ppermute | solution.py:240
  96.0 11.5 %collective-permute-done.14.refs_6_ = bf16[256,768]{1,0:T(8,128)(2,1)S(1)} collective-permute-done((bf16[256,768]{1,0:T(8,128)(2,1)S(1)}, bf16[256,768]{1,0:T(8,128)(2,1)S(1)}, u32[]{:S(2)}, u32[]{:S(2)}) %collective-permute-start.14) | collective-permute-done | bytes 393248 | tf_op jit(solution)/shard_map/ppermute | solution.py:240
  107.5 0.5 collective-permute-start.16
  108.0 1.5 %collective-permute-done.16.refs_3_ = bf16[128,2048]{1,0:T(8,128)(2,1)S(1)} collective-permute-done((bf16[128,2048]{1,0:T(8,128)(2,1)S(1)}, bf16[128,2048]{1,0:T(8,128)(2,1)S(1)}, u32[]{:S(2)}, u32[]{:S(2)}) %collective-permute-start.16) | collective-permute-done | bytes 524320 | tf_op jit(solution)/shard_map/ppermute | solution.py:240
  109.5 3.9 %product.1 = bf16[2048,768]{1,0:T(8,128)(2,1)} custom-call(bf16[128,2048]{1,0:T(8,128)(2,1)S(1)} %collective-permute-done.refs_0_, bf16[896,2048]{1,0:T(8,128)(2,1)S(1)} %collective-permute-done.11.refs_1_, bf16[128,2048]{1,0:T(8,128)(2,1)S(1)} %collective-permute-done.12.refs_2_, bf16[128,2048]{1,0:T(8,128)(2,1)S(1)} %collective-permute-done.16.refs_3_, ...), custom_call_target="tpu_custom_call" | custom-call | flops 2415919104 | bytes 3145728 | tf_op jit(solution)/shard_map/product/pallas_call | solution.py:213
  (19 shorter events, 0.9 us)
Async XLA Ops:
  0.6 13.3 %collective-permute-start.1 = (bf16[1024,768]{1,0:T(8,128)(2,1)}, bf16[1024,768]{1,0:T(8,128)(2,1)}, u32[]{:S(2)}, u32[]{:S(2)}) collective-permute-start(bf16[1024,768]{1,0:T(8,128)(2,1)} %bitcast.7), channel_id=1, source_target_pairs={{0,1},{1,0},{2,3},{3,2},{4,5},{5,4},{6,7},{7,6},{8,9},{9,8},{10,11... | collective-permute-start | bytes 4718600 | tf_op jit(solution)/shard_map/ppermute | solution.py:240
  1.4 22.9 %collective-permute-start.3 = (bf16[128,2048]{1,0:T(8,128)(2,1)}, bf16[128,2048]{1,0:T(8,128)(2,1)S(1)}, u32[]{:S(2)}, u32[]{:S(2)}) collective-permute-start(bf16[128,2048]{1,0:T(8,128)(2,1)} %refs_0_.1), channel_id=1, source_target_pairs={{0,4},{1,5},{2,6},{3,7},{4,0},{5,1},{6,2},{7,3},{8,12},{9,13},{10,... | collective-permute-start | bytes 1572872 | tf_op jit(solution)/shard_map/ppermute | solution.py:240
  1.4 26.0 %collective-permute-start = (bf16[128,2048]{1,0:T(8,128)(2,1)}, bf16[128,2048]{1,0:T(8,128)(2,1)S(1)}, u32[]{:S(2)}, u32[]{:S(2)}) collective-permute-start(bf16[128,2048]{1,0:T(8,128)(2,1)} %refs_0_.1), channel_id=1, source_target_pairs={{0,8},{1,9},{2,10},{3,11},{4,12},{5,13},{6,14},{7,15},{8,0},{9,1},... | collective-permute-start | bytes 1572872 | tf_op jit(solution)/shard_map/ppermute | solution.py:240
  3.9 23.6 %collective-permute-start.4 = (bf16[128,2048]{1,0:T(8,128)(2,1)}, bf16[128,2048]{1,0:T(8,128)(2,1)S(1)}, u32[]{:S(2)}, u32[]{:S(2)}) collective-permute-start(bf16[128,2048]{1,0:T(8,128)(2,1)} %refs_0_.1), channel_id=1, source_target_pairs={{0,2},{1,3},{2,0},{3,1},{4,6},{5,7},{6,4},{7,5},{8,10},{9,11},{10,... | collective-permute-start | bytes 1572872 | tf_op jit(solution)/shard_map/ppermute | solution.py:240
  5.1 24.1 %copy-start.1 = (bf16[128,2048]{1,0:T(8,128)(2,1)S(1)}, bf16[128,2048]{1,0:T(8,128)(2,1)}, u32[]{:S(2)}) copy-start(bf16[128,2048]{1,0:T(8,128)(2,1)} %refs_0_.1) | copy-start | bytes 1572868
  12.0 1.9 %collective-permute-start.2 = (f32[8,256]{1,0:T(8,128)}, f32[8,256]{1,0:T(8,128)S(1)}, u32[]{:S(2)}, u32[]{:S(2)}) collective-permute-start(f32[8,256]{1,0:T(8,128)} %get-tuple-element.23.own_meta_ref), channel_id=1, source_target_pairs={{0,1},{1,0},{2,3},{3,2},{4,5},{5,4},{6,7},{7,6},{8,9},{9,8},{10,11... | collective-permute-start | bytes 24584 | tf_op jit(solution)/shard_map/ppermute | solution.py:240
  14.0 1.4 %copy-start = (bf16[128,8,768]{2,1,0:T(8,128)(2,1)S(1)}, bf16[128,8,768]{2,1,0:T(8,128)(2,1)}, u32[]{:S(2)}) copy-start(bf16[128,8,768]{2,1,0:T(8,128)(2,1)} %param.5) | copy-start | bytes 4718596
  15.4 0.7 copy-start.2
  18.5 10.4 %collective-permute-start.5 = (bf16[256,768]{1,0:T(8,128)(2,1)S(1)}, bf16[256,768]{1,0:T(8,128)(2,1)S(1)}, u32[]{:S(2)}, u32[]{:S(2)}) collective-permute-start(bf16[256,768]{1,0:T(8,128)(2,1)S(1)} %get-tuple-element.30), channel_id=1, source_target_pairs={{0,2},{1,3},{2,0},{3,1},{4,6},{5,7},{6,4},{7,5},{8,10},{9,11},{10,... | collective-permute-start | bytes 1179656 | tf_op jit(solution)/shard_map/ppermute | solution.py:240
  28.9 31.9 %collective-permute-start.7 = (bf16[256,2048]{1,0:T(8,128)(2,1)S(1)}, bf16[256,2048]{1,0:T(8,128)(2,1)S(1)}, u32[]{:S(2)}, u32[]{:S(2)}) collective-permute-start(bf16[256,2048]{1,0:T(8,128)(2,1)S(1)} %pad_maximum_fusion), channel_id=1, source_target_pairs={{0,2},{1,3},{2,0},{3,1},{4,6},{5,7},{6,4},{7,5},{8,10},{9,11},{10,... | collective-permute-start | bytes 3145736 | tf_op jit(solution)/shard_map/ppermute | solution.py:240
  29.2 18.8 %collective-permute-start.6 = (bf16[128,2048]{1,0:T(8,128)(2,1)S(1)}, bf16[128,2048]{1,0:T(8,128)(2,1)S(1)}, u32[]{:S(2)}, u32[]{:S(2)}) collective-permute-start(bf16[128,2048]{1,0:T(8,128)(2,1)S(1)} %collective-permute-done.refs_0_), channel_id=1, source_target_pairs={{0,4},{1,5},{2,6},{3,7},{4,0},{5,1},{6,2},{7,3},{8,12},{9,13},{10,... | collective-permute-start | bytes 1572872 | tf_op jit(solution)/shard_map/ppermute | solution.py:240
  30.7 30.2 %collective-permute-start.8 = (bf16[256,768]{1,0:T(8,128)(2,1)S(1)}, bf16[256,768]{1,0:T(8,128)(2,1)S(1)}, u32[]{:S(2)}, u32[]{:S(2)}) collective-permute-start(bf16[256,768]{1,0:T(8,128)(2,1)S(1)} %get-tuple-element.33), channel_id=1, source_target_pairs={{0,10},{1,11},{2,8},{3,9},{4,14},{5,15},{6,12},{7,13},{8,2},{9,3},... | collective-permute-start | bytes 1179656 | tf_op jit(solution)/shard_map/ppermute | solution.py:240
  31.8 34.1 %collective-permute-start.9 = (bf16[256,768]{1,0:T(8,128)(2,1)S(1)}, bf16[256,768]{1,0:T(8,128)(2,1)S(1)}, u32[]{:S(2)}, u32[]{:S(2)}) collective-permute-start(bf16[256,768]{1,0:T(8,128)(2,1)S(1)} %get-tuple-element.34), channel_id=1, source_target_pairs={{0,12},{1,13},{2,14},{3,15},{4,8},{5,9},{6,10},{7,11},{8,4},{9,5},... | collective-permute-start | bytes 1179656 | tf_op jit(solution)/shard_map/ppermute | solution.py:240
  33.1 33.6 %collective-permute-start.10 = (bf16[256,768]{1,0:T(8,128)(2,1)S(1)}, bf16[256,768]{1,0:T(8,128)(2,1)S(1)}, u32[]{:S(2)}, u32[]{:S(2)}) collective-permute-start(bf16[256,768]{1,0:T(8,128)(2,1)S(1)} %get-tuple-element.35), channel_id=1, source_target_pairs={{0,4},{1,5},{2,6},{3,7},{4,0},{5,1},{6,2},{7,3},{8,12},{9,13},{10,... | collective-permute-start | bytes 1179656 | tf_op jit(solution)/shard_map/ppermute | solution.py:240
  66.6 8.4 %collective-permute-start.11 = (bf16[896,2048]{1,0:T(8,128)(2,1)S(1)}, bf16[896,2048]{1,0:T(8,128)(2,1)S(1)}, u32[]{:S(2)}, u32[]{:S(2)}) collective-permute-start(bf16[896,2048]{1,0:T(8,128)(2,1)S(1)} %constant_dynamic-update-slice_fusion), channel_id=1, source_target_pairs={{0,1},{1,0},{2,3},{3,2},{4,5},{5,4},{6,7},{7,6},{8,9},{9,8},{10,11... | collective-permute-start | bytes 11010056 | tf_op jit(solution)/shard_map/ppermute | solution.py:240
  69.0 38.5 %collective-permute-start.12 = (bf16[128,2048]{1,0:T(8,128)(2,1)S(1)}, bf16[128,2048]{1,0:T(8,128)(2,1)S(1)}, u32[]{:S(2)}, u32[]{:S(2)}) collective-permute-start(bf16[128,2048]{1,0:T(8,128)(2,1)S(1)} %collective-permute-done.6.refs_4_), channel_id=1, source_target_pairs={{0,2},{1,3},{2,0},{3,1},{4,6},{5,7},{6,4},{7,5},{8,10},{9,11},{10,... | collective-permute-start | bytes 1572872 | tf_op jit(solution)/shard_map/ppermute | solution.py:240
  70.2 25.8 %collective-permute-start.13 = (bf16[256,768]{1,0:T(8,128)(2,1)S(1)}, bf16[256,768]{1,0:T(8,128)(2,1)S(1)}, u32[]{:S(2)}, u32[]{:S(2)}) collective-permute-start(bf16[256,768]{1,0:T(8,128)(2,1)S(1)} %get-tuple-element.38), channel_id=1, source_target_pairs={{0,8},{1,9},{2,10},{3,11},{4,12},{5,13},{6,14},{7,15},{8,0},{9,1},... | collective-permute-start | bytes 1179656 | tf_op jit(solution)/shard_map/ppermute | solution.py:240
  70.8 36.7 %collective-permute-start.14 = (bf16[256,768]{1,0:T(8,128)(2,1)S(1)}, bf16[256,768]{1,0:T(8,128)(2,1)S(1)}, u32[]{:S(2)}, u32[]{:S(2)}) collective-permute-start(bf16[256,768]{1,0:T(8,128)(2,1)S(1)} %get-tuple-element.39), channel_id=1, source_target_pairs={{0,14},{1,15},{2,12},{3,13},{4,10},{5,11},{6,8},{7,9},{8,6},{9,7},... | collective-permute-start | bytes 1179656 | tf_op jit(solution)/shard_map/ppermute | solution.py:240
  72.6 34.9 %collective-permute-start.15 = (bf16[256,768]{1,0:T(8,128)(2,1)S(1)}, bf16[256,768]{1,0:T(8,128)(2,1)S(1)}, u32[]{:S(2)}, u32[]{:S(2)}) collective-permute-start(bf16[256,768]{1,0:T(8,128)(2,1)S(1)} %get-tuple-element.40), channel_id=1, source_target_pairs={{0,6},{1,7},{2,4},{3,5},{4,2},{5,3},{6,0},{7,1},{8,14},{9,15},{10,... | collective-permute-start | bytes 1179656 | tf_op jit(solution)/shard_map/ppermute | solution.py:240
  107.5 2.0 %collective-permute-start.16 = (bf16[128,2048]{1,0:T(8,128)(2,1)S(1)}, bf16[128,2048]{1,0:T(8,128)(2,1)S(1)}, u32[]{:S(2)}, u32[]{:S(2)}) collective-permute-start(bf16[128,2048]{1,0:T(8,128)(2,1)S(1)} %collective-permute-done.12.refs_2_), channel_id=1, source_target_pairs={{0,1},{1,0},{2,3},{3,2},{4,5},{5,4},{6,7},{7,6},{8,9},{9,8},{10,11... | collective-permute-start | bytes 1572872 | tf_op jit(solution)/shard_map/ppermute | solution.py:240

commit v6 on v5

--- a/solution.py
+++ b/solution.py
@@ -12,7 +12,6 @@
 VMEM_LIMIT = 16 * 1024 * 1024
 PRODUCT_LIMIT = 32 * 1024 * 1024
 LATE_BLOCK = 1024
-HIGHEST = lax.Precision.HIGHEST
 
 
 def per_device_sparse(hidden_saved, grad_out, expert_ids, gate_codes, clip_bound):
@@ -80,14 +79,24 @@
     return (summed[None], factors)
 
 
+def three_terms(value, axis):
+    first = value.astype(jnp.bfloat16)
+    rest = value - first.astype(jnp.float32)
+    second = rest.astype(jnp.bfloat16)
+    third = (rest - second.astype(jnp.float32)).astype(jnp.bfloat16)
+    return jnp.concatenate([first, second, third], axis=axis)
+
+
 def norm_kernel(experts, dy_ref, hid_ref, ids_ref, gate_ref, bound_ref, meta_ref, factor_ref):
     examples = bound_ref.shape[1]
     tokens = dy_ref.shape[0]
     pairs = EXLEN * TOPK
-    spread = (
-        lax.broadcasted_iota(jnp.int32, (pairs, EXLEN), 0) // TOPK
-        == lax.broadcasted_iota(jnp.int32, (pairs, EXLEN), 1)
-    ).astype(jnp.float32)
+    spread = jnp.where(
+        lax.broadcasted_iota(jnp.int32, (pairs, 3 * EXLEN), 0) // TOPK
+        == lax.broadcasted_iota(jnp.int32, (pairs, 3 * EXLEN), 1) % EXLEN,
+        1.0,
+        0.0,
+    ).astype(jnp.bfloat16)
     token = lax.broadcasted_iota(jnp.int32, (tokens, tokens * TOPK), 0)
     place = lax.broadcasted_iota(jnp.int32, (tokens, tokens * TOPK), 1)
     widen = (token == place // TOPK).astype(jnp.float32).astype(jnp.bfloat16)
@@ -98,29 +107,37 @@
     wide = jnp.where(own, wide, 0.0)
     ids_all = jnp.sum(wide[:TOPK], axis=0, keepdims=True)
     gate_all = jnp.sum(wide[TOPK:], axis=0, keepdims=True) / 1024.0
-    factor_row = jnp.zeros((1, examples), jnp.float32)
+    name = lax.broadcasted_iota(jnp.int32, (experts, pairs), 0).astype(jnp.float32)
+    lane = lax.broadcasted_iota(jnp.int32, (1, examples), 1)
+    gates, weights, halves, hid_grams = [], [], [], []
+    for x in range(examples):
+        dy = dy_ref[x * EXLEN : (x + 1) * EXLEN, :]
+        dy_gram = lax.dot_general(dy, dy, (((1,), (1,)), ((), ())), preferred_element_type=jnp.float32)
+        halves.append(jnp.dot(spread, three_terms(dy_gram, 0), preferred_element_type=jnp.float32))
     for x in range(examples):
         ids_row = ids_all[:, x * pairs : (x + 1) * pairs]
         gate_row = gate_all[:, x * pairs : (x + 1) * pairs]
+        named = jnp.where(name == ids_row, gate_row, 0.0).astype(jnp.bfloat16)
+        weights.append(
+            lax.dot_general(named, named, (((0,), (0,)), ((), ())), preferred_element_type=jnp.float32)
+        )
+        gates.append(gate_row)
+        meta_ref[examples + x : examples + x + 1, :] = ids_row
+    for x in range(examples):
         hid = hid_ref[x * pairs : (x + 1) * pairs, :]
-        dy = dy_ref[x * EXLEN : (x + 1) * EXLEN, :]
-        hid_gram = lax.dot_general(hid, hid, (((1,), (1,)), ((), ())), preferred_element_type=jnp.float32)
-        dy_gram = lax.dot_general(dy, dy, (((1,), (1,)), ((), ())), preferred_element_type=jnp.float32)
-        half = jnp.dot(spread, dy_gram, precision=HIGHEST, preferred_element_type=jnp.float32)
+        hid_grams.append(
+            lax.dot_general(hid, hid, (((1,), (1,)), ((), ())), preferred_element_type=jnp.float32)
+        )
+    factor_row = jnp.zeros((1, examples), jnp.float32)
+    for x in range(examples):
         pair_gram = lax.dot_general(
-            half, spread, (((1,), (1,)), ((), ())), precision=HIGHEST, preferred_element_type=jnp.float32
-        )
-        name = lax.broadcasted_iota(jnp.int32, (experts, pairs), 0).astype(jnp.float32)
-        onehot = (name == ids_row).astype(jnp.float32)
-        same = lax.dot_general(onehot, onehot, (((0,), (0,)), ((), ())), preferred_element_type=jnp.float32)
-        weights = hid_gram * pair_gram * same
-        sums = jnp.dot(gate_row, weights, precision=HIGHEST, preferred_element_type=jnp.float32)
-        norm = jnp.sum(sums * gate_row, axis=1, keepdims=True)
+            three_terms(halves[x], 1), spread, (((1,), (1,)), ((), ())), preferred_element_type=jnp.float32
+        )
+        products = hid_grams[x] * pair_gram * weights[x]
+        norm = jnp.sum(jnp.sum(products, axis=0, keepdims=True), axis=1, keepdims=True)
         factor = jnp.minimum(1.0, bound_ref[:, x : x + 1] / jnp.sqrt(norm + 1e-06))
-        lane = lax.broadcasted_iota(jnp.int32, (1, examples), 1)
         factor_row = jnp.where(lane == x, factor, factor_row)
-        meta_ref[x : x + 1, :] = factor * gate_row
-        meta_ref[examples + x : examples + x + 1, :] = ids_row
+        meta_ref[x : x + 1, :] = factor * gates[x]
     factor_ref[...] = factor_row
 
 

time: 114 us -> 113 us (level)
  waiting for transfers between devices: 72.4 us -> 76.1 us
  Pallas kernels: 17.5 us -> 14.7 us
  starting transfers between devices: 20.3 us -> 18.6 us
    ppermute x17, waiting for transfers between devices: 72.4 us -> 76.1 us  [swap(): lax.ppermute(array, 'expert', [(i, i ^ offset) for i in range(devices)])]
    pallas_call x1, Pallas kernels: 6.94 us -> 4.15 us  [per_device_dense(): pl.pallas_call(functools.partial(norm_kernel, devices), out_shape=(jax.Sh...]
    ppermute x17, starting transfers between devices: 20.3 us -> 18.6 us  [swap(): lax.ppermute(array, 'expert', [(i, i ^ offset) for i in range(devices)])]
  transfers between devices with their start and end apart: 17 -> 17, of which waited for: 12 -> 11; matrix products, arithmetic and copies ran while one was open for 0% -> 0% of each run, Pallas kernels for 12% -> 10%
where the time goes in v6:
time: 113 us
  waiting for transfers between devices  76.1 us (67%)
  starting transfers between devices  18.6 us (16%)
  Pallas kernels  14.7 us (13%)
  local copies, waits for them, and re-layouts  2.39 us (2%)
    ppermute x17, waiting for transfers between devices, swap(): lax.ppermute(array, 'expert', [(i, i ^ offset) for i in range(devices)])  76.1 us
    ppermute x17, starting transfers between devices, swap(): lax.ppermute(array, 'expert', [(i, i ^ offset) for i in range(devices)])  18.6 us
    pallas_call x2, Pallas kernels, product(): pl.pallas_call(kernel, out_shape=jax.ShapeDtypeStruct((width, hidden), jn...  8.11 us
    pallas_call x1, Pallas kernels, per_device_dense(): pl.pallas_call(functools.partial(norm_kernel, devices), out_shape=(jax.Sh...  4.15 us
    pallas_call x1, Pallas kernels, per_device_dense(): pl.pallas_call(functools.partial(build_kernel, chips), out_shape=[jax.Sha...  2.44 us
    unnamed x11, local copies, waits for them, and re-layouts  2.29 us
  transfers between devices with their start and end apart: 17, of which 11 were waited for; matrix products, arithmetic and copies ran while one was open for 0% of the time, Pallas kernels for 10%

profile of v6, /device:TPU:9, one launch (start us, length us, event | category | flops | bytes accessed | tf_op | source)
XLA Modules:
  0.0 112.6 jit_solution(4503936580543671472)
XLA Ops:
  0.6 0.7 collective-permute-start.1
  1.4 2.5 %collective-permute-start = (bf16[128,2048]{1,0:T(8,128)(2,1)}, bf16[128,2048]{1,0:T(8,128)(2,1)S(1)}, u32[]{:S(2)}, u32[]{:S(2)}) collective-permute-start(bf16[128,2048]{1,0:T(8,128)(2,1)} %refs_0_.1), channel_id=1, source_target_pairs={{0,8},{1,9},{2,10},{3,11},{4,12},{5,13},{6,14},{7,15},{8,0},{9,1},... | collective-permute-start | bytes 1572872 | tf_op jit(solution)/shard_map/ppermute | solution.py:257
  3.9 1.2 %collective-permute-start.4 = (bf16[128,2048]{1,0:T(8,128)(2,1)}, bf16[128,2048]{1,0:T(8,128)(2,1)S(1)}, u32[]{:S(2)}, u32[]{:S(2)}) collective-permute-start(bf16[128,2048]{1,0:T(8,128)(2,1)} %refs_0_.1), channel_id=1, source_target_pairs={{0,2},{1,3},{2,0},{3,1},{4,6},{5,7},{6,4},{7,5},{8,10},{9,11},{10,... | collective-permute-start | bytes 1572872 | tf_op jit(solution)/shard_map/ppermute | solution.py:257
  5.1 4.1 %norms.1 = (f32[8,256]{1,0:T(8,128)}, f32[1,4]{1,0:T(1,128)}) custom-call(bf16[128,2048]{1,0:T(8,128)(2,1)} %refs_0_.1, bf16[1024,768]{1,0:T(8,128)(2,1)} %bitcast.8, s32[8,128]{1,0:T(8,128)} %bitcast.11, s32[8,128]{1,0:T(8,128)} %bitcast.12, f32[1,4]{1,0:T(1,128)} %bitcast.13), custom_call_target="tpu_custom_call" | custom-call | tf_op jit(solution)/shard_map/norms/pallas_call | solution.py:265
  9.2 0.9 collective-permute-start.2
  10.1 1.0 collective-permute-done.2.sib_meta_ref
  11.2 1.4 %copy-done = bf16[128,8,768]{2,1,0:T(8,128)(2,1)S(1)} copy-done((bf16[128,8,768]{2,1,0:T(8,128)(2,1)S(1)}, bf16[128,8,768]{2,1,0:T(8,128)(2,1)}, u32[]{:S(2)}) %copy-start) | copy-done | bytes 1572888
  12.6 0.7 copy-done.2
  13.3 2.4 %build.1 = (bf16[256,768]{1,0:T(8,128)(2,1)S(1)}, bf16[256,768]{1,0:T(8,128)(2,1)S(1)}, bf16[256,768]{1,0:T(8,128)(2,1)S(1)}, bf16[256,768]{1,0:T(8,128)(2,1)S(1...) custom-call(s32[1]{0:T(128)} %bitcast.place_ref, ...), custom_call_target="tpu_custom_call" | custom-call | tf_op jit(solution)/shard_map/build/pallas_call | solution.py:275
  15.7 0.3 collective-permute-start.5
  16.0 8.2 %collective-permute-done.3.refs_5_ = bf16[128,2048]{1,0:T(8,128)(2,1)S(1)} collective-permute-done((bf16[128,2048]{1,0:T(8,128)(2,1)}, bf16[128,2048]{1,0:T(8,128)(2,1)S(1)}, u32[]{:S(2)}, u32[]{:S(2)}) %collective-permute-start.3) | collective-permute-done | bytes 524320 | tf_op jit(solution)/shard_map/ppermute | solution.py:257
  24.3 3.1 %collective-permute-done.refs_0_ = bf16[128,2048]{1,0:T(8,128)(2,1)S(1)} collective-permute-done((bf16[128,2048]{1,0:T(8,128)(2,1)}, bf16[128,2048]{1,0:T(8,128)(2,1)S(1)}, u32[]{:S(2)}, u32[]{:S(2)}) %collective-permute-start) | collective-permute-done | bytes 524320 | tf_op jit(solution)/shard_map/ppermute | solution.py:257
  27.5 1.3 %collective-permute-start.7 = (bf16[256,2048]{1,0:T(8,128)(2,1)S(1)}, bf16[256,2048]{1,0:T(8,128)(2,1)S(1)}, u32[]{:S(2)}, u32[]{:S(2)}) collective-permute-start(bf16[256,2048]{1,0:T(8,128)(2,1)S(1)} %pad_maximum_fusion), channel_id=1, source_target_pairs={{0,2},{1,3},{2,0},{3,1},{4,6},{5,7},{6,4},{7,5},{8,10},{9,11},{10,... | collective-permute-start | bytes 3145736 | tf_op jit(solution)/shard_map/ppermute | solution.py:257
  29.0 2.1 %collective-permute-start.8 = (bf16[256,768]{1,0:T(8,128)(2,1)S(1)}, bf16[256,768]{1,0:T(8,128)(2,1)S(1)}, u32[]{:S(2)}, u32[]{:S(2)}) collective-permute-start(bf16[256,768]{1,0:T(8,128)(2,1)S(1)} %get-tuple-element.33), channel_id=1, source_target_pairs={{0,10},{1,11},{2,8},{3,9},{4,14},{5,15},{6,12},{7,13},{8,2},{9,3},... | collective-permute-start | bytes 1179656 | tf_op jit(solution)/shard_map/ppermute | solution.py:257
  31.1 0.6 collective-permute-start.9
  31.7 0.9 collective-permute-start.10
  32.6 13.8 %collective-permute-done.6.refs_4_ = bf16[128,2048]{1,0:T(8,128)(2,1)S(1)} collective-permute-done((bf16[128,2048]{1,0:T(8,128)(2,1)S(1)}, bf16[128,2048]{1,0:T(8,128)(2,1)S(1)}, u32[]{:S(2)}, u32[]{:S(2)}) %collective-permute-start.6) | collective-permute-done | bytes 524320 | tf_op jit(solution)/shard_map/ppermute | solution.py:257
  46.4 13.3 %collective-permute-done.7.refs_3_.refs_4_ = bf16[256,2048]{1,0:T(8,128)(2,1)S(1)} collective-permute-done((bf16[256,2048]{1,0:T(8,128)(2,1)S(1)}, bf16[256,2048]{1,0:T(8,128)(2,1)S(1)}, u32[]{:S(2)}, u32[]{:S(2)}) %collective-permute-start.7) | collective-permute-done | bytes 1048608 | tf_op jit(solution)/shard_map/ppermute | solution.py:257
  59.7 0.1 constant_dynamic-update-slice_fusion
  59.8 4.9 %collective-permute-done.9.refs_9_ = bf16[256,768]{1,0:T(8,128)(2,1)S(1)} collective-permute-done((bf16[256,768]{1,0:T(8,128)(2,1)S(1)}, bf16[256,768]{1,0:T(8,128)(2,1)S(1)}, u32[]{:S(2)}, u32[]{:S(2)}) %collective-permute-start.9) | collective-permute-done | bytes 393248 | tf_op jit(solution)/shard_map/ppermute | solution.py:257
  64.7 1.7 %collective-permute-done.10.refs_10_ = bf16[256,768]{1,0:T(8,128)(2,1)S(1)} collective-permute-done((bf16[256,768]{1,0:T(8,128)(2,1)S(1)}, bf16[256,768]{1,0:T(8,128)(2,1)S(1)}, u32[]{:S(2)}, u32[]{:S(2)}) %collective-permute-start.10) | collective-permute-done | bytes 393248 | tf_op jit(solution)/shard_map/ppermute | solution.py:257
  66.4 2.1 %collective-permute-start.11 = (bf16[896,2048]{1,0:T(8,128)(2,1)S(1)}, bf16[896,2048]{1,0:T(8,128)(2,1)S(1)}, u32[]{:S(2)}, u32[]{:S(2)}) collective-permute-start(bf16[896,2048]{1,0:T(8,128)(2,1)S(1)} %constant_dynamic-update-slice_fusion), channel_id=1, source_target_pairs={{0,1},{1,0},{2,3},{3,2},{4,5},{5,4},{6,7},{7,6},{8,9},{9,8},{10,11... | collective-permute-start | bytes 11010056 | tf_op jit(solution)/shard_map/ppermute | solution.py:257
  68.6 0.3 collective-permute-start.12
  68.8 2.0 %collective-permute-start.13 = (bf16[256,768]{1,0:T(8,128)(2,1)S(1)}, bf16[256,768]{1,0:T(8,128)(2,1)S(1)}, u32[]{:S(2)}, u32[]{:S(2)}) collective-permute-start(bf16[256,768]{1,0:T(8,128)(2,1)S(1)} %get-tuple-element.38), channel_id=1, source_target_pairs={{0,8},{1,9},{2,10},{3,11},{4,12},{5,13},{6,14},{7,15},{8,0},{9,1},... | collective-permute-start | bytes 1179656 | tf_op jit(solution)/shard_map/ppermute | solution.py:257
  70.8 2.4 %collective-permute-start.15 = (bf16[256,768]{1,0:T(8,128)(2,1)S(1)}, bf16[256,768]{1,0:T(8,128)(2,1)S(1)}, u32[]{:S(2)}, u32[]{:S(2)}) collective-permute-start(bf16[256,768]{1,0:T(8,128)(2,1)S(1)} %get-tuple-element.40), channel_id=1, source_target_pairs={{0,6},{1,7},{2,4},{3,5},{4,2},{5,3},{6,0},{7,1},{8,14},{9,15},{10,... | collective-permute-start | bytes 1179656 | tf_op jit(solution)/shard_map/ppermute | solution.py:257
  73.3 1.3 %collective-permute-done.11.refs_1_ = bf16[896,2048]{1,0:T(8,128)(2,1)S(1)} collective-permute-done((bf16[896,2048]{1,0:T(8,128)(2,1)S(1)}, bf16[896,2048]{1,0:T(8,128)(2,1)S(1)}, u32[]{:S(2)}, u32[]{:S(2)}) %collective-permute-start.11) | collective-permute-done | bytes 3670048 | tf_op jit(solution)/shard_map/ppermute | solution.py:257
  74.6 4.3 %early_product.1.refs_8_ = f32[2048,768]{1,0:T(8,128)S(1)} custom-call(bf16[128,2048]{1,0:T(8,128)(2,1)S(1)} %copy-done.1, bf16[896,2048]{1,0:T(8,128)(2,1)S(1)} %collective-permute-done.11.refs_1_, bf16[128,2048]{1,0:T(8,128)(2,1)S(1)} %collective-permute-done.4.refs_2_, bf16[256,2048]{1,0:T(8,128)(2,1)S(1)} %collective-permute-done.7.refs_3_.refs_4_, ...), custom_call_target="tpu_custom_call" | custom-call | flops 4026531840 | bytes 3145728 | tf_op jit(solution)/shard_map/early_product/pallas_call | solution.py:230
  78.8 17.5 %collective-permute-done.13.refs_5_ = bf16[256,768]{1,0:T(8,128)(2,1)S(1)} collective-permute-done((bf16[256,768]{1,0:T(8,128)(2,1)S(1)}, bf16[256,768]{1,0:T(8,128)(2,1)S(1)}, u32[]{:S(2)}, u32[]{:S(2)}) %collective-permute-start.13) | collective-permute-done | bytes 393248 | tf_op jit(solution)/shard_map/ppermute | solution.py:257
  96.3 9.7 %collective-permute-done.14.refs_6_ = bf16[256,768]{1,0:T(8,128)(2,1)S(1)} collective-permute-done((bf16[256,768]{1,0:T(8,128)(2,1)S(1)}, bf16[256,768]{1,0:T(8,128)(2,1)S(1)}, u32[]{:S(2)}, u32[]{:S(2)}) %collective-permute-start.14) | collective-permute-done | bytes 393248 | tf_op jit(solution)/shard_map/ppermute | solution.py:257
  106.1 1.2 %collective-permute-start.16 = (bf16[128,2048]{1,0:T(8,128)(2,1)S(1)}, bf16[128,2048]{1,0:T(8,128)(2,1)S(1)}, u32[]{:S(2)}, u32[]{:S(2)}) collective-permute-start(bf16[128,2048]{1,0:T(8,128)(2,1)S(1)} %collective-permute-done.12.refs_2_), channel_id=1, source_target_pairs={{0,1},{1,0},{2,3},{3,2},{4,5},{5,4},{6,7},{7,6},{8,9},{9,8},{10,11... | collective-permute-start | bytes 1572872 | tf_op jit(solution)/shard_map/ppermute | solution.py:257
  107.2 1.5 %collective-permute-done.16.refs_3_ = bf16[128,2048]{1,0:T(8,128)(2,1)S(1)} collective-permute-done((bf16[128,2048]{1,0:T(8,128)(2,1)S(1)}, bf16[128,2048]{1,0:T(8,128)(2,1)S(1)}, u32[]{:S(2)}, u32[]{:S(2)}) %collective-permute-start.16) | collective-permute-done | bytes 524320 | tf_op jit(solution)/shard_map/ppermute | solution.py:257
  108.8 3.9 %product.1 = bf16[2048,768]{1,0:T(8,128)(2,1)} custom-call(bf16[128,2048]{1,0:T(8,128)(2,1)S(1)} %collective-permute-done.refs_0_, bf16[896,2048]{1,0:T(8,128)(2,1)S(1)} %collective-permute-done.11.refs_1_, bf16[128,2048]{1,0:T(8,128)(2,1)S(1)} %collective-permute-done.12.refs_2_, bf16[128,2048]{1,0:T(8,128)(2,1)S(1)} %collective-permute-done.16.refs_3_, ...), custom_call_target="tpu_custom_call" | custom-call | flops 2415919104 | bytes 3145728 | tf_op jit(solution)/shard_map/product/pallas_call | solution.py:230
  (19 shorter events, 0.4 us)
Async XLA Ops:
  0.6 10.5 %collective-permute-start.1 = (bf16[1024,768]{1,0:T(8,128)(2,1)}, bf16[1024,768]{1,0:T(8,128)(2,1)}, u32[]{:S(2)}, u32[]{:S(2)}) collective-permute-start(bf16[1024,768]{1,0:T(8,128)(2,1)} %bitcast.7), channel_id=1, source_target_pairs={{0,1},{1,0},{2,3},{3,2},{4,5},{5,4},{6,7},{7,6},{8,9},{9,8},{10,11... | collective-permute-start | bytes 4718600 | tf_op jit(solution)/shard_map/ppermute | solution.py:257
  1.4 22.9 %collective-permute-start.3 = (bf16[128,2048]{1,0:T(8,128)(2,1)}, bf16[128,2048]{1,0:T(8,128)(2,1)S(1)}, u32[]{:S(2)}, u32[]{:S(2)}) collective-permute-start(bf16[128,2048]{1,0:T(8,128)(2,1)} %refs_0_.1), channel_id=1, source_target_pairs={{0,4},{1,5},{2,6},{3,7},{4,0},{5,1},{6,2},{7,3},{8,12},{9,13},{10,... | collective-permute-start | bytes 1572872 | tf_op jit(solution)/shard_map/ppermute | solution.py:257
  1.4 26.0 %collective-permute-start = (bf16[128,2048]{1,0:T(8,128)(2,1)}, bf16[128,2048]{1,0:T(8,128)(2,1)S(1)}, u32[]{:S(2)}, u32[]{:S(2)}) collective-permute-start(bf16[128,2048]{1,0:T(8,128)(2,1)} %refs_0_.1), channel_id=1, source_target_pairs={{0,8},{1,9},{2,10},{3,11},{4,12},{5,13},{6,14},{7,15},{8,0},{9,1},... | collective-permute-start | bytes 1572872 | tf_op jit(solution)/shard_map/ppermute | solution.py:257
  3.9 23.6 %collective-permute-start.4 = (bf16[128,2048]{1,0:T(8,128)(2,1)}, bf16[128,2048]{1,0:T(8,128)(2,1)S(1)}, u32[]{:S(2)}, u32[]{:S(2)}) collective-permute-start(bf16[128,2048]{1,0:T(8,128)(2,1)} %refs_0_.1), channel_id=1, source_target_pairs={{0,2},{1,3},{2,0},{3,1},{4,6},{5,7},{6,4},{7,5},{8,10},{9,11},{10,... | collective-permute-start | bytes 1572872 | tf_op jit(solution)/shard_map/ppermute | solution.py:257
  5.1 23.7 %copy-start.1 = (bf16[128,2048]{1,0:T(8,128)(2,1)S(1)}, bf16[128,2048]{1,0:T(8,128)(2,1)}, u32[]{:S(2)}) copy-start(bf16[128,2048]{1,0:T(8,128)(2,1)} %refs_0_.1) | copy-start | bytes 1572868
  9.2 1.9 %collective-permute-start.2 = (f32[8,256]{1,0:T(8,128)}, f32[8,256]{1,0:T(8,128)S(1)}, u32[]{:S(2)}, u32[]{:S(2)}) collective-permute-start(f32[8,256]{1,0:T(8,128)} %get-tuple-element.23.own_meta_ref), channel_id=1, source_target_pairs={{0,1},{1,0},{2,3},{3,2},{4,5},{5,4},{6,7},{7,6},{8,9},{9,8},{10,11... | collective-permute-start | bytes 24584 | tf_op jit(solution)/shard_map/ppermute | solution.py:257
  11.2 1.4 %copy-start = (bf16[128,8,768]{2,1,0:T(8,128)(2,1)S(1)}, bf16[128,8,768]{2,1,0:T(8,128)(2,1)}, u32[]{:S(2)}) copy-start(bf16[128,8,768]{2,1,0:T(8,128)(2,1)} %param.5) | copy-start | bytes 4718596
  12.6 0.7 copy-start.2
  15.7 11.7 %collective-permute-start.5 = (bf16[256,768]{1,0:T(8,128)(2,1)S(1)}, bf16[256,768]{1,0:T(8,128)(2,1)S(1)}, u32[]{:S(2)}, u32[]{:S(2)}) collective-permute-start(bf16[256,768]{1,0:T(8,128)(2,1)S(1)} %get-tuple-element.30), channel_id=1, source_target_pairs={{0,2},{1,3},{2,0},{3,1},{4,6},{5,7},{6,4},{7,5},{8,10},{9,11},{10,... | collective-permute-start | bytes 1179656 | tf_op jit(solution)/shard_map/ppermute | solution.py:257
  27.5 32.2 %collective-permute-start.7 = (bf16[256,2048]{1,0:T(8,128)(2,1)S(1)}, bf16[256,2048]{1,0:T(8,128)(2,1)S(1)}, u32[]{:S(2)}, u32[]{:S(2)}) collective-permute-start(bf16[256,2048]{1,0:T(8,128)(2,1)S(1)} %pad_maximum_fusion), channel_id=1, source_target_pairs={{0,2},{1,3},{2,0},{3,1},{4,6},{5,7},{6,4},{7,5},{8,10},{9,11},{10,... | collective-permute-start | bytes 3145736 | tf_op jit(solution)/shard_map/ppermute | solution.py:257
  28.8 17.6 %collective-permute-start.6 = (bf16[128,2048]{1,0:T(8,128)(2,1)S(1)}, bf16[128,2048]{1,0:T(8,128)(2,1)S(1)}, u32[]{:S(2)}, u32[]{:S(2)}) collective-permute-start(bf16[128,2048]{1,0:T(8,128)(2,1)S(1)} %collective-permute-done.refs_0_), channel_id=1, source_target_pairs={{0,4},{1,5},{2,6},{3,7},{4,0},{5,1},{6,2},{7,3},{8,12},{9,13},{10,... | collective-permute-start | bytes 1572872 | tf_op jit(solution)/shard_map/ppermute | solution.py:257
  29.0 30.8 %collective-permute-start.8 = (bf16[256,768]{1,0:T(8,128)(2,1)S(1)}, bf16[256,768]{1,0:T(8,128)(2,1)S(1)}, u32[]{:S(2)}, u32[]{:S(2)}) collective-permute-start(bf16[256,768]{1,0:T(8,128)(2,1)S(1)} %get-tuple-element.33), channel_id=1, source_target_pairs={{0,10},{1,11},{2,8},{3,9},{4,14},{5,15},{6,12},{7,13},{8,2},{9,3},... | collective-permute-start | bytes 1179656 | tf_op jit(solution)/shard_map/ppermute | solution.py:257
  31.1 33.6 %collective-permute-start.9 = (bf16[256,768]{1,0:T(8,128)(2,1)S(1)}, bf16[256,768]{1,0:T(8,128)(2,1)S(1)}, u32[]{:S(2)}, u32[]{:S(2)}) collective-permute-start(bf16[256,768]{1,0:T(8,128)(2,1)S(1)} %get-tuple-element.34), channel_id=1, source_target_pairs={{0,12},{1,13},{2,14},{3,15},{4,8},{5,9},{6,10},{7,11},{8,4},{9,5},... | collective-permute-start | bytes 1179656 | tf_op jit(solution)/shard_map/ppermute | solution.py:257
  31.7 34.8 %collective-permute-start.10 = (bf16[256,768]{1,0:T(8,128)(2,1)S(1)}, bf16[256,768]{1,0:T(8,128)(2,1)S(1)}, u32[]{:S(2)}, u32[]{:S(2)}) collective-permute-start(bf16[256,768]{1,0:T(8,128)(2,1)S(1)} %get-tuple-element.35), channel_id=1, source_target_pairs={{0,4},{1,5},{2,6},{3,7},{4,0},{5,1},{6,2},{7,3},{8,12},{9,13},{10,... | collective-permute-start | bytes 1179656 | tf_op jit(solution)/shard_map/ppermute | solution.py:257
  66.4 8.2 %collective-permute-start.11 = (bf16[896,2048]{1,0:T(8,128)(2,1)S(1)}, bf16[896,2048]{1,0:T(8,128)(2,1)S(1)}, u32[]{:S(2)}, u32[]{:S(2)}) collective-permute-start(bf16[896,2048]{1,0:T(8,128)(2,1)S(1)} %constant_dynamic-update-slice_fusion), channel_id=1, source_target_pairs={{0,1},{1,0},{2,3},{3,2},{4,5},{5,4},{6,7},{7,6},{8,9},{9,8},{10,11... | collective-permute-start | bytes 11010056 | tf_op jit(solution)/shard_map/ppermute | solution.py:257
  68.6 37.5 %collective-permute-start.12 = (bf16[128,2048]{1,0:T(8,128)(2,1)S(1)}, bf16[128,2048]{1,0:T(8,128)(2,1)S(1)}, u32[]{:S(2)}, u32[]{:S(2)}) collective-permute-start(bf16[128,2048]{1,0:T(8,128)(2,1)S(1)} %collective-permute-done.6.refs_4_), channel_id=1, source_target_pairs={{0,2},{1,3},{2,0},{3,1},{4,6},{5,7},{6,4},{7,5},{8,10},{9,11},{10,... | collective-permute-start | bytes 1572872 | tf_op jit(solution)/shard_map/ppermute | solution.py:257
  68.8 27.5 %collective-permute-start.13 = (bf16[256,768]{1,0:T(8,128)(2,1)S(1)}, bf16[256,768]{1,0:T(8,128)(2,1)S(1)}, u32[]{:S(2)}, u32[]{:S(2)}) collective-permute-start(bf16[256,768]{1,0:T(8,128)(2,1)S(1)} %get-tuple-element.38), channel_id=1, source_target_pairs={{0,8},{1,9},{2,10},{3,11},{4,12},{5,13},{6,14},{7,15},{8,0},{9,1},... | collective-permute-start | bytes 1179656 | tf_op jit(solution)/shard_map/ppermute | solution.py:257
  70.8 35.3 %collective-permute-start.14 = (bf16[256,768]{1,0:T(8,128)(2,1)S(1)}, bf16[256,768]{1,0:T(8,128)(2,1)S(1)}, u32[]{:S(2)}, u32[]{:S(2)}) collective-permute-start(bf16[256,768]{1,0:T(8,128)(2,1)S(1)} %get-tuple-element.39), channel_id=1, source_target_pairs={{0,14},{1,15},{2,12},{3,13},{4,10},{5,11},{6,8},{7,9},{8,6},{9,7},... | collective-permute-start | bytes 1179656 | tf_op jit(solution)/shard_map/ppermute | solution.py:257
  70.8 35.2 %collective-permute-start.15 = (bf16[256,768]{1,0:T(8,128)(2,1)S(1)}, bf16[256,768]{1,0:T(8,128)(2,1)S(1)}, u32[]{:S(2)}, u32[]{:S(2)}) collective-permute-start(bf16[256,768]{1,0:T(8,128)(2,1)S(1)} %get-tuple-element.40), channel_id=1, source_target_pairs={{0,6},{1,7},{2,4},{3,5},{4,2},{5,3},{6,0},{7,1},{8,14},{9,15},{10,... | collective-permute-start | bytes 1179656 | tf_op jit(solution)/shard_map/ppermute | solution.py:257
  106.1 2.7 %collective-permute-start.16 = (bf16[128,2048]{1,0:T(8,128)(2,1)S(1)}, bf16[128,2048]{1,0:T(8,128)(2,1)S(1)}, u32[]{:S(2)}, u32[]{:S(2)}) collective-permute-start(bf16[128,2048]{1,0:T(8,128)(2,1)S(1)} %collective-permute-done.12.refs_2_), channel_id=1, source_target_pairs={{0,1},{1,0},{2,3},{3,2},{4,5},{5,4},{6,7},{7,6},{8,9},{9,8},{10,11... | collective-permute-start | bytes 1572872 | tf_op jit(solution)/shard_map/ppermute | solution.py:257
